TPU v7x, 256 devices: a whole 4x4x8 slice. The times are simulated.
256 devices in a mesh: tensor: 8 (over x, y_lo), seq: 32 (over y_hi, z, core).
Axes of the slice: x: 4, y: 4 (y_hi: 2, y_lo: 2; y = y_hi * 2 + y_lo), z: 8, core: 2. Of those that a mesh axis runs over, the one named last changes fastest.
Arguments:
- tokens: bfloat16 [32, 1024, 5120], P('seq', 'tensor'), may hold values from -6 to 6
- query_weight: bfloat16 [5120, 1024], P(None, 'tensor'), may hold values from -0.078125 to 0.078125
- key_weight: bfloat16 [5120, 1024], P(None, 'tensor'), may hold values from -0.078125 to 0.078125
- value_weight: bfloat16 [5120, 5120], P(None, 'tensor'), may hold values from -0.078125 to 0.078125
- conv_taps: float32 [3, 5120], P(None, 'tensor'), may hold values from 0.2 to 2
- norm_gain: float32 [5120], P('tensor'), may hold values from 8 to 64
Outputs:
- mixed: bfloat16 [32, 1024, 5120], P('seq', 'tensor')
All inputs are finite; a program needn't handle non-finite values.
Results may differ from a plain program's by a relative error of at most 0.012.
Values may be sent and summed in bfloat16 or wider, within the bound.
No kernel may reach another device: no remote copies, remote signals or barrier semaphores. Data moves between devices by JAX's collectives and lax.ppermute only.
A program may use at most 128 MiB of HBM per device.

v0:
```python
import functools

import jax
import jax.numpy as jnp
from jax import lax
from jax.experimental import pallas as pl
from jax.experimental.pallas import tpu as pltpu
from jax.sharding import PartitionSpec as P

FEAT = 16
HEAD_DIM = 80
GROUP = 8
NX, NY, NZ = 4, 4, 8
AXES = ("tensor", "seq")
PIECE = 512
PIECES = (PIECE,) * 10
VMEM_LIMIT = 58 * 1024 * 1024
VMEM_SMALL = 16 * 1024 * 1024
FROWS = 160
MROWS = 192
BLOCK = 128
ROWS = 4 * BLOCK
PARTS = ((4,), (0, 1), (2, 3), (5, 6), (7, 8), (9,))
AHEAD = 2
EARLY = 1024
EARLY_COST = 3 * 10**9
ORDER_COST = 5 * 10**9
SLOTS = (0, 1, 3, 2)
VCOLS = GROUP * HEAD_DIM
QCOLS = GROUP * FEAT
GCOLS = VCOLS + 2 * QCOLS
SPLIT = MROWS // NY


def device_of(x, y, z, core):
    x, y, z = x % NX, y % NY, z % NZ
    tensor = x * 2 + (y & 1)
    seq = ((y >> 1) * NZ + z) * 2 + core
    return tensor * 32 + seq


def everywhere():
    return [
        (x, y, z, core)
        for x in range(NX)
        for y in range(NY)
        for z in range(NZ)
        for core in range(2)
    ]


def receive(array, source_of):
    pairs = [(device_of(*source_of(*place)), device_of(*place)) for place in everywhere()]
    return lax.ppermute(array, AXES, pairs)


def from_x(array, step):
    return receive(array, lambda x, y, z, c: (x + step, y, z, c))


def from_y(array, step):
    return receive(array, lambda x, y, z, c: (x, y + step, z, c))


def from_z(array, step):
    return receive(array, lambda x, y, z, c: (x, y, z + step, c))


def from_core(array):
    return receive(array, lambda x, y, z, c: (x, y, z, 1 - c))


def from_far(array):
    place = {}
    for x, y, z, core in everywhere():
        place[x, y & 1, ((y >> 1) * NZ + z) * 2 + core] = device_of(x, y, z, core)
    pairs = []
    for (x, odd, segment), target in place.items():
        source = place.get((x, 1 - odd, segment + (1 if odd else -1)))
        if source is not None:
            pairs.append((source, target))
    return lax.ppermute(array, AXES, pairs)


def features(scaled, off_weight):
    root = 0.5**0.5
    rows = scaled.shape[1]
    parts = [scaled, scaled * scaled * root]
    for step in range(1, FEAT // 2):
        turned = pltpu.roll(scaled, FEAT - step, 0)
        parts.append(scaled * turned * (root * off_weight))
    half = scaled[: FEAT // 2] * scaled[FEAT // 2 :] * (root * off_weight)
    parts.append(half)
    first = lax.broadcasted_iota(jnp.int32, (FEAT // 2, rows), 0) == 0
    parts.append(jnp.where(first, 1.0, 0.0).astype(jnp.float32))
    return jnp.concatenate(parts, axis=0)


def window_of(head):
    start = head * HEAD_DIM // 128 * 128
    stop = -(-(head + 1) * HEAD_DIM // 128) * 128
    return start, stop


def head_mask(head, rows):
    start, stop = window_of(head)
    lane = lax.broadcasted_iota(jnp.int32, (rows, stop - start), 1) + start
    return (lane >= head * HEAD_DIM) & (lane < (head + 1) * HEAD_DIM)


def early_kernel(counts, *refs):
    refs = list(refs)
    blocks = [refs.pop(0) for _ in counts]
    weights = [refs.pop(0) for _ in range(3)]
    taps, gain = refs.pop(0), refs.pop(0)
    value_out, query_key_out, edge_out, small_out, xs, ws, acc, xsem, wsem = refs
    small_out[: taps.shape[0], :] = taps[...]
    small_out[taps.shape[0] :, :] = gain[...]

    def copies_of(index):
        span, copies, row = pl.ds(pl.multiple_of(index * EARLY, EARLY), EARLY), [], 0
        for number, (ref, rows) in enumerate(zip(blocks, counts)):
            copies.append(
                pltpu.make_async_copy(ref.at[:, span], xs.at[pl.ds(row, rows), span], xsem.at[index, number])
            )
            row += rows
        for kind, (col, width) in enumerate(((0, QCOLS), (QCOLS, QCOLS), (2 * QCOLS, VCOLS))):
            copies.append(
                pltpu.make_async_copy(
                    weights[kind].at[span], ws.at[span, pl.ds(col, width)], wsem.at[index, kind]
                )
            )
        return copies

    count = xs.shape[1] // EARLY
    for index in range(AHEAD):
        for copy in copies_of(index):
            copy.start()
    acc[...] = jnp.zeros_like(acc)

    def step(index, carry):
        for copy in copies_of(index):
            copy.wait()

        @pl.when(index + AHEAD < count)
        def _():
            for copy in copies_of(index + AHEAD):
                copy.start()

        span = pl.ds(pl.multiple_of(index * EARLY, EARLY), EARLY)
        acc[...] += jnp.dot(xs[:, span], ws[span, :], preferred_element_type=jnp.float32)
        return carry

    lax.fori_loop(0, count, step, 0)
    query_key_out[...] = acc[:, : 2 * QCOLS]
    value_out[...] = acc[:, 2 * QCOLS :].astype(jnp.bfloat16)
    edge_out[...] = jnp.zeros_like(edge_out)
    for block, slot in enumerate(SLOTS[:3]):
        for end, row in ((0, block * BLOCK), (1, block * BLOCK + BLOCK - 1)):
            line = acc[row : row + 1, 2 * QCOLS :]
            edge_out[2 * slot + end : 2 * slot + end + 1, :] = line.astype(jnp.bfloat16).astype(jnp.float32)


def project_early(blocks, weights, taps, gain):
    counts = tuple(block.shape[0] for block in blocks)
    depth, rows = blocks[0].shape[1], sum(counts)
    hbm = pl.BlockSpec(memory_space=pltpu.HBM)
    vmem = pl.BlockSpec(memory_space=pltpu.VMEM)
    return pl.pallas_call(
        functools.partial(early_kernel, counts),
        out_shape=[
            jax.ShapeDtypeStruct((rows, VCOLS), jnp.bfloat16),
            jax.ShapeDtypeStruct((rows, 2 * QCOLS), jnp.float32),
            jax.ShapeDtypeStruct((8, VCOLS), jnp.float32),
            jax.ShapeDtypeStruct((taps.shape[0] + 1, VCOLS), jnp.float32),
        ],
        in_specs=[hbm] * (len(blocks) + 3) + [vmem] * 2,
        out_specs=[vmem] * 4,
        scratch_shapes=[
            pltpu.VMEM((rows, depth), jnp.bfloat16),
            pltpu.VMEM((depth, GCOLS), jnp.bfloat16),
            pltpu.VMEM((rows, GCOLS), jnp.float32),
            pltpu.SemaphoreType.DMA((depth // EARLY, len(blocks))),
            pltpu.SemaphoreType.DMA((depth // EARLY, 3)),
        ],
        compiler_params=pltpu.CompilerParams(vmem_limit_bytes=VMEM_LIMIT),
        cost_estimate=pl.CostEstimate(flops=EARLY_COST, bytes_accessed=EARLY_COST // 1000, transcendentals=0),
    )(*blocks, *weights, taps, gain)


def project_kernel(counts, offsets, *refs):
    refs = list(refs)
    blocks = [refs.pop(0) for _ in counts]
    weights = [refs.pop(0) for _ in range(3)]
    pieces = [refs.pop(0) for _ in PIECES]
    edge_early = refs.pop(0)
    refs.pop(0)
    value_outs, query_key_outs, edge_out = refs[0:2], refs[2:4], refs[4]
    xs, ws, acc, late, xsem, wsem, psem = refs[5:]
    stages, at = [], 0
    for index, members in enumerate(PARTS):
        count = len(members) * PIECE
        start = pl.multiple_of(offsets[members[0]], PIECE)
        copies, row = [], 0
        for number, (ref, rows) in enumerate(zip(blocks, counts)):
            copies.append(
                pltpu.make_async_copy(
                    ref.at[:, pl.ds(start, count)],
                    xs.at[pl.ds(row, rows), pl.ds(at, count)],
                    xsem.at[index, number],
                )
            )
            row += rows
        for kind, (col, width) in enumerate(((0, QCOLS), (QCOLS, QCOLS), (2 * QCOLS, VCOLS))):
            copies.append(
                pltpu.make_async_copy(
                    weights[kind].at[pl.ds(start, count)],
                    ws.at[pl.ds(at, count), pl.ds(col, width)],
                    wsem.at[index, kind],
                )
            )
        for step, member in enumerate(members):
            copies.append(
                pltpu.make_async_copy(
                    pieces[member],
                    ws.at[pl.ds(at + step * PIECE, PIECE), pl.ds(GCOLS, GCOLS)],
                    psem.at[member],
                )
            )
        stages.append((copies, at, count))
        at += count
    for copies, _, _ in stages[:AHEAD]:
        for copy in copies:
            copy.start()
    for index, (copies, at, count) in enumerate(stages):
        for copy in copies:
            copy.wait()
        if index + AHEAD < len(stages):
            for copy in stages[index + AHEAD][0]:
                copy.start()
        span = slice(at, at + count)
        part = jnp.dot(xs[:, span], ws[span, GCOLS:], preferred_element_type=jnp.float32)
        last = jnp.dot(xs[ROWS - BLOCK :, span], ws[span, :GCOLS], preferred_element_type=jnp.float32)
        if index == 0:
            acc[...] = part
            late[...] = last
        else:
            acc[...] += part
            late[...] += last
    edge_out[:8, :] = edge_early[...]
    for group, (total, slots) in enumerate(((late, SLOTS[3:]), (acc, SLOTS))):
        query_key_outs[group][...] = total[:, : 2 * QCOLS]
        value_outs[group][...] = total[:, 2 * QCOLS :].astype(jnp.bfloat16)
        for block, slot in enumerate(slots):
            for end, row in ((0, block * BLOCK), (1, block * BLOCK + BLOCK - 1)):
                line = total[row : row + 1, 2 * QCOLS :]
                at = 8 * group + 2 * slot + end
                edge_out[at : at + 1, :] = line.astype(jnp.bfloat16).astype(jnp.float32)


def project(offsets, blocks, weights, pieces, edge_early, after):
    counts = tuple(block.shape[0] for block in blocks)
    depth = blocks[0].shape[1]
    hbm = pl.BlockSpec(memory_space=pltpu.HBM)
    vmem = pl.BlockSpec(memory_space=pltpu.VMEM)
    return pl.pallas_call(
        functools.partial(project_kernel, counts),
        out_shape=[jax.ShapeDtypeStruct((rows, VCOLS), jnp.bfloat16) for rows in (BLOCK, ROWS)]
        + [jax.ShapeDtypeStruct((rows, 2 * QCOLS), jnp.float32) for rows in (BLOCK, ROWS)]
        + [jax.ShapeDtypeStruct((16, VCOLS), jnp.float32)],
        in_specs=[pl.BlockSpec(memory_space=pltpu.SMEM)] + [hbm] * (len(blocks) + 3 + len(pieces)) + [vmem, hbm],
        out_specs=[vmem] * 5,
        scratch_shapes=[
            pltpu.VMEM((ROWS, depth), jnp.bfloat16),
            pltpu.VMEM((depth, 2 * GCOLS), jnp.bfloat16),
            pltpu.VMEM((ROWS, GCOLS), jnp.float32),
            pltpu.VMEM((BLOCK, GCOLS), jnp.float32),
            pltpu.SemaphoreType.DMA((len(PARTS), len(blocks))),
            pltpu.SemaphoreType.DMA((len(PARTS), 3)),
            pltpu.SemaphoreType.DMA((len(pieces),)),
        ],
        compiler_params=pltpu.CompilerParams(vmem_limit_bytes=VMEM_LIMIT),
        cost_estimate=pl.CostEstimate(
            flops=3 * ROWS * depth * GCOLS, bytes_accessed=2 * depth * (ROWS + 2 * GCOLS), transcendentals=0
        ),
    )(offsets, *blocks, *weights, *pieces, edge_early, after)


def order_kernel(top, low, early, out):
    del top, low, early
    out[...] = jnp.zeros_like(out)


def arrived(top, low, early):
    hbm = pl.BlockSpec(memory_space=pltpu.HBM)
    return pl.pallas_call(
        order_kernel,
        out_shape=jax.ShapeDtypeStruct((8, 128), jnp.float32),
        in_specs=[hbm] * 3,
        out_specs=pl.BlockSpec(memory_space=pltpu.VMEM),
        compiler_params=pltpu.CompilerParams(vmem_limit_bytes=VMEM_LIMIT),
        cost_estimate=pl.CostEstimate(flops=ORDER_COST, bytes_accessed=15 * 10**6, transcendentals=0),
    )(top, low, early)


def state_kernel(place, *refs):
    values, query_keys = ((refs[0], refs[1]), (refs[2],)), ((refs[3], refs[4]), (refs[5],))
    (near, far), taps = refs[6:8], refs[8:10]
    convs, queries, (keep_out, give_out), states = refs[10:12], refs[12:14], refs[14:16], refs[16]
    x_at, even = place[0], place[1] == 0
    row = lax.broadcasted_iota(jnp.int32, (BLOCK, VCOLS), 0)
    ones = jnp.ones((8, ROWS), jnp.bfloat16)
    states[...] = jnp.zeros_like(states)
    for group in range(2):
        state, conv_out = states.at[group], convs[group]
        turned = [array[...].T * 0.5 for array in query_keys[group]]
        turned = turned[0] if len(turned) == 1 else jnp.concatenate(turned, axis=1)
        queries[group][...] = turned[:QCOLS]
        key = turned[QCOLS:]
        pieces = [
            array[start : start + BLOCK, :]
            for array in values[group]
            for start in range(0, array.shape[0], BLOCK)
        ]

        def line(ref, block, end):
            at = 8 * (1 - group) + 2 * (block % 4) + end
            return ref[at : at + 1, :]

        for number, block in enumerate(SLOTS):
            span = slice(number * BLOCK, (number + 1) * BLOCK)
            mid = pieces[number].astype(jnp.float32)
            opening = jnp.where((x_at + block) % NX == 0, line(far, block - 1, 1), line(near, block - 1, 1))
            before = jnp.where(even, opening, line(near, block, 1))
            closing = jnp.where((x_at + block) % NX == NX - 1, line(far, block + 1, 0), line(near, block + 1, 0))
            after = jnp.where(even, line(near, block, 0), closing)
            low = jnp.where(row == 0, before, pltpu.roll(mid, 1, 0))
            high = jnp.where(row == BLOCK - 1, after, pltpu.roll(mid, BLOCK - 1, 0))
            tap = taps[group]
            conv = tap[0:1, :] * low + tap[1:2, :] * mid + tap[2:3, :] * high
            conv_out[span, :] = conv.astype(jnp.bfloat16)
        for head in range(GROUP):
            feat = features(key[head * FEAT : (head + 1) * FEAT], 1.0).astype(jnp.bfloat16)
            start, stop = window_of(head)
            share = jnp.dot(feat, conv_out[:, start:stop], preferred_element_type=jnp.float32)
            state[:FROWS, start:stop] += jnp.where(head_mask(head, FROWS), share, 0.0)
            total = lax.dot_general(
                ones, feat, (((1,), (1,)), ((), ())), preferred_element_type=jnp.float32
            )
            state[FROWS + head : FROWS + head + 1, :FROWS] = total[0:1]
    same = place[2] == 1
    keep_out[...] = jnp.where(same, states[0], states[1])
    give_out[...] = jnp.where(same, states[1], states[0]).astype(jnp.bfloat16)


def states_of(place, values, query_keys, near, far, taps):
    vmem = pl.BlockSpec(memory_space=pltpu.VMEM)
    return pl.pallas_call(
        state_kernel,
        out_shape=[jax.ShapeDtypeStruct((ROWS, VCOLS), jnp.bfloat16)] * 2
        + [jax.ShapeDtypeStruct((QCOLS, ROWS), jnp.float32)] * 2
        + [
            jax.ShapeDtypeStruct((MROWS, VCOLS), jnp.float32),
            jax.ShapeDtypeStruct((MROWS, VCOLS), jnp.bfloat16),
        ],
        in_specs=[pl.BlockSpec(memory_space=pltpu.SMEM)] + [vmem] * 10,
        out_specs=[vmem] * 6,
        scratch_shapes=[pltpu.VMEM((2, MROWS, VCOLS), jnp.float32)],
        compiler_params=pltpu.CompilerParams(vmem_limit_bytes=VMEM_SMALL),
        cost_estimate=pl.CostEstimate(flops=6 * 10**9, bytes_accessed=8 * 10**6, transcendentals=0),
    )(place, *values, *query_keys, near, far, *taps)


def pack_kernel(start, query, key, value, *refs):
    outs, sems = refs[:-1], refs[-1]
    copies = []
    for index, out in enumerate(outs):
        count = out.shape[0]
        span = pl.ds(pl.multiple_of(start[index], 256), count)
        for kind, (ref, col, width) in enumerate(
            ((query, 0, QCOLS), (key, QCOLS, QCOLS), (value, 2 * QCOLS, VCOLS))
        ):
            copies.append(
                pltpu.make_async_copy(ref.at[span], out.at[:, pl.ds(col, width)], sems.at[index, kind])
            )
    for copy in copies:
        copy.start()
    for copy in copies:
        copy.wait()


def pack(weights, starts, counts):
    hbm = pl.BlockSpec(memory_space=pltpu.HBM)
    return pl.pallas_call(
        pack_kernel,
        out_shape=[jax.ShapeDtypeStruct((count, GCOLS), jnp.bfloat16) for count in counts],
        in_specs=[pl.BlockSpec(memory_space=pltpu.SMEM)] + [hbm] * 3,
        out_specs=[pl.BlockSpec(memory_space=pltpu.VMEM)] * len(counts),
        scratch_shapes=[pltpu.SemaphoreType.DMA((len(counts), 3))],
        compiler_params=pltpu.CompilerParams(vmem_limit_bytes=VMEM_LIMIT),
    )(jnp.stack(starts).astype(jnp.int32), *weights)


def split_kernel(place, keep, got, part_out, *lows):
    for step in range(NY):
        span = pl.ds(pl.multiple_of((place[0] + step) % NY * SPLIT, SPLIT), SPLIT)
        total = keep[span, :] + got[span, :].astype(jnp.float32)
        if step == 0:
            part_out[...] = total
        else:
            lows[step - 1][...] = total.astype(jnp.bfloat16)


def split(place, keep, got):
    vmem = pl.BlockSpec(memory_space=pltpu.VMEM)
    return pl.pallas_call(
        split_kernel,
        out_shape=[jax.ShapeDtypeStruct((SPLIT, VCOLS), jnp.float32)]
        + [jax.ShapeDtypeStruct((SPLIT, VCOLS), jnp.bfloat16)] * 3,
        in_specs=[pl.BlockSpec(memory_space=pltpu.SMEM), vmem, vmem],
        out_specs=[vmem] * 4,
        compiler_params=pltpu.CompilerParams(vmem_limit_bytes=VMEM_SMALL),
    )(place, keep, got)


def join_kernel(place, *refs):
    blocks, out = refs[:NX], refs[NX]
    width = blocks[0].shape[1]
    for step, block in enumerate(blocks):
        span = pl.ds(pl.multiple_of((place[0] + step) % NX * width, 128), width)
        out[:, span] = block[...]


def join(place, blocks):
    vmem = pl.BlockSpec(memory_space=pltpu.VMEM)
    rows, width = blocks[0].shape
    return pl.pallas_call(
        join_kernel,
        out_shape=jax.ShapeDtypeStruct((rows, NX * width), blocks[0].dtype),
        in_specs=[pl.BlockSpec(memory_space=pltpu.SMEM)] + [vmem] * NX,
        out_specs=vmem,
        compiler_params=pltpu.CompilerParams(vmem_limit_bytes=VMEM_SMALL),
    )(place, *blocks)


def attend_kernel(y_place, same, *refs):
    groups = (refs[0:3], refs[3:6])
    mine, theirs = refs[6:10], refs[10:14]
    outs, acc, states = refs[14:18], refs[18], refs[19]
    for step in range(NY):
        span = pl.ds(pl.multiple_of((y_place[0] + step) % NY * SPLIT, SPLIT), SPLIT)
        states[1 - same[0], span, :] = mine[step][...]
        states[same[0], span, :] = theirs[step][...]
    for number, (query, conv, gain) in enumerate(groups):
        state = states.at[number]
        acc[...] = jnp.zeros_like(acc)
        totals = state[FROWS : FROWS + 16, :FROWS]
        for head in range(GROUP):
            feat = features(query[head * FEAT : (head + 1) * FEAT, :], 2.0)
            denom = jnp.dot(totals, feat.astype(jnp.bfloat16), preferred_element_type=jnp.float32)
            scale = 1.0 / denom[head : head + 1, :]
            scaled = (feat * scale).astype(jnp.bfloat16)
            start, stop = window_of(head)
            part = state[:FROWS, start:stop]
            part = jnp.where(head_mask(head, FROWS), part, jnp.zeros_like(part))
            acc[:, start:stop] += lax.dot_general(
                scaled, part, (((0,), (0,)), ((), ())), preferred_element_type=jnp.float32
            )
        low = y_place[0] % 2
        spot = low if number == 0 else 1 - low
        span = pl.ds(pl.multiple_of(spot * VCOLS, VCOLS), VCOLS)
        for block, slot in enumerate(SLOTS):
            rows = slice(block * BLOCK, (block + 1) * BLOCK)
            mixed = acc[rows, :] * gain[3:4, :] + conv[rows, :].astype(jnp.float32)
            outs[slot][:, span] = mixed.astype(jnp.bfloat16)


def attend(y_place, same, groups, mine, theirs):
    vmem = pl.BlockSpec(memory_space=pltpu.VMEM)
    return pl.pallas_call(
        attend_kernel,
        out_shape=[jax.ShapeDtypeStruct((BLOCK, 2 * VCOLS), jnp.bfloat16)] * 4,
        in_specs=[pl.BlockSpec(memory_space=pltpu.SMEM)] * 2 + [vmem] * 14,
        out_specs=[vmem] * 4,
        scratch_shapes=[
            pltpu.VMEM((ROWS, VCOLS), jnp.float32),
            pltpu.VMEM((2, MROWS, VCOLS), jnp.bfloat16),
        ],
        compiler_params=pltpu.CompilerParams(vmem_limit_bytes=VMEM_SMALL),
    )(y_place, same, *[array for group in groups for array in group], *mine, *theirs)


def body(tokens, query_weight, key_weight, value_weight, conv_taps, norm_gain):
    tensor, seq = lax.axis_index("tensor"), lax.axis_index("seq")
    x_at, y_low = tensor // 2, tensor % 2
    core, z_odd = seq % 2, (seq // 2) % 2
    y_at = (seq // 16) * 2 + y_low
    rows = tokens.reshape(BLOCK, tokens.shape[-1])
    weights = (query_weight, key_weight, value_weight)
    half = rows.shape[1] // 2

    y_place = y_at.reshape(1).astype(jnp.int32)
    x_place = x_at.reshape(1).astype(jnp.int32)
    same = (core == y_low).astype(jnp.int32).reshape(1)
    part = BLOCK // 2

    def from_side(array):
        return receive(array, lambda x, y, z, c: (x, y + 2 * c - 1, z, c))

    def from_other(array):
        return receive(array, lambda x, y, z, c: (x, y ^ 1, z, c))

    one = from_x(rows, 1)
    three = from_x(rows, -1)
    two_top = from_x(one[:part], 1)
    two_low = from_x(three[part:], -1)

    base = core * half
    mixed_z = z_odd * 2 * PIECE
    packed = pack(weights, (base + mixed_z, base + mixed_z + PIECE, base + 4 * PIECE), (PIECE,) * 3)
    side = [from_side(array) for array in packed]
    side_z = [receive(array, lambda x, y, z, c: (x, y, z + 2 * c - 1, c)) for array in side[:2]]
    mine = [side[0], side[1], *side_z, side[2]]
    theirs = [from_core(array) for array in mine]
    flip = 2 * PIECE - mixed_z
    steps = jnp.stack([mixed_z, mixed_z + PIECE, flip, flip + PIECE, jnp.full_like(z_odd, 4 * PIECE)])
    offsets = jnp.concatenate([base + steps, (half - base) + steps]).astype(jnp.int32)

    blocks = (rows, one, three, two_top, two_low)
    place = jnp.concatenate([x_place, y_low.reshape(1).astype(jnp.int32), same])
    value_early, query_key_early, edge_early, small = project_early(
        blocks[:3], weights, conv_taps, norm_gain[None]
    )
    small_other = from_other(small)
    value_late, value_other, query_key_late, query_key_other, edge = project(
        offsets, blocks, weights, (*mine, *theirs), edge_early, arrived(two_top, two_low, small_other)
    )
    conv_own, conv_other, query_own, query_other, keep, give = states_of(
        place,
        (value_early, value_late, value_other),
        (query_key_early, query_key_late, query_key_other),
        from_other(edge),
        from_far(edge),
        (small, small_other),
    )

    total, *lows = split(y_place, keep, from_core(give))
    for step, low in zip((1, 2, 3), lows):
        total = total + from_y(low, -step).astype(jnp.float32)
    low = total.astype(jnp.bfloat16)
    for step in (1, -1, 2):
        total = total + from_z(low, step).astype(jnp.float32)
    low = total.astype(jnp.bfloat16)
    quarter = (total + from_z(low, 4).astype(jnp.float32)).astype(jnp.bfloat16)
    mine = [quarter] + [from_y(quarter, step) for step in (1, 2, 3)]
    theirs = [from_core(array) for array in mine]

    out = attend(
        y_place,
        same,
        ((query_own, conv_own, small), (query_other, conv_other, small_other)),
        mine,
        theirs,
    )
    result = join(x_place, [out[0], from_x(out[3], 1), from_x(out[2], 2), from_x(out[1], -1)])
    return result.reshape(tokens.shape)


def solution(mesh):
    return jax.shard_map(
        body,
        mesh=mesh,
        in_specs=(
            P("seq", "tensor", None),
            P(None, "tensor"),
            P(None, "tensor"),
            P(None, "tensor"),
            P(None, "tensor"),
            P("tensor"),
        ),
        out_specs=P("seq", "tensor", None),
        check_vma=False,
    )
```

profile of v0, /device:TPU:1, one launch (start us, length us, event | category | flops | bytes accessed | tf_op | source)
XLA Modules:
  0.0 148.4 jit_solution(14704176626020996956)
XLA Ops:
  0.0 2.0 %collective-permute-start.1 = (bf16[128,5120]{1,0:T(8,128)(2,1)}, bf16[128,5120]{1,0:T(8,128)(2,1)S(1)}, u32[]{:S(2)}, u32[]{:S(2)}) collective-permute-start(bf16[128,5120]{1,0:T(8,128)(2,1)} %bitcast.13), channel_id=1, source_target_pairs={{192,0},{193,1},{194,2},{195,3},{196,4},{197,5},{198,6},{199,7},{2... | collective-permute-start | bytes 3932168 | tf_op jit(solution)/shard_map/ppermute | solution.py:54
  4.0 4.1 %shard_map.65 = (bf16[512,896]{1,0:T(8,128)(2,1)}, bf16[512,896]{1,0:T(8,128)(2,1)}, bf16[512,896]{1,0:T(8,128)(2,1)}) custom-call(s32[3]{0:T(128)} %pad_add_fusion.2.start, bf16[5120,128]{1,0:T(8,128)(2,1)} %refs_5_.3, bf16[5120,128]{1,0:T(8,128)(2,1)} %refs_6_.3, bf16[5120,640]{1,0:T(8,128)(2,1)} %refs_7_.1), custom_call_target="tpu_custom_call" | custom-call | tf_op jit(solution)/shard_map/pallas_call | solution.py:394
  8.0 3.0 %collective-permute-start.4 = (bf16[512,896]{1,0:T(8,128)(2,1)}, bf16[512,896]{1,0:T(8,128)(2,1)S(1)}, u32[]{:S(2)}, u32[]{:S(2)}) collective-permute-start(bf16[512,896]{1,0:T(8,128)(2,1)} %get-tuple-element.32), channel_id=1, source_target_pairs={{48,0},{33,1},{50,2},{35,3},{52,4},{37,5},{54,6},{39,7},{56,8},{41... | collective-permute-start | bytes 2752520 | tf_op jit(solution)/shard_map/ppermute | solution.py:54
  11.7 10.0 %collective-permute-done.4.refs_8_ = bf16[512,896]{1,0:T(8,128)(2,1)S(1)} collective-permute-done((bf16[512,896]{1,0:T(8,128)(2,1)}, bf16[512,896]{1,0:T(8,128)(2,1)S(1)}, u32[]{:S(2)}, u32[]{:S(2)}) %collective-permute-start.4) | collective-permute-done | bytes 917536 | tf_op jit(solution)/shard_map/ppermute | solution.py:54
  21.7 5.6 %collective-permute-start.6 = (bf16[512,896]{1,0:T(8,128)(2,1)S(1)}, bf16[512,896]{1,0:T(8,128)(2,1)}, u32[]{:S(2)}, u32[]{:S(2)}) collective-permute-start(bf16[512,896]{1,0:T(8,128)(2,1)S(1)} %collective-permute-done.4.refs_8_), channel_id=1, source_target_pairs={{14,0},{3,1},{0,2},{5,3},{2,4},{7,5},{4,6},{9,7},{6,8},{11,9},{8,1... | collective-permute-start | bytes 2752520 | tf_op jit(solution)/shard_map/ppermute | solution.py:54
  27.3 4.3 %collective-permute-done.5.refs_9_ = bf16[512,896]{1,0:T(8,128)(2,1)} collective-permute-done((bf16[512,896]{1,0:T(8,128)(2,1)}, bf16[512,896]{1,0:T(8,128)(2,1)}, u32[]{:S(2)}, u32[]{:S(2)}) %collective-permute-start.5) | collective-permute-done | bytes 917536 | tf_op jit(solution)/shard_map/ppermute | solution.py:54
  31.5 5.6 %collective-permute-start.7 = (bf16[512,896]{1,0:T(8,128)(2,1)}, bf16[512,896]{1,0:T(8,128)(2,1)}, u32[]{:S(2)}, u32[]{:S(2)}) collective-permute-start(bf16[512,896]{1,0:T(8,128)(2,1)} %collective-permute-done.5.refs_9_), channel_id=1, source_target_pairs={{14,0},{3,1},{0,2},{5,3},{2,4},{7,5},{4,6},{9,7},{6,8},{11,9},{8,1... | collective-permute-start | bytes 2752520 | tf_op jit(solution)/shard_map/ppermute | solution.py:54
  38.2 1.8 %collective-permute-start.2 = (bf16[64,5120]{1,0:T(8,128)(2,1)S(1)}, bf16[64,5120]{1,0:T(8,128)(2,1)S(1)}, u32[]{:S(2)}, u32[]{:S(2)}) collective-permute-start(bf16[64,5120]{1,0:T(8,128)(2,1)S(1)} %slice.8), channel_id=1, source_target_pairs={{64,0},{65,1},{66,2},{67,3},{68,4},{69,5},{70,6},{71,7},{72,8},{73... | collective-permute-start | bytes 1966088 | tf_op jit(solution)/shard_map/ppermute | solution.py:54
  40.6 8.6 %shard_map.64 = (bf16[384,640]{1,0:T(8,128)(2,1)}, f32[384,256]{1,0:T(8,128)}, f32[8,640]{1,0:T(8,128)}, f32[4,640]{1,0:T(4,128)}) custom-call(bf16[128,5120]{1,0:T(8,128)(2,1)} %bitcast.15, bf16[128,5120]{1,0:T(8,128)(2,1)} %copy-done.10, bf16[128,5120]{1,0:T(8,128)(2,1)} %copy-done.9, bf16[5120,128]{1,0:T(8,128)(2,1)} %refs_5_.3, ...), custom_call_target="tpu_custom_call" | custom-call | flops 3000000000 | bytes 3000000 | tf_op jit(solution)/shard_map/pallas_call | solution.py:169
  50.1 2.3 %collective-permute-done.14.early.refs_9_.refs_5_ = f32[4,640]{1,0:T(4,128)S(1)} collective-permute-done((f32[4,640]{1,0:T(4,128)}, f32[4,640]{1,0:T(4,128)S(1)}, u32[]{:S(2)}, u32[]{:S(2)}) %collective-permute-start.14) | collective-permute-done | bytes 10272 | tf_op jit(solution)/shard_map/ppermute | solution.py:54
  60.7 12.4 %shard_map.67 = (bf16[128,640]{1,0:T(8,128)(2,1)}, bf16[512,640]{1,0:T(8,128)(2,1)}, f32[128,256]{1,0:T(8,128)}, f32[512,256]{1,0:T(8,128)}, f32[16,640]{1,0:T(8,128)}) custom-call(s32[10]{0:T(128)} %pad_add_fusion.1.offsets, bf16[128,5120]{1,0:T(8,128)(2,1)} %bitcast.16, bf16[128,5120]{1,0:T(8,128)(2,1)} %copy-done.10, bf16[128,5120]{1,0:T(8,128)(2,1)} %copy-done.9, ...), custom_call_target="tpu_custom_call" | custom-call | flops 7046430720 | bytes 23592960 | tf_op jit(solution)/shard_map/pallas_call | solution.py:266
  73.0 2.5 %collective-permute-start.16 = (f32[16,640]{1,0:T(8,128)}, f32[16,640]{1,0:T(8,128)S(1)}, u32[]{:S(2)}, u32[]{:S(2)}) collective-permute-start(f32[16,640]{1,0:T(8,128)} %get-tuple-element.42), channel_id=1, source_target_pairs={{32,1},{33,2},{34,3},{35,4},{36,5},{37,6},{38,7},{39,8},{40,9},{41... | collective-permute-start | bytes 122888 | tf_op jit(solution)/shard_map/ppermute | solution.py:82
  75.6 2.5 %collective-permute-start.15 = (f32[16,640]{1,0:T(8,128)}, f32[16,640]{1,0:T(8,128)S(1)}, u32[]{:S(2)}, u32[]{:S(2)}) collective-permute-start(f32[16,640]{1,0:T(8,128)} %get-tuple-element.42), channel_id=1, source_target_pairs={{32,0},{33,1},{34,2},{35,3},{36,4},{37,5},{38,6},{39,7},{40,8},{41... | collective-permute-start | bytes 122888 | tf_op jit(solution)/shard_map/ppermute | solution.py:54
  83.7 3.0 %shard_map.68 = (bf16[512,640]{1,0:T(8,128)(2,1)S(1)}, bf16[512,640]{1,0:T(8,128)(2,1)S(1)}, f32[128,512]{1,0:T(8,128)S(1)}, f32[128,512]{1,0:T(8,128)S(1)}, f32...) custom-call(s32[3]{0:T(128)S(1)} %pad_add_fusion.place, bf16[384,640]{1,0:T(8,128)(2,1)S(1)} %copy-done.3, ...), custom_call_target="tpu_custom_call" | custom-call | flops 6000000000 | bytes 8000000 | tf_op jit(solution)/shard_map/pallas_call | solution.py:358
  86.8 1.5 collective-permute-done.17.got
  88.4 1.5 %collective-permute-start.18 = (bf16[48,640]{1,0:T(8,128)(2,1)S(1)}, bf16[48,640]{1,0:T(8,128)(2,1)S(1)}, u32[]{:S(2)}, u32[]{:S(2)}) collective-permute-start(bf16[48,640]{1,0:T(8,128)(2,1)S(1)} %get-tuple-element.50), channel_id=1, source_target_pairs={{48,0},{49,1},{50,2},{51,3},{52,4},{53,5},{54,6},{55,7},{56,8},{57... | collective-permute-start | bytes 184328 | tf_op jit(solution)/shard_map/ppermute | solution.py:54
  89.9 3.8 %collective-permute-start.19 = (bf16[48,640]{1,0:T(8,128)(2,1)S(1)}, bf16[48,640]{1,0:T(8,128)(2,1)S(1)}, u32[]{:S(2)}, u32[]{:S(2)}) collective-permute-start(bf16[48,640]{1,0:T(8,128)(2,1)S(1)} %get-tuple-element.51), channel_id=1, source_target_pairs={{16,0},{17,1},{18,2},{19,3},{20,4},{21,5},{22,6},{23,7},{24,8},{25... | collective-permute-start | bytes 184328 | tf_op jit(solution)/shard_map/ppermute | solution.py:54
  93.7 2.0 %collective-permute-start.20 = (bf16[48,640]{1,0:T(8,128)(2,1)S(1)}, bf16[48,640]{1,0:T(8,128)(2,1)S(1)}, u32[]{:S(2)}, u32[]{:S(2)}) collective-permute-start(bf16[48,640]{1,0:T(8,128)(2,1)S(1)} %get-tuple-element.52), channel_id=1, source_target_pairs={{32,0},{33,1},{34,2},{35,3},{36,4},{37,5},{38,6},{39,7},{40,8},{41... | collective-permute-start | bytes 184328 | tf_op jit(solution)/shard_map/ppermute | solution.py:54
  95.7 1.3 collective-permute-done.19
  97.1 3.9 %collective-permute-start.23 = (bf16[48,640]{1,0:T(8,128)(2,1)S(1)}, bf16[48,640]{1,0:T(8,128)(2,1)S(1)}, u32[]{:S(2)}, u32[]{:S(2)}) collective-permute-start(bf16[48,640]{1,0:T(8,128)(2,1)S(1)} %fusion), channel_id=1, source_target_pairs={{4,0},{5,1},{6,2},{7,3},{8,4},{9,5},{10,6},{11,7},{12,8},{13,9},{1... | collective-permute-start | bytes 184328 | tf_op jit(solution)/shard_map/ppermute | solution.py:54
  101.3 2.4 %collective-permute-start.21 = (bf16[48,640]{1,0:T(8,128)(2,1)S(1)}, bf16[48,640]{1,0:T(8,128)(2,1)S(1)}, u32[]{:S(2)}, u32[]{:S(2)}) collective-permute-start(bf16[48,640]{1,0:T(8,128)(2,1)S(1)} %fusion), channel_id=1, source_target_pairs={{2,0},{3,1},{4,2},{5,3},{6,4},{7,5},{8,6},{9,7},{10,8},{11,9},{12,... | collective-permute-start | bytes 184328 | tf_op jit(solution)/shard_map/ppermute | solution.py:54
  103.6 1.6 %collective-permute-done.22 = bf16[48,640]{1,0:T(8,128)(2,1)S(1)} collective-permute-done((bf16[48,640]{1,0:T(8,128)(2,1)S(1)}, bf16[48,640]{1,0:T(8,128)(2,1)S(1)}, u32[]{:S(2)}, u32[]{:S(2)}) %collective-permute-start.22) | collective-permute-done | bytes 61472 | tf_op jit(solution)/shard_map/ppermute | solution.py:54
  105.4 4.4 %collective-permute-start.24 = (bf16[48,640]{1,0:T(8,128)(2,1)S(1)}, bf16[48,640]{1,0:T(8,128)(2,1)S(1)}, u32[]{:S(2)}, u32[]{:S(2)}) collective-permute-start(bf16[48,640]{1,0:T(8,128)(2,1)S(1)} %get-tuple-element.57), channel_id=1, source_target_pairs={{8,0},{9,1},{10,2},{11,3},{12,4},{13,5},{14,6},{15,7},{0,8},{1,9},... | collective-permute-start | bytes 184328 | tf_op jit(solution)/shard_map/ppermute | solution.py:54
  109.8 2.7 %collective-permute-done.24 = bf16[48,640]{1,0:T(8,128)(2,1)S(1)} collective-permute-done((bf16[48,640]{1,0:T(8,128)(2,1)S(1)}, bf16[48,640]{1,0:T(8,128)(2,1)S(1)}, u32[]{:S(2)}, u32[]{:S(2)}) %collective-permute-start.24) | collective-permute-done | bytes 61472 | tf_op jit(solution)/shard_map/ppermute | solution.py:54
  113.5 3.1 %collective-permute-start.26 = (bf16[48,640]{1,0:T(8,128)(2,1)S(1)}, bf16[48,640]{1,0:T(8,128)(2,1)S(1)}, u32[]{:S(2)}, u32[]{:S(2)}) collective-permute-start(bf16[48,640]{1,0:T(8,128)(2,1)S(1)} %add_convert_fusion.refs_6_), channel_id=1, source_target_pairs={{16,0},{17,1},{18,2},{19,3},{20,4},{21,5},{22,6},{23,7},{24,8},{25... | collective-permute-start | bytes 184328 | tf_op jit(solution)/shard_map/ppermute | solution.py:54
  116.7 4.6 %collective-permute-start.28 = (bf16[48,640]{1,0:T(8,128)(2,1)S(1)}, bf16[48,640]{1,0:T(8,128)(2,1)S(1)}, u32[]{:S(2)}, u32[]{:S(2)}) collective-permute-start(bf16[48,640]{1,0:T(8,128)(2,1)S(1)} %add_convert_fusion.refs_6_), channel_id=1, source_target_pairs={{1,0},{0,1},{3,2},{2,3},{5,4},{4,5},{7,6},{6,7},{9,8},{8,9},{11,10... | collective-permute-start | bytes 184328 | tf_op jit(solution)/shard_map/ppermute | solution.py:54
  122.2 1.6 %collective-permute-start.30 = (bf16[48,640]{1,0:T(8,128)(2,1)S(1)}, bf16[48,640]{1,0:T(8,128)(2,1)S(1)}, u32[]{:S(2)}, u32[]{:S(2)}) collective-permute-start(bf16[48,640]{1,0:T(8,128)(2,1)S(1)} %collective-permute-done.26.refs_8_), channel_id=1, source_target_pairs={{1,0},{0,1},{3,2},{2,3},{5,4},{4,5},{7,6},{6,7},{9,8},{8,9},{11,10... | collective-permute-start | bytes 184328 | tf_op jit(solution)/shard_map/ppermute | solution.py:54
  123.7 1.4 collective-permute-start.29
  126.0 3.0 %shard_map.70 = (bf16[128,1280]{1,0:T(8,128)(2,1)S(1)}, bf16[128,1280]{1,0:T(8,128)(2,1)S(1)}, bf16[128,1280]{1,0:T(8,128)(2,1)S(1)}, bf16[128,1280]{1,0:T(8,128)(2,1)S(1)}) custom-call(s32[1]{0:T(128)} %bitcast.1.place.y_place, s32[1]{0:T(128)} %bitcast.2.same, f32[128,512]{1,0:T(8,128)S(1)} %get-tuple-element.43.refs_0_, ...), custom_call_target="tpu_custom_call" | custom-call | tf_op jit(solution)/shard_map/pallas_call | solution.py:480
  130.5 7.5 %collective-permute-done.32.refs_1_ = bf16[128,1280]{1,0:T(8,128)(2,1)S(1)} collective-permute-done((bf16[128,1280]{1,0:T(8,128)(2,1)S(1)}, bf16[128,1280]{1,0:T(8,128)(2,1)S(1)}, u32[]{:S(2)}, u32[]{:S(2)}) %collective-permute-start.32) | collective-permute-done | bytes 327712 | tf_op jit(solution)/shard_map/ppermute | solution.py:54
  138.0 1.4 collective-permute-done.33.refs_2_
  139.3 7.9 %collective-permute-done.34.refs_3_ = bf16[128,1280]{1,0:T(8,128)(2,1)S(1)} collective-permute-done((bf16[128,1280]{1,0:T(8,128)(2,1)S(1)}, bf16[128,1280]{1,0:T(8,128)(2,1)S(1)}, u32[]{:S(2)}, u32[]{:S(2)}) %collective-permute-start.34) | collective-permute-done | bytes 327712 | tf_op jit(solution)/shard_map/ppermute | solution.py:54
  (91 shorter events, 25.1 us)
Async XLA Ops:
  0.0 37.1 %collective-permute-start.1 = (bf16[128,5120]{1,0:T(8,128)(2,1)}, bf16[128,5120]{1,0:T(8,128)(2,1)S(1)}, u32[]{:S(2)}, u32[]{:S(2)}) collective-permute-start(bf16[128,5120]{1,0:T(8,128)(2,1)} %bitcast.13), channel_id=1, source_target_pairs={{192,0},{193,1},{194,2},{195,3},{196,4},{197,5},{198,6},{199,7},{2... | collective-permute-start | bytes 3932168 | tf_op jit(solution)/shard_map/ppermute | solution.py:54
  2.0 35.2 %collective-permute-start = (bf16[128,5120]{1,0:T(8,128)(2,1)}, bf16[128,5120]{1,0:T(8,128)(2,1)S(1)}, u32[]{:S(2)}, u32[]{:S(2)}) collective-permute-start(bf16[128,5120]{1,0:T(8,128)(2,1)} %bitcast.14), channel_id=1, source_target_pairs={{64,0},{65,1},{66,2},{67,3},{68,4},{69,5},{70,6},{71,7},{72,8},{73... | collective-permute-start | bytes 3932168 | tf_op jit(solution)/shard_map/ppermute | solution.py:54
  8.0 13.7 %collective-permute-start.4 = (bf16[512,896]{1,0:T(8,128)(2,1)}, bf16[512,896]{1,0:T(8,128)(2,1)S(1)}, u32[]{:S(2)}, u32[]{:S(2)}) collective-permute-start(bf16[512,896]{1,0:T(8,128)(2,1)} %get-tuple-element.32), channel_id=1, source_target_pairs={{48,0},{33,1},{50,2},{35,3},{52,4},{37,5},{54,6},{39,7},{56,8},{41... | collective-permute-start | bytes 2752520 | tf_op jit(solution)/shard_map/ppermute | solution.py:54
  11.0 20.5 %collective-permute-start.5 = (bf16[512,896]{1,0:T(8,128)(2,1)}, bf16[512,896]{1,0:T(8,128)(2,1)}, u32[]{:S(2)}, u32[]{:S(2)}) collective-permute-start(bf16[512,896]{1,0:T(8,128)(2,1)} %get-tuple-element.33), channel_id=1, source_target_pairs={{48,0},{33,1},{50,2},{35,3},{52,4},{37,5},{54,6},{39,7},{56,8},{41... | collective-permute-start | bytes 2752520 | tf_op jit(solution)/shard_map/ppermute | solution.py:54
  11.5 37.8 %collective-permute-start.8 = (bf16[512,896]{1,0:T(8,128)(2,1)}, bf16[512,896]{1,0:T(8,128)(2,1)}, u32[]{:S(2)}, u32[]{:S(2)}) collective-permute-start(bf16[512,896]{1,0:T(8,128)(2,1)} %get-tuple-element.34), channel_id=1, source_target_pairs={{48,0},{33,1},{50,2},{35,3},{52,4},{37,5},{54,6},{39,7},{56,8},{41... | collective-permute-start | bytes 2752520 | tf_op jit(solution)/shard_map/ppermute | solution.py:54
  21.7 31.3 %collective-permute-start.6 = (bf16[512,896]{1,0:T(8,128)(2,1)S(1)}, bf16[512,896]{1,0:T(8,128)(2,1)}, u32[]{:S(2)}, u32[]{:S(2)}) collective-permute-start(bf16[512,896]{1,0:T(8,128)(2,1)S(1)} %collective-permute-done.4.refs_8_), channel_id=1, source_target_pairs={{14,0},{3,1},{0,2},{5,3},{2,4},{7,5},{4,6},{9,7},{6,8},{11,9},{8,1... | collective-permute-start | bytes 2752520 | tf_op jit(solution)/shard_map/ppermute | solution.py:54
  31.5 21.5 %collective-permute-start.7 = (bf16[512,896]{1,0:T(8,128)(2,1)}, bf16[512,896]{1,0:T(8,128)(2,1)}, u32[]{:S(2)}, u32[]{:S(2)}) collective-permute-start(bf16[512,896]{1,0:T(8,128)(2,1)} %collective-permute-done.5.refs_9_), channel_id=1, source_target_pairs={{14,0},{3,1},{0,2},{5,3},{2,4},{7,5},{4,6},{9,7},{6,8},{11,9},{8,1... | collective-permute-start | bytes 2752520 | tf_op jit(solution)/shard_map/ppermute | solution.py:54
  37.1 17.3 %collective-permute-start.3 = (bf16[64,5120]{1,0:T(8,128)(2,1)S(1)}, bf16[64,5120]{1,0:T(8,128)(2,1)S(1)}, u32[]{:S(2)}, u32[]{:S(2)}) collective-permute-start(bf16[64,5120]{1,0:T(8,128)(2,1)S(1)} %slice.9), channel_id=1, source_target_pairs={{192,0},{193,1},{194,2},{195,3},{196,4},{197,5},{198,6},{199,7},{2... | collective-permute-start | bytes 1966088 | tf_op jit(solution)/shard_map/ppermute | solution.py:54
  38.2 16.6 %collective-permute-start.2 = (bf16[64,5120]{1,0:T(8,128)(2,1)S(1)}, bf16[64,5120]{1,0:T(8,128)(2,1)S(1)}, u32[]{:S(2)}, u32[]{:S(2)}) collective-permute-start(bf16[64,5120]{1,0:T(8,128)(2,1)S(1)} %slice.8), channel_id=1, source_target_pairs={{64,0},{65,1},{66,2},{67,3},{68,4},{69,5},{70,6},{71,7},{72,8},{73... | collective-permute-start | bytes 1966088 | tf_op jit(solution)/shard_map/ppermute | solution.py:54
  49.3 3.1 %collective-permute-start.14 = (f32[4,640]{1,0:T(4,128)}, f32[4,640]{1,0:T(4,128)S(1)}, u32[]{:S(2)}, u32[]{:S(2)}) collective-permute-start(f32[4,640]{1,0:T(4,128)} %get-tuple-element.36.refs_8_.refs_2_), channel_id=1, source_target_pairs={{32,0},{33,1},{34,2},{35,3},{36,4},{37,5},{38,6},{39,7},{40,8},{41... | collective-permute-start | bytes 30728 | tf_op jit(solution)/shard_map/ppermute | solution.py:54
  52.4 5.4 %collective-permute-start.9 = (bf16[512,896]{1,0:T(8,128)(2,1)S(1)}, bf16[512,896]{1,0:T(8,128)(2,1)S(1)}, u32[]{:S(2)}, u32[]{:S(2)}) collective-permute-start(bf16[512,896]{1,0:T(8,128)(2,1)S(1)} %collective-permute-done.4.refs_8_), channel_id=1, source_target_pairs={{1,0},{0,1},{3,2},{2,3},{5,4},{4,5},{7,6},{6,7},{9,8},{8,9},{11,10... | collective-permute-start | bytes 2752520 | tf_op jit(solution)/shard_map/ppermute | solution.py:54
  52.9 4.9 %collective-permute-start.10 = (bf16[512,896]{1,0:T(8,128)(2,1)}, bf16[512,896]{1,0:T(8,128)(2,1)S(1)}, u32[]{:S(2)}, u32[]{:S(2)}) collective-permute-start(bf16[512,896]{1,0:T(8,128)(2,1)} %collective-permute-done.5.refs_9_), channel_id=1, source_target_pairs={{1,0},{0,1},{3,2},{2,3},{5,4},{4,5},{7,6},{6,7},{9,8},{8,9},{11,10... | collective-permute-start | bytes 2752520 | tf_op jit(solution)/shard_map/ppermute | solution.py:54
  53.0 5.0 %collective-permute-start.13 = (bf16[512,896]{1,0:T(8,128)(2,1)}, bf16[512,896]{1,0:T(8,128)(2,1)}, u32[]{:S(2)}, u32[]{:S(2)}) collective-permute-start(bf16[512,896]{1,0:T(8,128)(2,1)} %collective-permute-done.8.refs_12_), channel_id=1, source_target_pairs={{1,0},{0,1},{3,2},{2,3},{5,4},{4,5},{7,6},{6,7},{9,8},{8,9},{11,10... | collective-permute-start | bytes 2752520 | tf_op jit(solution)/shard_map/ppermute | solution.py:54
  54.5 4.9 %collective-permute-start.11 = (bf16[512,896]{1,0:T(8,128)(2,1)}, bf16[512,896]{1,0:T(8,128)(2,1)}, u32[]{:S(2)}, u32[]{:S(2)}) collective-permute-start(bf16[512,896]{1,0:T(8,128)(2,1)} %collective-permute-done.6.refs_10_), channel_id=1, source_target_pairs={{1,0},{0,1},{3,2},{2,3},{5,4},{4,5},{7,6},{6,7},{9,8},{8,9},{11,10... | collective-permute-start | bytes 2752520 | tf_op jit(solution)/shard_map/ppermute | solution.py:54
  56.1 4.5 %collective-permute-start.12 = (bf16[512,896]{1,0:T(8,128)(2,1)}, bf16[512,896]{1,0:T(8,128)(2,1)}, u32[]{:S(2)}, u32[]{:S(2)}) collective-permute-start(bf16[512,896]{1,0:T(8,128)(2,1)} %collective-permute-done.7.refs_11_), channel_id=1, source_target_pairs={{1,0},{0,1},{3,2},{2,3},{5,4},{4,5},{7,6},{6,7},{9,8},{8,9},{11,10... | collective-permute-start | bytes 2752520 | tf_op jit(solution)/shard_map/ppermute | solution.py:54
  73.0 5.5 %collective-permute-start.16 = (f32[16,640]{1,0:T(8,128)}, f32[16,640]{1,0:T(8,128)S(1)}, u32[]{:S(2)}, u32[]{:S(2)}) collective-permute-start(f32[16,640]{1,0:T(8,128)} %get-tuple-element.42), channel_id=1, source_target_pairs={{32,1},{33,2},{34,3},{35,4},{36,5},{37,6},{38,7},{39,8},{40,9},{41... | collective-permute-start | bytes 122888 | tf_op jit(solution)/shard_map/ppermute | solution.py:82
  75.6 4.1 %collective-permute-start.15 = (f32[16,640]{1,0:T(8,128)}, f32[16,640]{1,0:T(8,128)S(1)}, u32[]{:S(2)}, u32[]{:S(2)}) collective-permute-start(f32[16,640]{1,0:T(8,128)} %get-tuple-element.42), channel_id=1, source_target_pairs={{32,0},{33,1},{34,2},{35,3},{36,4},{37,5},{38,6},{39,7},{40,8},{41... | collective-permute-start | bytes 122888 | tf_op jit(solution)/shard_map/ppermute | solution.py:54
  88.4 7.3 %collective-permute-start.18 = (bf16[48,640]{1,0:T(8,128)(2,1)S(1)}, bf16[48,640]{1,0:T(8,128)(2,1)S(1)}, u32[]{:S(2)}, u32[]{:S(2)}) collective-permute-start(bf16[48,640]{1,0:T(8,128)(2,1)S(1)} %get-tuple-element.50), channel_id=1, source_target_pairs={{48,0},{49,1},{50,2},{51,3},{52,4},{53,5},{54,6},{55,7},{56,8},{57... | collective-permute-start | bytes 184328 | tf_op jit(solution)/shard_map/ppermute | solution.py:54
  89.9 7.1 %collective-permute-start.19 = (bf16[48,640]{1,0:T(8,128)(2,1)S(1)}, bf16[48,640]{1,0:T(8,128)(2,1)S(1)}, u32[]{:S(2)}, u32[]{:S(2)}) collective-permute-start(bf16[48,640]{1,0:T(8,128)(2,1)S(1)} %get-tuple-element.51), channel_id=1, source_target_pairs={{16,0},{17,1},{18,2},{19,3},{20,4},{21,5},{22,6},{23,7},{24,8},{25... | collective-permute-start | bytes 184328 | tf_op jit(solution)/shard_map/ppermute | solution.py:54
  93.7 3.4 %collective-permute-start.20 = (bf16[48,640]{1,0:T(8,128)(2,1)S(1)}, bf16[48,640]{1,0:T(8,128)(2,1)S(1)}, u32[]{:S(2)}, u32[]{:S(2)}) collective-permute-start(bf16[48,640]{1,0:T(8,128)(2,1)S(1)} %get-tuple-element.52), channel_id=1, source_target_pairs={{32,0},{33,1},{34,2},{35,3},{36,4},{37,5},{38,6},{39,7},{40,8},{41... | collective-permute-start | bytes 184328 | tf_op jit(solution)/shard_map/ppermute | solution.py:54
  97.1 6.5 %collective-permute-start.23 = (bf16[48,640]{1,0:T(8,128)(2,1)S(1)}, bf16[48,640]{1,0:T(8,128)(2,1)S(1)}, u32[]{:S(2)}, u32[]{:S(2)}) collective-permute-start(bf16[48,640]{1,0:T(8,128)(2,1)S(1)} %fusion), channel_id=1, source_target_pairs={{4,0},{5,1},{6,2},{7,3},{8,4},{9,5},{10,6},{11,7},{12,8},{13,9},{1... | collective-permute-start | bytes 184328 | tf_op jit(solution)/shard_map/ppermute | solution.py:54
  101.0 4.3 %collective-permute-start.22 = (bf16[48,640]{1,0:T(8,128)(2,1)S(1)}, bf16[48,640]{1,0:T(8,128)(2,1)S(1)}, u32[]{:S(2)}, u32[]{:S(2)}) collective-permute-start(bf16[48,640]{1,0:T(8,128)(2,1)S(1)} %fusion), channel_id=1, source_target_pairs={{14,0},{15,1},{0,2},{1,3},{2,4},{3,5},{4,6},{5,7},{6,8},{7,9},{8,1... | collective-permute-start | bytes 184328 | tf_op jit(solution)/shard_map/ppermute | solution.py:54
  101.3 4.1 %collective-permute-start.21 = (bf16[48,640]{1,0:T(8,128)(2,1)S(1)}, bf16[48,640]{1,0:T(8,128)(2,1)S(1)}, u32[]{:S(2)}, u32[]{:S(2)}) collective-permute-start(bf16[48,640]{1,0:T(8,128)(2,1)S(1)} %fusion), channel_id=1, source_target_pairs={{2,0},{3,1},{4,2},{5,3},{6,4},{7,5},{8,6},{9,7},{10,8},{11,9},{12,... | collective-permute-start | bytes 184328 | tf_op jit(solution)/shard_map/ppermute | solution.py:54
  105.4 7.1 %collective-permute-start.24 = (bf16[48,640]{1,0:T(8,128)(2,1)S(1)}, bf16[48,640]{1,0:T(8,128)(2,1)S(1)}, u32[]{:S(2)}, u32[]{:S(2)}) collective-permute-start(bf16[48,640]{1,0:T(8,128)(2,1)S(1)} %get-tuple-element.57), channel_id=1, source_target_pairs={{8,0},{9,1},{10,2},{11,3},{12,4},{13,5},{14,6},{15,7},{0,8},{1,9},... | collective-permute-start | bytes 184328 | tf_op jit(solution)/shard_map/ppermute | solution.py:54
  112.5 8.8 %collective-permute-start.27 = (bf16[48,640]{1,0:T(8,128)(2,1)S(1)}, bf16[48,640]{1,0:T(8,128)(2,1)S(1)}, u32[]{:S(2)}, u32[]{:S(2)}) collective-permute-start(bf16[48,640]{1,0:T(8,128)(2,1)S(1)} %add_convert_fusion.refs_6_), channel_id=1, source_target_pairs={{48,0},{49,1},{50,2},{51,3},{52,4},{53,5},{54,6},{55,7},{56,8},{57... | collective-permute-start | bytes 184328 | tf_op jit(solution)/shard_map/ppermute | solution.py:54
  113.5 8.6 %collective-permute-start.26 = (bf16[48,640]{1,0:T(8,128)(2,1)S(1)}, bf16[48,640]{1,0:T(8,128)(2,1)S(1)}, u32[]{:S(2)}, u32[]{:S(2)}) collective-permute-start(bf16[48,640]{1,0:T(8,128)(2,1)S(1)} %add_convert_fusion.refs_6_), channel_id=1, source_target_pairs={{16,0},{17,1},{18,2},{19,3},{20,4},{21,5},{22,6},{23,7},{24,8},{25... | collective-permute-start | bytes 184328 | tf_op jit(solution)/shard_map/ppermute | solution.py:54
  116.7 7.0 %collective-permute-start.25 = (bf16[48,640]{1,0:T(8,128)(2,1)S(1)}, bf16[48,640]{1,0:T(8,128)(2,1)S(1)}, u32[]{:S(2)}, u32[]{:S(2)}) collective-permute-start(bf16[48,640]{1,0:T(8,128)(2,1)S(1)} %add_convert_fusion.refs_6_), channel_id=1, source_target_pairs={{32,0},{33,1},{34,2},{35,3},{36,4},{37,5},{38,6},{39,7},{40,8},{41... | collective-permute-start | bytes 184328 | tf_op jit(solution)/shard_map/ppermute | solution.py:54
  116.7 8.4 %collective-permute-start.28 = (bf16[48,640]{1,0:T(8,128)(2,1)S(1)}, bf16[48,640]{1,0:T(8,128)(2,1)S(1)}, u32[]{:S(2)}, u32[]{:S(2)}) collective-permute-start(bf16[48,640]{1,0:T(8,128)(2,1)S(1)} %add_convert_fusion.refs_6_), channel_id=1, source_target_pairs={{1,0},{0,1},{3,2},{2,3},{5,4},{4,5},{7,6},{6,7},{9,8},{8,9},{11,10... | collective-permute-start | bytes 184328 | tf_op jit(solution)/shard_map/ppermute | solution.py:54
  121.3 3.8 %collective-permute-start.31 = (bf16[48,640]{1,0:T(8,128)(2,1)S(1)}, bf16[48,640]{1,0:T(8,128)(2,1)S(1)}, u32[]{:S(2)}, u32[]{:S(2)}) collective-permute-start(bf16[48,640]{1,0:T(8,128)(2,1)S(1)} %collective-permute-done.27.refs_9_), channel_id=1, source_target_pairs={{1,0},{0,1},{3,2},{2,3},{5,4},{4,5},{7,6},{6,7},{9,8},{8,9},{11,10... | collective-permute-start | bytes 184328 | tf_op jit(solution)/shard_map/ppermute | solution.py:54
  128.9 9.0 %collective-permute-start.32 = (bf16[128,1280]{1,0:T(8,128)(2,1)S(1)}, bf16[128,1280]{1,0:T(8,128)(2,1)S(1)}, u32[]{:S(2)}, u32[]{:S(2)}) collective-permute-start(bf16[128,1280]{1,0:T(8,128)(2,1)S(1)} %get-tuple-element.54), channel_id=1, source_target_pairs={{64,0},{65,1},{66,2},{67,3},{68,4},{69,5},{70,6},{71,7},{72,8},{73... | collective-permute-start | bytes 983048 | tf_op jit(solution)/shard_map/ppermute | solution.py:54
  129.1 10.3 %collective-permute-start.33 = (bf16[128,1280]{1,0:T(8,128)(2,1)S(1)}, bf16[128,1280]{1,0:T(8,128)(2,1)S(1)}, u32[]{:S(2)}, u32[]{:S(2)}) collective-permute-start(bf16[128,1280]{1,0:T(8,128)(2,1)S(1)} %get-tuple-element.55), channel_id=1, source_target_pairs={{128,0},{129,1},{130,2},{131,3},{132,4},{133,5},{134,6},{135,7},{1... | collective-permute-start | bytes 983048 | tf_op jit(solution)/shard_map/ppermute | solution.py:54
  130.1 17.1 %collective-permute-start.34 = (bf16[128,1280]{1,0:T(8,128)(2,1)S(1)}, bf16[128,1280]{1,0:T(8,128)(2,1)S(1)}, u32[]{:S(2)}, u32[]{:S(2)}) collective-permute-start(bf16[128,1280]{1,0:T(8,128)(2,1)S(1)} %get-tuple-element.56), channel_id=1, source_target_pairs={{192,0},{193,1},{194,2},{195,3},{196,4},{197,5},{198,6},{199,7},{2... | collective-permute-start | bytes 983048 | tf_op jit(solution)/shard_map/ppermute | solution.py:54
  (20 other events, 162.9 us)
where the time goes:
time: 149 us; the launch traced here: 148 us
  starting transfers between devices  60.2 us (40%)
  waiting for transfers between devices  46.8 us (31%)
  Pallas kernels  32.8 us (22%)
  local copies, waits for them, and re-layouts  6.95 us (5%)
  other arithmetic  1.53 us (1%)
    ppermute x34, starting transfers between devices, receive(): return lax.ppermute(array, AXES, pairs)  57.6 us
    ppermute x34, waiting for transfers between devices, receive(): return lax.ppermute(array, AXES, pairs)  46.4 us
    pallas_call x1, Pallas kernels, project(): pl.pallas_call(functools.partial(project_kernel, counts), out_shape=[jax....  12.4 us
    pallas_call x1, Pallas kernels, project_early(): pl.pallas_call(functools.partial(early_kernel, counts), out_shape=[jax.Sh...  8.64 us
    unnamed x34, local copies, waits for them, and re-layouts  6.19 us
    pallas_call x1, Pallas kernels, pack(): pl.pallas_call(pack_kernel, out_shape=[jax.ShapeDtypeStruct((count, GCOLS...  4.05 us
    pallas_call x1, Pallas kernels, states_of(): pl.pallas_call(state_kernel, out_shape=[jax.ShapeDtypeStruct((ROWS, VCOLS...  2.99 us
  transfers between devices with their start and end apart: 35, of which 19 were waited for; matrix products, arithmetic and copies ran while one was open for 1% of the time, Pallas kernels for 9%

commit v1 on v0

--- a/solution.py
+++ b/solution.py
@@ -14,6 +14,7 @@
 AXES = ("tensor", "seq")
 PIECE = 512
 PIECES = (PIECE,) * 10
+X_AT, Y_LOW, SAME, Y_AT = 10, 11, 12, 13
 VMEM_LIMIT = 58 * 1024 * 1024
 VMEM_SMALL = 16 * 1024 * 1024
 FROWS = 160
@@ -108,11 +109,12 @@
     return (lane >= head * HEAD_DIM) & (lane < (head + 1) * HEAD_DIM)
 
 
-def early_kernel(counts, *refs):
+def early_kernel(counts, idle, *refs):
     refs = list(refs)
     blocks = [refs.pop(0) for _ in counts]
     weights = [refs.pop(0) for _ in range(3)]
     taps, gain = refs.pop(0), refs.pop(0)
+    del refs[:idle]
     value_out, query_key_out, edge_out, small_out, xs, ws, acc, xsem, wsem = refs
     small_out[: taps.shape[0], :] = taps[...]
     small_out[taps.shape[0] :, :] = gain[...]
@@ -161,20 +163,20 @@
             edge_out[2 * slot + end : 2 * slot + end + 1, :] = line.astype(jnp.bfloat16).astype(jnp.float32)
 
 
-def project_early(blocks, weights, taps, gain):
+def project_early(blocks, weights, taps, gain, after):
     counts = tuple(block.shape[0] for block in blocks)
     depth, rows = blocks[0].shape[1], sum(counts)
     hbm = pl.BlockSpec(memory_space=pltpu.HBM)
     vmem = pl.BlockSpec(memory_space=pltpu.VMEM)
     return pl.pallas_call(
-        functools.partial(early_kernel, counts),
+        functools.partial(early_kernel, counts, len(after)),
         out_shape=[
             jax.ShapeDtypeStruct((rows, VCOLS), jnp.bfloat16),
             jax.ShapeDtypeStruct((rows, 2 * QCOLS), jnp.float32),
             jax.ShapeDtypeStruct((8, VCOLS), jnp.float32),
             jax.ShapeDtypeStruct((taps.shape[0] + 1, VCOLS), jnp.float32),
         ],
-        in_specs=[hbm] * (len(blocks) + 3) + [vmem] * 2,
+        in_specs=[hbm] * (len(blocks) + 3) + [vmem] * 2 + [hbm] * len(after),
         out_specs=[vmem] * 4,
         scratch_shapes=[
             pltpu.VMEM((rows, depth), jnp.bfloat16),
@@ -185,7 +187,7 @@
         ],
         compiler_params=pltpu.CompilerParams(vmem_limit_bytes=VMEM_LIMIT),
         cost_estimate=pl.CostEstimate(flops=EARLY_COST, bytes_accessed=EARLY_COST // 1000, transcendentals=0),
-    )(*blocks, *weights, taps, gain)
+    )(*blocks, *weights, taps, gain, *after)
 
 
 def project_kernel(counts, offsets, *refs):
@@ -307,7 +309,7 @@
     values, query_keys = ((refs[0], refs[1]), (refs[2],)), ((refs[3], refs[4]), (refs[5],))
     (near, far), taps = refs[6:8], refs[8:10]
     convs, queries, (keep_out, give_out), states = refs[10:12], refs[12:14], refs[14:16], refs[16]
-    x_at, even = place[0], place[1] == 0
+    x_at, even = place[X_AT], place[Y_LOW] == 0
     row = lax.broadcasted_iota(jnp.int32, (BLOCK, VCOLS), 0)
     ones = jnp.ones((8, ROWS), jnp.bfloat16)
     states[...] = jnp.zeros_like(states)
@@ -348,7 +350,7 @@
                 ones, feat, (((1,), (1,)), ((), ())), preferred_element_type=jnp.float32
             )
             state[FROWS + head : FROWS + head + 1, :FROWS] = total[0:1]
-    same = place[2] == 1
+    same = place[SAME] == 1
     keep_out[...] = jnp.where(same, states[0], states[1])
     give_out[...] = jnp.where(same, states[1], states[0]).astype(jnp.bfloat16)
 
@@ -371,12 +373,12 @@
     )(place, *values, *query_keys, near, far, *taps)
 
 
-def pack_kernel(start, query, key, value, *refs):
+def pack_kernel(members, control, query, key, value, *refs):
     outs, sems = refs[:-1], refs[-1]
     copies = []
     for index, out in enumerate(outs):
         count = out.shape[0]
-        span = pl.ds(pl.multiple_of(start[index], 256), count)
+        span = pl.ds(pl.multiple_of(control[members[index]], 512), count)
         for kind, (ref, col, width) in enumerate(
             ((query, 0, QCOLS), (key, QCOLS, QCOLS), (value, 2 * QCOLS, VCOLS))
         ):
@@ -389,21 +391,22 @@
         copy.wait()
 
 
-def pack(weights, starts, counts):
+def pack(control, weights, members):
+    counts = [PIECES[member] for member in members]
     hbm = pl.BlockSpec(memory_space=pltpu.HBM)
     return pl.pallas_call(
-        pack_kernel,
+        functools.partial(pack_kernel, members),
         out_shape=[jax.ShapeDtypeStruct((count, GCOLS), jnp.bfloat16) for count in counts],
         in_specs=[pl.BlockSpec(memory_space=pltpu.SMEM)] + [hbm] * 3,
         out_specs=[pl.BlockSpec(memory_space=pltpu.VMEM)] * len(counts),
         scratch_shapes=[pltpu.SemaphoreType.DMA((len(counts), 3))],
         compiler_params=pltpu.CompilerParams(vmem_limit_bytes=VMEM_LIMIT),
-    )(jnp.stack(starts).astype(jnp.int32), *weights)
+    )(control, *weights)
 
 
 def split_kernel(place, keep, got, part_out, *lows):
     for step in range(NY):
-        span = pl.ds(pl.multiple_of((place[0] + step) % NY * SPLIT, SPLIT), SPLIT)
+        span = pl.ds(pl.multiple_of((place[Y_AT] + step) % NY * SPLIT, SPLIT), SPLIT)
         total = keep[span, :] + got[span, :].astype(jnp.float32)
         if step == 0:
             part_out[...] = total
@@ -427,7 +430,7 @@
     blocks, out = refs[:NX], refs[NX]
     width = blocks[0].shape[1]
     for step, block in enumerate(blocks):
-        span = pl.ds(pl.multiple_of((place[0] + step) % NX * width, 128), width)
+        span = pl.ds(pl.multiple_of((place[X_AT] + step) % NX * width, 128), width)
         out[:, span] = block[...]
 
 
@@ -443,14 +446,14 @@
     )(place, *blocks)
 
 
-def attend_kernel(y_place, same, *refs):
+def attend_kernel(place, *refs):
     groups = (refs[0:3], refs[3:6])
     mine, theirs = refs[6:10], refs[10:14]
     outs, acc, states = refs[14:18], refs[18], refs[19]
     for step in range(NY):
-        span = pl.ds(pl.multiple_of((y_place[0] + step) % NY * SPLIT, SPLIT), SPLIT)
-        states[1 - same[0], span, :] = mine[step][...]
-        states[same[0], span, :] = theirs[step][...]
+        span = pl.ds(pl.multiple_of((place[Y_AT] + step) % NY * SPLIT, SPLIT), SPLIT)
+        states[1 - place[SAME], span, :] = mine[step][...]
+        states[place[SAME], span, :] = theirs[step][...]
     for number, (query, conv, gain) in enumerate(groups):
         state = states.at[number]
         acc[...] = jnp.zeros_like(acc)
@@ -466,7 +469,7 @@
             acc[:, start:stop] += lax.dot_general(
                 scaled, part, (((0,), (0,)), ((), ())), preferred_element_type=jnp.float32
             )
-        low = y_place[0] % 2
+        low = place[Y_LOW]
         spot = low if number == 0 else 1 - low
         span = pl.ds(pl.multiple_of(spot * VCOLS, VCOLS), VCOLS)
         for block, slot in enumerate(SLOTS):
@@ -475,19 +478,19 @@
             outs[slot][:, span] = mixed.astype(jnp.bfloat16)
 
 
-def attend(y_place, same, groups, mine, theirs):
+def attend(place, groups, mine, theirs):
     vmem = pl.BlockSpec(memory_space=pltpu.VMEM)
     return pl.pallas_call(
         attend_kernel,
         out_shape=[jax.ShapeDtypeStruct((BLOCK, 2 * VCOLS), jnp.bfloat16)] * 4,
-        in_specs=[pl.BlockSpec(memory_space=pltpu.SMEM)] * 2 + [vmem] * 14,
+        in_specs=[pl.BlockSpec(memory_space=pltpu.SMEM)] + [vmem] * 14,
         out_specs=[vmem] * 4,
         scratch_shapes=[
             pltpu.VMEM((ROWS, VCOLS), jnp.float32),
             pltpu.VMEM((2, MROWS, VCOLS), jnp.bfloat16),
         ],
         compiler_params=pltpu.CompilerParams(vmem_limit_bytes=VMEM_SMALL),
-    )(y_place, same, *[array for group in groups for array in group], *mine, *theirs)
+    )(place, *[array for group in groups for array in group], *mine, *theirs)
 
 
 def body(tokens, query_weight, key_weight, value_weight, conv_taps, norm_gain):
@@ -499,9 +502,14 @@
     weights = (query_weight, key_weight, value_weight)
     half = rows.shape[1] // 2
 
-    y_place = y_at.reshape(1).astype(jnp.int32)
-    x_place = x_at.reshape(1).astype(jnp.int32)
-    same = (core == y_low).astype(jnp.int32).reshape(1)
+    base = core * half
+    mixed_z = z_odd * 2 * PIECE
+    flip = 2 * PIECE - mixed_z
+    parts = (mixed_z, mixed_z + PIECE, flip, flip + PIECE, jnp.full_like(z_odd, 4 * PIECE))
+    control = jnp.stack(
+        [start + shift for start in (base, half - base) for shift in parts]
+        + [x_at, y_low, (core == y_low).astype(x_at.dtype), y_at]
+    ).astype(jnp.int32)
     part = BLOCK // 2
 
     def from_side(array):
@@ -515,28 +523,22 @@
     two_top = from_x(one[:part], 1)
     two_low = from_x(three[part:], -1)
 
-    base = core * half
-    mixed_z = z_odd * 2 * PIECE
-    packed = pack(weights, (base + mixed_z, base + mixed_z + PIECE, base + 4 * PIECE), (PIECE,) * 3)
+    packed = pack(control, weights, (0, 1, 4))
     side = [from_side(array) for array in packed]
     side_z = [receive(array, lambda x, y, z, c: (x, y, z + 2 * c - 1, c)) for array in side[:2]]
     mine = [side[0], side[1], *side_z, side[2]]
     theirs = [from_core(array) for array in mine]
-    flip = 2 * PIECE - mixed_z
-    steps = jnp.stack([mixed_z, mixed_z + PIECE, flip, flip + PIECE, jnp.full_like(z_odd, 4 * PIECE)])
-    offsets = jnp.concatenate([base + steps, (half - base) + steps]).astype(jnp.int32)
 
     blocks = (rows, one, three, two_top, two_low)
-    place = jnp.concatenate([x_place, y_low.reshape(1).astype(jnp.int32), same])
     value_early, query_key_early, edge_early, small = project_early(
-        blocks[:3], weights, conv_taps, norm_gain[None]
+        blocks[:3], weights, conv_taps, norm_gain[None], (theirs[0], theirs[1])
     )
     small_other = from_other(small)
     value_late, value_other, query_key_late, query_key_other, edge = project(
-        offsets, blocks, weights, (*mine, *theirs), edge_early, arrived(two_top, two_low, small_other)
+        control, blocks, weights, (*mine, *theirs), edge_early, arrived(two_top, two_low, small_other)
     )
     conv_own, conv_other, query_own, query_other, keep, give = states_of(
-        place,
+        control,
         (value_early, value_late, value_other),
         (query_key_early, query_key_late, query_key_other),
         from_other(edge),
@@ -544,7 +546,7 @@
         (small, small_other),
     )
 
-    total, *lows = split(y_place, keep, from_core(give))
+    total, *lows = split(control, keep, from_core(give))
     for step, low in zip((1, 2, 3), lows):
         total = total + from_y(low, -step).astype(jnp.float32)
     low = total.astype(jnp.bfloat16)
@@ -556,13 +558,12 @@
     theirs = [from_core(array) for array in mine]
 
     out = attend(
-        y_place,
-        same,
+        control,
         ((query_own, conv_own, small), (query_other, conv_other, small_other)),
         mine,
         theirs,
     )
-    result = join(x_place, [out[0], from_x(out[3], 1), from_x(out[2], 2), from_x(out[1], -1)])
+    result = join(control, [out[0], from_x(out[3], 1), from_x(out[2], 2), from_x(out[1], -1)])
     return result.reshape(tokens.shape)
 
 

time: 149 us -> 156 us (1.047)
  waiting for transfers between devices: 46.8 us -> 53.9 us
  Pallas kernels: 32.8 us -> 34.7 us
    ppermute x34, waiting for transfers between devices: 46.4 us -> 51.7 us  [receive(): return lax.ppermute(array, AXES, pairs)]
    ppermute x1, waiting for transfers between devices: 0.37 us -> 2.18 us  [from_far(): return lax.ppermute(array, AXES, pairs)]
    unnamed x34 -> x36, local copies, waits for them, and re-layouts: 6.19 us -> 5.13 us
  transfers between devices with their start and end apart: 35 -> 35, of which waited for: 19 -> 16; matrix products, arithmetic and copies ran while one was open for 1% -> 1% of each run, Pallas kernels for 9% -> 9%
where the time goes in v1:
time: 156 us
  starting transfers between devices  60.2 us (39%)
  waiting for transfers between devices  53.9 us (35%)
  Pallas kernels  34.7 us (22%)
  local copies, waits for them, and re-layouts  6.48 us (4%)
    ppermute x34, starting transfers between devices, receive(): return lax.ppermute(array, AXES, pairs)  56.9 us
    ppermute x34, waiting for transfers between devices, receive(): return lax.ppermute(array, AXES, pairs)  51.7 us
    pallas_call x1, Pallas kernels, project(): pl.pallas_call(functools.partial(project_kernel, counts), out_shape=[jax....  12.4 us
    pallas_call x1, Pallas kernels, project_early(): pl.pallas_call(functools.partial(early_kernel, counts, len(after)), out_s...  8.64 us
    unnamed x36, local copies, waits for them, and re-layouts  5.13 us
    pallas_call x1, Pallas kernels, pack(): pl.pallas_call(functools.partial(pack_kernel, members), out_shape=[jax.Sh...  4.28 us
    pallas_call x1, Pallas kernels, attend(): pl.pallas_call(attend_kernel, out_shape=[jax.ShapeDtypeStruct((BLOCK, 2 *...  3.5 us
    ppermute x1, starting transfers between devices, from_far(): return lax.ppermute(array, AXES, pairs)  3.25 us
  transfers between devices with their start and end apart: 35, of which 16 were waited for; matrix products, arithmetic and copies ran while one was open for 1% of the time, Pallas kernels for 9%

profile of v1, /device:TPU:1, one launch (start us, length us, event | category | flops | bytes accessed | tf_op | source)
XLA Modules:
  0.0 155.6 jit_solution(10572743458468975742)
XLA Ops:
  0.0 2.0 %collective-permute-start.1 = (bf16[128,5120]{1,0:T(8,128)(2,1)}, bf16[128,5120]{1,0:T(8,128)(2,1)S(1)}, u32[]{:S(2)}, u32[]{:S(2)}) collective-permute-start(bf16[128,5120]{1,0:T(8,128)(2,1)} %bitcast.16), channel_id=1, source_target_pairs={{192,0},{193,1},{194,2},{195,3},{196,4},{197,5},{198,6},{199,7},{2... | collective-permute-start | bytes 3932168 | tf_op jit(solution)/shard_map/ppermute | solution.py:55
  4.0 4.3 %shard_map.64 = (bf16[512,896]{1,0:T(8,128)(2,1)}, bf16[512,896]{1,0:T(8,128)(2,1)}, bf16[512,896]{1,0:T(8,128)(2,1)}) custom-call(s32[14]{0:T(128)} %stack.63.control.offsets.place, bf16[5120,128]{1,0:T(8,128)(2,1)} %refs_5_.3, bf16[5120,128]{1,0:T(8,128)(2,1)} %refs_6_.3, bf16[5120,640]{1,0:T(8,128)(2,1)} %refs_7_.1), custom_call_target="tpu_custom_call" | custom-call | tf_op jit(solution)/shard_map/pallas_call | solution.py:397
  8.3 3.0 %collective-permute-start.2 = (bf16[512,896]{1,0:T(8,128)(2,1)}, bf16[512,896]{1,0:T(8,128)(2,1)}, u32[]{:S(2)}, u32[]{:S(2)}) collective-permute-start(bf16[512,896]{1,0:T(8,128)(2,1)} %get-tuple-element.31), channel_id=1, source_target_pairs={{48,0},{33,1},{50,2},{35,3},{52,4},{37,5},{54,6},{39,7},{56,8},{41... | collective-permute-start | bytes 2752520 | tf_op jit(solution)/shard_map/ppermute | solution.py:55
  11.7 10.2 %collective-permute-done.2.refs_8_ = bf16[512,896]{1,0:T(8,128)(2,1)} collective-permute-done((bf16[512,896]{1,0:T(8,128)(2,1)}, bf16[512,896]{1,0:T(8,128)(2,1)}, u32[]{:S(2)}, u32[]{:S(2)}) %collective-permute-start.2) | collective-permute-done | bytes 917536 | tf_op jit(solution)/shard_map/ppermute | solution.py:55
  21.9 4.5 %collective-permute-start.3 = (bf16[512,896]{1,0:T(8,128)(2,1)}, bf16[512,896]{1,0:T(8,128)(2,1)S(1)}, u32[]{:S(2)}, u32[]{:S(2)}) collective-permute-start(bf16[512,896]{1,0:T(8,128)(2,1)} %collective-permute-done.2.refs_8_), channel_id=1, source_target_pairs={{1,0},{0,1},{3,2},{2,3},{5,4},{4,5},{7,6},{6,7},{9,8},{8,9},{11,10... | collective-permute-start | bytes 2752520 | tf_op jit(solution)/shard_map/ppermute | solution.py:55
  26.4 5.3 %collective-permute-done.4.refs_9_ = bf16[512,896]{1,0:T(8,128)(2,1)} collective-permute-done((bf16[512,896]{1,0:T(8,128)(2,1)}, bf16[512,896]{1,0:T(8,128)(2,1)}, u32[]{:S(2)}, u32[]{:S(2)}) %collective-permute-start.4) | collective-permute-done | bytes 917536 | tf_op jit(solution)/shard_map/ppermute | solution.py:55
  31.8 4.5 %collective-permute-start.5 = (bf16[512,896]{1,0:T(8,128)(2,1)}, bf16[512,896]{1,0:T(8,128)(2,1)S(1)}, u32[]{:S(2)}, u32[]{:S(2)}) collective-permute-start(bf16[512,896]{1,0:T(8,128)(2,1)} %collective-permute-done.4.refs_9_), channel_id=1, source_target_pairs={{1,0},{0,1},{3,2},{2,3},{5,4},{4,5},{7,6},{6,7},{9,8},{8,9},{11,10... | collective-permute-start | bytes 2752520 | tf_op jit(solution)/shard_map/ppermute | solution.py:55
  36.3 5.4 %collective-permute-start.8 = (bf16[512,896]{1,0:T(8,128)(2,1)}, bf16[512,896]{1,0:T(8,128)(2,1)}, u32[]{:S(2)}, u32[]{:S(2)}) collective-permute-start(bf16[512,896]{1,0:T(8,128)(2,1)} %collective-permute-done.2.refs_8_), channel_id=1, source_target_pairs={{14,0},{3,1},{0,2},{5,3},{2,4},{7,5},{4,6},{9,7},{6,8},{11,9},{8,1... | collective-permute-start | bytes 2752520 | tf_op jit(solution)/shard_map/ppermute | solution.py:55
  43.2 2.6 %collective-permute-start.6 = (bf16[64,5120]{1,0:T(8,128)(2,1)S(1)}, bf16[64,5120]{1,0:T(8,128)(2,1)}, u32[]{:S(2)}, u32[]{:S(2)}) collective-permute-start(bf16[64,5120]{1,0:T(8,128)(2,1)S(1)} %slice.8), channel_id=1, source_target_pairs={{64,0},{65,1},{66,2},{67,3},{68,4},{69,5},{70,6},{71,7},{72,8},{73... | collective-permute-start | bytes 1966088 | tf_op jit(solution)/shard_map/ppermute | solution.py:55
  45.9 8.6 %shard_map.65 = (bf16[384,640]{1,0:T(8,128)(2,1)}, f32[384,256]{1,0:T(8,128)}, f32[8,640]{1,0:T(8,128)}, f32[4,640]{1,0:T(4,128)}) custom-call(bf16[128,5120]{1,0:T(8,128)(2,1)} %bitcast.18, bf16[128,5120]{1,0:T(8,128)(2,1)} %copy-done.11, bf16[128,5120]{1,0:T(8,128)(2,1)} %copy-done.10, bf16[5120,128]{1,0:T(8,128)(2,1)} %refs_5_.3, ...), custom_call_target="tpu_custom_call" | custom-call | flops 3000000000 | bytes 3000000 | tf_op jit(solution)/shard_map/pallas_call | solution.py:171
  54.7 7.4 %collective-permute-done.9.refs_11_ = bf16[512,896]{1,0:T(8,128)(2,1)} collective-permute-done((bf16[512,896]{1,0:T(8,128)(2,1)}, bf16[512,896]{1,0:T(8,128)(2,1)}, u32[]{:S(2)}, u32[]{:S(2)}) %collective-permute-start.9) | collective-permute-done | bytes 917536 | tf_op jit(solution)/shard_map/ppermute | solution.py:55
  67.1 12.4 %shard_map.67 = (bf16[128,640]{1,0:T(8,128)(2,1)}, bf16[512,640]{1,0:T(8,128)(2,1)}, f32[128,256]{1,0:T(8,128)}, f32[512,256]{1,0:T(8,128)}, f32[16,640]{1,0:T(8,128)}) custom-call(s32[14]{0:T(128)} %stack.63.control.offsets.place, bf16[128,5120]{1,0:T(8,128)(2,1)} %bitcast.19, bf16[128,5120]{1,0:T(8,128)(2,1)} %copy-done.11, bf16[128,5120]{1,0:T(8,128)(2,1)} %copy-done.10, ...), custom_call_target="tpu_custom_call" | custom-call | flops 7046430720 | bytes 23592960 | tf_op jit(solution)/shard_map/pallas_call | solution.py:268
  79.4 3.2 %collective-permute-start.16 = (f32[16,640]{1,0:T(8,128)}, f32[16,640]{1,0:T(8,128)S(1)}, u32[]{:S(2)}, u32[]{:S(2)}) collective-permute-start(f32[16,640]{1,0:T(8,128)} %get-tuple-element.42), channel_id=1, source_target_pairs={{32,1},{33,2},{34,3},{35,4},{36,5},{37,6},{38,7},{39,8},{40,9},{41... | collective-permute-start | bytes 122888 | tf_op jit(solution)/shard_map/ppermute | solution.py:83
  82.8 2.2 %collective-permute-done.16.refs_7_ = f32[16,640]{1,0:T(8,128)S(1)} collective-permute-done((f32[16,640]{1,0:T(8,128)}, f32[16,640]{1,0:T(8,128)S(1)}, u32[]{:S(2)}, u32[]{:S(2)}) %collective-permute-start.16) | collective-permute-done | bytes 40992 | tf_op jit(solution)/shard_map/ppermute | solution.py:83
  89.8 3.0 %shard_map.68 = (bf16[512,640]{1,0:T(8,128)(2,1)S(1)}, bf16[512,640]{1,0:T(8,128)(2,1)S(1)}, f32[128,512]{1,0:T(8,128)S(1)}, f32[128,512]{1,0:T(8,128)S(1)}, f32...) custom-call(s32[14]{0:T(128)S(1)} %copy-done, bf16[384,640]{1,0:T(8,128)(2,1)S(1)} %copy-done.4, ...), custom_call_target="tpu_custom_call" | custom-call | flops 6000000000 | bytes 8000000 | tf_op jit(solution)/shard_map/pallas_call | solution.py:360
  95.0 1.8 %collective-permute-start.18 = (bf16[48,640]{1,0:T(8,128)(2,1)S(1)}, bf16[48,640]{1,0:T(8,128)(2,1)S(1)}, u32[]{:S(2)}, u32[]{:S(2)}) collective-permute-start(bf16[48,640]{1,0:T(8,128)(2,1)S(1)} %get-tuple-element.50), channel_id=1, source_target_pairs={{48,0},{49,1},{50,2},{51,3},{52,4},{53,5},{54,6},{55,7},{56,8},{57... | collective-permute-start | bytes 184328 | tf_op jit(solution)/shard_map/ppermute | solution.py:55
  96.8 2.8 %collective-permute-start.19 = (bf16[48,640]{1,0:T(8,128)(2,1)S(1)}, bf16[48,640]{1,0:T(8,128)(2,1)S(1)}, u32[]{:S(2)}, u32[]{:S(2)}) collective-permute-start(bf16[48,640]{1,0:T(8,128)(2,1)S(1)} %get-tuple-element.51), channel_id=1, source_target_pairs={{16,0},{17,1},{18,2},{19,3},{20,4},{21,5},{22,6},{23,7},{24,8},{25... | collective-permute-start | bytes 184328 | tf_op jit(solution)/shard_map/ppermute | solution.py:55
  99.6 2.0 %collective-permute-start.20 = (bf16[48,640]{1,0:T(8,128)(2,1)S(1)}, bf16[48,640]{1,0:T(8,128)(2,1)S(1)}, u32[]{:S(2)}, u32[]{:S(2)}) collective-permute-start(bf16[48,640]{1,0:T(8,128)(2,1)S(1)} %get-tuple-element.52), channel_id=1, source_target_pairs={{32,0},{33,1},{34,2},{35,3},{36,4},{37,5},{38,6},{39,7},{40,8},{41... | collective-permute-start | bytes 184328 | tf_op jit(solution)/shard_map/ppermute | solution.py:55
  103.0 2.9 %collective-permute-start.23 = (bf16[48,640]{1,0:T(8,128)(2,1)S(1)}, bf16[48,640]{1,0:T(8,128)(2,1)S(1)}, u32[]{:S(2)}, u32[]{:S(2)}) collective-permute-start(bf16[48,640]{1,0:T(8,128)(2,1)S(1)} %fusion), channel_id=1, source_target_pairs={{4,0},{5,1},{6,2},{7,3},{8,4},{9,5},{10,6},{11,7},{12,8},{13,9},{1... | collective-permute-start | bytes 184328 | tf_op jit(solution)/shard_map/ppermute | solution.py:55
  106.2 2.4 %collective-permute-start.21 = (bf16[48,640]{1,0:T(8,128)(2,1)S(1)}, bf16[48,640]{1,0:T(8,128)(2,1)S(1)}, u32[]{:S(2)}, u32[]{:S(2)}) collective-permute-start(bf16[48,640]{1,0:T(8,128)(2,1)S(1)} %fusion), channel_id=1, source_target_pairs={{2,0},{3,1},{4,2},{5,3},{6,4},{7,5},{8,6},{9,7},{10,8},{11,9},{12,... | collective-permute-start | bytes 184328 | tf_op jit(solution)/shard_map/ppermute | solution.py:55
  108.6 1.7 %collective-permute-done.22 = bf16[48,640]{1,0:T(8,128)(2,1)S(1)} collective-permute-done((bf16[48,640]{1,0:T(8,128)(2,1)S(1)}, bf16[48,640]{1,0:T(8,128)(2,1)S(1)}, u32[]{:S(2)}, u32[]{:S(2)}) %collective-permute-start.22) | collective-permute-done | bytes 61472 | tf_op jit(solution)/shard_map/ppermute | solution.py:55
  110.4 4.1 %collective-permute-start.24 = (bf16[48,640]{1,0:T(8,128)(2,1)S(1)}, bf16[48,640]{1,0:T(8,128)(2,1)S(1)}, u32[]{:S(2)}, u32[]{:S(2)}) collective-permute-start(bf16[48,640]{1,0:T(8,128)(2,1)S(1)} %get-tuple-element.57), channel_id=1, source_target_pairs={{8,0},{9,1},{10,2},{11,3},{12,4},{13,5},{14,6},{15,7},{0,8},{1,9},... | collective-permute-start | bytes 184328 | tf_op jit(solution)/shard_map/ppermute | solution.py:55
  114.5 3.0 %collective-permute-done.24 = bf16[48,640]{1,0:T(8,128)(2,1)S(1)} collective-permute-done((bf16[48,640]{1,0:T(8,128)(2,1)S(1)}, bf16[48,640]{1,0:T(8,128)(2,1)S(1)}, u32[]{:S(2)}, u32[]{:S(2)}) %collective-permute-start.24) | collective-permute-done | bytes 61472 | tf_op jit(solution)/shard_map/ppermute | solution.py:55
  117.5 2.1 %collective-permute-start.27 = (bf16[48,640]{1,0:T(8,128)(2,1)S(1)}, bf16[48,640]{1,0:T(8,128)(2,1)S(1)}, u32[]{:S(2)}, u32[]{:S(2)}) collective-permute-start(bf16[48,640]{1,0:T(8,128)(2,1)S(1)} %add_convert_fusion.refs_6_), channel_id=1, source_target_pairs={{48,0},{49,1},{50,2},{51,3},{52,4},{53,5},{54,6},{55,7},{56,8},{57... | collective-permute-start | bytes 184328 | tf_op jit(solution)/shard_map/ppermute | solution.py:55
  119.6 2.1 %collective-permute-start.26 = (bf16[48,640]{1,0:T(8,128)(2,1)S(1)}, bf16[48,640]{1,0:T(8,128)(2,1)S(1)}, u32[]{:S(2)}, u32[]{:S(2)}) collective-permute-start(bf16[48,640]{1,0:T(8,128)(2,1)S(1)} %add_convert_fusion.refs_6_), channel_id=1, source_target_pairs={{16,0},{17,1},{18,2},{19,3},{20,4},{21,5},{22,6},{23,7},{24,8},{25... | collective-permute-start | bytes 184328 | tf_op jit(solution)/shard_map/ppermute | solution.py:55
  122.1 3.9 %collective-permute-start.28 = (bf16[48,640]{1,0:T(8,128)(2,1)S(1)}, bf16[48,640]{1,0:T(8,128)(2,1)S(1)}, u32[]{:S(2)}, u32[]{:S(2)}) collective-permute-start(bf16[48,640]{1,0:T(8,128)(2,1)S(1)} %add_convert_fusion.refs_6_), channel_id=1, source_target_pairs={{1,0},{0,1},{3,2},{2,3},{5,4},{4,5},{7,6},{6,7},{9,8},{8,9},{11,10... | collective-permute-start | bytes 184328 | tf_op jit(solution)/shard_map/ppermute | solution.py:55
  127.1 1.5 collective-permute-start.30
  130.9 3.5 %shard_map.70 = (bf16[128,1280]{1,0:T(8,128)(2,1)S(1)}, bf16[128,1280]{1,0:T(8,128)(2,1)S(1)}, bf16[128,1280]{1,0:T(8,128)(2,1)S(1)}, bf16[128,1280]{1,0:T(8,128)(2,1)S(1)}) custom-call(s32[14]{0:T(128)S(1)} %copy-done, f32[128,512]{1,0:T(8,128)S(1)} %get-tuple-element.43.refs_0_, bf16[512,640]{1,0:T(8,128)(2,1)S(1)} %get-tuple-element.44.refs_1_, ...), custom_call_target="tpu_custom_call" | custom-call | tf_op jit(solution)/shard_map/pallas_call | solution.py:483
  136.8 6.6 %collective-permute-done.32.refs_1_ = bf16[128,1280]{1,0:T(8,128)(2,1)S(1)} collective-permute-done((bf16[128,1280]{1,0:T(8,128)(2,1)S(1)}, bf16[128,1280]{1,0:T(8,128)(2,1)S(1)}, u32[]{:S(2)}, u32[]{:S(2)}) %collective-permute-start.32) | collective-permute-done | bytes 327712 | tf_op jit(solution)/shard_map/ppermute | solution.py:55
  143.4 2.5 %collective-permute-done.33.refs_2_ = bf16[128,1280]{1,0:T(8,128)(2,1)S(1)} collective-permute-done((bf16[128,1280]{1,0:T(8,128)(2,1)S(1)}, bf16[128,1280]{1,0:T(8,128)(2,1)S(1)}, u32[]{:S(2)}, u32[]{:S(2)}) %collective-permute-start.33) | collective-permute-done | bytes 327712 | tf_op jit(solution)/shard_map/ppermute | solution.py:55
  145.9 8.0 %collective-permute-done.34.refs_3_ = bf16[128,1280]{1,0:T(8,128)(2,1)S(1)} collective-permute-done((bf16[128,1280]{1,0:T(8,128)(2,1)S(1)}, bf16[128,1280]{1,0:T(8,128)(2,1)S(1)}, u32[]{:S(2)}, u32[]{:S(2)}) %collective-permute-start.34) | collective-permute-done | bytes 327712 | tf_op jit(solution)/shard_map/ppermute | solution.py:55
  153.9 1.7 %shard_map.71 = bf16[128,5120]{1,0:T(8,128)(2,1)} custom-call(s32[14]{0:T(128)S(1)} %copy-done, bf16[128,1280]{1,0:T(8,128)(2,1)S(1)} %get-tuple-element.53.refs_0_, bf16[128,1280]{1,0:T(8,128)(2,1)S(1)} %collective-permute-done.32.refs_1_, bf16[128,1280]{1,0:T(8,128)(2,1)S(1)} %collective-permute-done.33.refs_2_, ...), custom_call_target="tpu_custom_call" | custom-call | tf_op jit(solution)/shard_map/pallas_call | solution.py:440
  (89 shorter events, 24.2 us)
Async XLA Ops:
  0.0 36.3 %collective-permute-start.1 = (bf16[128,5120]{1,0:T(8,128)(2,1)}, bf16[128,5120]{1,0:T(8,128)(2,1)S(1)}, u32[]{:S(2)}, u32[]{:S(2)}) collective-permute-start(bf16[128,5120]{1,0:T(8,128)(2,1)} %bitcast.16), channel_id=1, source_target_pairs={{192,0},{193,1},{194,2},{195,3},{196,4},{197,5},{198,6},{199,7},{2... | collective-permute-start | bytes 3932168 | tf_op jit(solution)/shard_map/ppermute | solution.py:55
  2.0 39.6 %collective-permute-start = (bf16[128,5120]{1,0:T(8,128)(2,1)}, bf16[128,5120]{1,0:T(8,128)(2,1)S(1)}, u32[]{:S(2)}, u32[]{:S(2)}) collective-permute-start(bf16[128,5120]{1,0:T(8,128)(2,1)} %bitcast.17), channel_id=1, source_target_pairs={{64,0},{65,1},{66,2},{67,3},{68,4},{69,5},{70,6},{71,7},{72,8},{73... | collective-permute-start | bytes 3932168 | tf_op jit(solution)/shard_map/ppermute | solution.py:55
  8.3 13.7 %collective-permute-start.2 = (bf16[512,896]{1,0:T(8,128)(2,1)}, bf16[512,896]{1,0:T(8,128)(2,1)}, u32[]{:S(2)}, u32[]{:S(2)}) collective-permute-start(bf16[512,896]{1,0:T(8,128)(2,1)} %get-tuple-element.31), channel_id=1, source_target_pairs={{48,0},{33,1},{50,2},{35,3},{52,4},{37,5},{54,6},{39,7},{56,8},{41... | collective-permute-start | bytes 2752520 | tf_op jit(solution)/shard_map/ppermute | solution.py:55
  11.3 20.5 %collective-permute-start.4 = (bf16[512,896]{1,0:T(8,128)(2,1)}, bf16[512,896]{1,0:T(8,128)(2,1)}, u32[]{:S(2)}, u32[]{:S(2)}) collective-permute-start(bf16[512,896]{1,0:T(8,128)(2,1)} %get-tuple-element.32), channel_id=1, source_target_pairs={{48,0},{33,1},{50,2},{35,3},{52,4},{37,5},{54,6},{39,7},{56,8},{41... | collective-permute-start | bytes 2752520 | tf_op jit(solution)/shard_map/ppermute | solution.py:55
  21.9 21.2 %collective-permute-start.3 = (bf16[512,896]{1,0:T(8,128)(2,1)}, bf16[512,896]{1,0:T(8,128)(2,1)S(1)}, u32[]{:S(2)}, u32[]{:S(2)}) collective-permute-start(bf16[512,896]{1,0:T(8,128)(2,1)} %collective-permute-done.2.refs_8_), channel_id=1, source_target_pairs={{1,0},{0,1},{3,2},{2,3},{5,4},{4,5},{7,6},{6,7},{9,8},{8,9},{11,10... | collective-permute-start | bytes 2752520 | tf_op jit(solution)/shard_map/ppermute | solution.py:55
  31.8 11.4 %collective-permute-start.5 = (bf16[512,896]{1,0:T(8,128)(2,1)}, bf16[512,896]{1,0:T(8,128)(2,1)S(1)}, u32[]{:S(2)}, u32[]{:S(2)}) collective-permute-start(bf16[512,896]{1,0:T(8,128)(2,1)} %collective-permute-done.4.refs_9_), channel_id=1, source_target_pairs={{1,0},{0,1},{3,2},{2,3},{5,4},{4,5},{7,6},{6,7},{9,8},{8,9},{11,10... | collective-permute-start | bytes 2752520 | tf_op jit(solution)/shard_map/ppermute | solution.py:55
  36.3 18.3 %collective-permute-start.10 = (bf16[512,896]{1,0:T(8,128)(2,1)}, bf16[512,896]{1,0:T(8,128)(2,1)}, u32[]{:S(2)}, u32[]{:S(2)}) collective-permute-start(bf16[512,896]{1,0:T(8,128)(2,1)} %get-tuple-element.34), channel_id=1, source_target_pairs={{48,0},{33,1},{50,2},{35,3},{52,4},{37,5},{54,6},{39,7},{56,8},{41... | collective-permute-start | bytes 2752520 | tf_op jit(solution)/shard_map/ppermute | solution.py:55
  36.3 18.4 %collective-permute-start.8 = (bf16[512,896]{1,0:T(8,128)(2,1)}, bf16[512,896]{1,0:T(8,128)(2,1)}, u32[]{:S(2)}, u32[]{:S(2)}) collective-permute-start(bf16[512,896]{1,0:T(8,128)(2,1)} %collective-permute-done.2.refs_8_), channel_id=1, source_target_pairs={{14,0},{3,1},{0,2},{5,3},{2,4},{7,5},{4,6},{9,7},{6,8},{11,9},{8,1... | collective-permute-start | bytes 2752520 | tf_op jit(solution)/shard_map/ppermute | solution.py:55
  41.6 20.5 %collective-permute-start.9 = (bf16[512,896]{1,0:T(8,128)(2,1)}, bf16[512,896]{1,0:T(8,128)(2,1)}, u32[]{:S(2)}, u32[]{:S(2)}) collective-permute-start(bf16[512,896]{1,0:T(8,128)(2,1)} %collective-permute-done.4.refs_9_), channel_id=1, source_target_pairs={{14,0},{3,1},{0,2},{5,3},{2,4},{7,5},{4,6},{9,7},{6,8},{11,9},{8,1... | collective-permute-start | bytes 2752520 | tf_op jit(solution)/shard_map/ppermute | solution.py:55
  43.1 19.5 %collective-permute-start.7 = (bf16[64,5120]{1,0:T(8,128)(2,1)S(1)}, bf16[64,5120]{1,0:T(8,128)(2,1)}, u32[]{:S(2)}, u32[]{:S(2)}) collective-permute-start(bf16[64,5120]{1,0:T(8,128)(2,1)S(1)} %slice.9), channel_id=1, source_target_pairs={{192,0},{193,1},{194,2},{195,3},{196,4},{197,5},{198,6},{199,7},{2... | collective-permute-start | bytes 1966088 | tf_op jit(solution)/shard_map/ppermute | solution.py:55
  43.2 19.4 %collective-permute-start.6 = (bf16[64,5120]{1,0:T(8,128)(2,1)S(1)}, bf16[64,5120]{1,0:T(8,128)(2,1)}, u32[]{:S(2)}, u32[]{:S(2)}) collective-permute-start(bf16[64,5120]{1,0:T(8,128)(2,1)S(1)} %slice.8), channel_id=1, source_target_pairs={{64,0},{65,1},{66,2},{67,3},{68,4},{69,5},{70,6},{71,7},{72,8},{73... | collective-permute-start | bytes 1966088 | tf_op jit(solution)/shard_map/ppermute | solution.py:55
  54.5 7.8 %collective-permute-start.14 = (f32[4,640]{1,0:T(4,128)}, f32[4,640]{1,0:T(4,128)S(1)}, u32[]{:S(2)}, u32[]{:S(2)}) collective-permute-start(f32[4,640]{1,0:T(4,128)} %get-tuple-element.36.refs_8_.refs_2_), channel_id=1, source_target_pairs={{32,0},{33,1},{34,2},{35,3},{36,4},{37,5},{38,6},{39,7},{40,8},{41... | collective-permute-start | bytes 30728 | tf_op jit(solution)/shard_map/ppermute | solution.py:55
  54.6 8.8 %collective-permute-start.13 = (bf16[512,896]{1,0:T(8,128)(2,1)}, bf16[512,896]{1,0:T(8,128)(2,1)S(1)}, u32[]{:S(2)}, u32[]{:S(2)}) collective-permute-start(bf16[512,896]{1,0:T(8,128)(2,1)} %collective-permute-done.10.refs_12_), channel_id=1, source_target_pairs={{1,0},{0,1},{3,2},{2,3},{5,4},{4,5},{7,6},{6,7},{9,8},{8,9},{11,10... | collective-permute-start | bytes 2752520 | tf_op jit(solution)/shard_map/ppermute | solution.py:55
  62.3 3.8 %collective-permute-start.12 = (bf16[512,896]{1,0:T(8,128)(2,1)}, bf16[512,896]{1,0:T(8,128)(2,1)S(1)}, u32[]{:S(2)}, u32[]{:S(2)}) collective-permute-start(bf16[512,896]{1,0:T(8,128)(2,1)} %collective-permute-done.9.refs_11_), channel_id=1, source_target_pairs={{1,0},{0,1},{3,2},{2,3},{5,4},{4,5},{7,6},{6,7},{9,8},{8,9},{11,10... | collective-permute-start | bytes 2752520 | tf_op jit(solution)/shard_map/ppermute | solution.py:55
  79.4 5.5 %collective-permute-start.16 = (f32[16,640]{1,0:T(8,128)}, f32[16,640]{1,0:T(8,128)S(1)}, u32[]{:S(2)}, u32[]{:S(2)}) collective-permute-start(f32[16,640]{1,0:T(8,128)} %get-tuple-element.42), channel_id=1, source_target_pairs={{32,1},{33,2},{34,3},{35,4},{36,5},{37,6},{38,7},{39,8},{40,9},{41... | collective-permute-start | bytes 122888 | tf_op jit(solution)/shard_map/ppermute | solution.py:83
  82.7 3.2 %collective-permute-start.15 = (f32[16,640]{1,0:T(8,128)}, f32[16,640]{1,0:T(8,128)S(1)}, u32[]{:S(2)}, u32[]{:S(2)}) collective-permute-start(f32[16,640]{1,0:T(8,128)} %get-tuple-element.42), channel_id=1, source_target_pairs={{32,0},{33,1},{34,2},{35,3},{36,4},{37,5},{38,6},{39,7},{40,8},{41... | collective-permute-start | bytes 122888 | tf_op jit(solution)/shard_map/ppermute | solution.py:55
  95.0 6.5 %collective-permute-start.18 = (bf16[48,640]{1,0:T(8,128)(2,1)S(1)}, bf16[48,640]{1,0:T(8,128)(2,1)S(1)}, u32[]{:S(2)}, u32[]{:S(2)}) collective-permute-start(bf16[48,640]{1,0:T(8,128)(2,1)S(1)} %get-tuple-element.50), channel_id=1, source_target_pairs={{48,0},{49,1},{50,2},{51,3},{52,4},{53,5},{54,6},{55,7},{56,8},{57... | collective-permute-start | bytes 184328 | tf_op jit(solution)/shard_map/ppermute | solution.py:55
  96.8 5.5 %collective-permute-start.19 = (bf16[48,640]{1,0:T(8,128)(2,1)S(1)}, bf16[48,640]{1,0:T(8,128)(2,1)S(1)}, u32[]{:S(2)}, u32[]{:S(2)}) collective-permute-start(bf16[48,640]{1,0:T(8,128)(2,1)S(1)} %get-tuple-element.51), channel_id=1, source_target_pairs={{16,0},{17,1},{18,2},{19,3},{20,4},{21,5},{22,6},{23,7},{24,8},{25... | collective-permute-start | bytes 184328 | tf_op jit(solution)/shard_map/ppermute | solution.py:55
  99.6 3.4 %collective-permute-start.20 = (bf16[48,640]{1,0:T(8,128)(2,1)S(1)}, bf16[48,640]{1,0:T(8,128)(2,1)S(1)}, u32[]{:S(2)}, u32[]{:S(2)}) collective-permute-start(bf16[48,640]{1,0:T(8,128)(2,1)S(1)} %get-tuple-element.52), channel_id=1, source_target_pairs={{32,0},{33,1},{34,2},{35,3},{36,4},{37,5},{38,6},{39,7},{40,8},{41... | collective-permute-start | bytes 184328 | tf_op jit(solution)/shard_map/ppermute | solution.py:55
  103.0 5.6 %collective-permute-start.23 = (bf16[48,640]{1,0:T(8,128)(2,1)S(1)}, bf16[48,640]{1,0:T(8,128)(2,1)S(1)}, u32[]{:S(2)}, u32[]{:S(2)}) collective-permute-start(bf16[48,640]{1,0:T(8,128)(2,1)S(1)} %fusion), channel_id=1, source_target_pairs={{4,0},{5,1},{6,2},{7,3},{8,4},{9,5},{10,6},{11,7},{12,8},{13,9},{1... | collective-permute-start | bytes 184328 | tf_op jit(solution)/shard_map/ppermute | solution.py:55
  105.9 4.4 %collective-permute-start.22 = (bf16[48,640]{1,0:T(8,128)(2,1)S(1)}, bf16[48,640]{1,0:T(8,128)(2,1)S(1)}, u32[]{:S(2)}, u32[]{:S(2)}) collective-permute-start(bf16[48,640]{1,0:T(8,128)(2,1)S(1)} %fusion), channel_id=1, source_target_pairs={{14,0},{15,1},{0,2},{1,3},{2,4},{3,5},{4,6},{5,7},{6,8},{7,9},{8,1... | collective-permute-start | bytes 184328 | tf_op jit(solution)/shard_map/ppermute | solution.py:55
  106.2 4.1 %collective-permute-start.21 = (bf16[48,640]{1,0:T(8,128)(2,1)S(1)}, bf16[48,640]{1,0:T(8,128)(2,1)S(1)}, u32[]{:S(2)}, u32[]{:S(2)}) collective-permute-start(bf16[48,640]{1,0:T(8,128)(2,1)S(1)} %fusion), channel_id=1, source_target_pairs={{2,0},{3,1},{4,2},{5,3},{6,4},{7,5},{8,6},{9,7},{10,8},{11,9},{12,... | collective-permute-start | bytes 184328 | tf_op jit(solution)/shard_map/ppermute | solution.py:55
  110.4 7.1 %collective-permute-start.24 = (bf16[48,640]{1,0:T(8,128)(2,1)S(1)}, bf16[48,640]{1,0:T(8,128)(2,1)S(1)}, u32[]{:S(2)}, u32[]{:S(2)}) collective-permute-start(bf16[48,640]{1,0:T(8,128)(2,1)S(1)} %get-tuple-element.57), channel_id=1, source_target_pairs={{8,0},{9,1},{10,2},{11,3},{12,4},{13,5},{14,6},{15,7},{0,8},{1,9},... | collective-permute-start | bytes 184328 | tf_op jit(solution)/shard_map/ppermute | solution.py:55
  117.5 8.5 %collective-permute-start.27 = (bf16[48,640]{1,0:T(8,128)(2,1)S(1)}, bf16[48,640]{1,0:T(8,128)(2,1)S(1)}, u32[]{:S(2)}, u32[]{:S(2)}) collective-permute-start(bf16[48,640]{1,0:T(8,128)(2,1)S(1)} %add_convert_fusion.refs_6_), channel_id=1, source_target_pairs={{48,0},{49,1},{50,2},{51,3},{52,4},{53,5},{54,6},{55,7},{56,8},{57... | collective-permute-start | bytes 184328 | tf_op jit(solution)/shard_map/ppermute | solution.py:55
  119.6 7.5 %collective-permute-start.26 = (bf16[48,640]{1,0:T(8,128)(2,1)S(1)}, bf16[48,640]{1,0:T(8,128)(2,1)S(1)}, u32[]{:S(2)}, u32[]{:S(2)}) collective-permute-start(bf16[48,640]{1,0:T(8,128)(2,1)S(1)} %add_convert_fusion.refs_6_), channel_id=1, source_target_pairs={{16,0},{17,1},{18,2},{19,3},{20,4},{21,5},{22,6},{23,7},{24,8},{25... | collective-permute-start | bytes 184328 | tf_op jit(solution)/shard_map/ppermute | solution.py:55
  121.7 6.9 %collective-permute-start.25 = (bf16[48,640]{1,0:T(8,128)(2,1)S(1)}, bf16[48,640]{1,0:T(8,128)(2,1)S(1)}, u32[]{:S(2)}, u32[]{:S(2)}) collective-permute-start(bf16[48,640]{1,0:T(8,128)(2,1)S(1)} %add_convert_fusion.refs_6_), channel_id=1, source_target_pairs={{32,0},{33,1},{34,2},{35,3},{36,4},{37,5},{38,6},{39,7},{40,8},{41... | collective-permute-start | bytes 184328 | tf_op jit(solution)/shard_map/ppermute | solution.py:55
  122.1 7.9 %collective-permute-start.28 = (bf16[48,640]{1,0:T(8,128)(2,1)S(1)}, bf16[48,640]{1,0:T(8,128)(2,1)S(1)}, u32[]{:S(2)}, u32[]{:S(2)}) collective-permute-start(bf16[48,640]{1,0:T(8,128)(2,1)S(1)} %add_convert_fusion.refs_6_), channel_id=1, source_target_pairs={{1,0},{0,1},{3,2},{2,3},{5,4},{4,5},{7,6},{6,7},{9,8},{8,9},{11,10... | collective-permute-start | bytes 184328 | tf_op jit(solution)/shard_map/ppermute | solution.py:55
  126.0 4.0 %collective-permute-start.31 = (bf16[48,640]{1,0:T(8,128)(2,1)S(1)}, bf16[48,640]{1,0:T(8,128)(2,1)S(1)}, u32[]{:S(2)}, u32[]{:S(2)}) collective-permute-start(bf16[48,640]{1,0:T(8,128)(2,1)S(1)} %collective-permute-done.27.refs_9_), channel_id=1, source_target_pairs={{1,0},{0,1},{3,2},{2,3},{5,4},{4,5},{7,6},{6,7},{9,8},{8,9},{11,10... | collective-permute-start | bytes 184328 | tf_op jit(solution)/shard_map/ppermute | solution.py:55
  127.1 2.9 %collective-permute-start.30 = (bf16[48,640]{1,0:T(8,128)(2,1)S(1)}, bf16[48,640]{1,0:T(8,128)(2,1)S(1)}, u32[]{:S(2)}, u32[]{:S(2)}) collective-permute-start(bf16[48,640]{1,0:T(8,128)(2,1)S(1)} %collective-permute-done.26.refs_8_), channel_id=1, source_target_pairs={{1,0},{0,1},{3,2},{2,3},{5,4},{4,5},{7,6},{6,7},{9,8},{8,9},{11,10... | collective-permute-start | bytes 184328 | tf_op jit(solution)/shard_map/ppermute | solution.py:55
  134.4 9.0 %collective-permute-start.32 = (bf16[128,1280]{1,0:T(8,128)(2,1)S(1)}, bf16[128,1280]{1,0:T(8,128)(2,1)S(1)}, u32[]{:S(2)}, u32[]{:S(2)}) collective-permute-start(bf16[128,1280]{1,0:T(8,128)(2,1)S(1)} %get-tuple-element.54), channel_id=1, source_target_pairs={{64,0},{65,1},{66,2},{67,3},{68,4},{69,5},{70,6},{71,7},{72,8},{73... | collective-permute-start | bytes 983048 | tf_op jit(solution)/shard_map/ppermute | solution.py:55
  135.7 10.2 %collective-permute-start.33 = (bf16[128,1280]{1,0:T(8,128)(2,1)S(1)}, bf16[128,1280]{1,0:T(8,128)(2,1)S(1)}, u32[]{:S(2)}, u32[]{:S(2)}) collective-permute-start(bf16[128,1280]{1,0:T(8,128)(2,1)S(1)} %get-tuple-element.55), channel_id=1, source_target_pairs={{128,0},{129,1},{130,2},{131,3},{132,4},{133,5},{134,6},{135,7},{1... | collective-permute-start | bytes 983048 | tf_op jit(solution)/shard_map/ppermute | solution.py:55
  136.2 17.6 %collective-permute-start.34 = (bf16[128,1280]{1,0:T(8,128)(2,1)S(1)}, bf16[128,1280]{1,0:T(8,128)(2,1)S(1)}, u32[]{:S(2)}, u32[]{:S(2)}) collective-permute-start(bf16[128,1280]{1,0:T(8,128)(2,1)S(1)} %get-tuple-element.56), channel_id=1, source_target_pairs={{192,0},{193,1},{194,2},{195,3},{196,4},{197,5},{198,6},{199,7},{2... | collective-permute-start | bytes 983048 | tf_op jit(solution)/shard_map/ppermute | solution.py:55
  (21 other events, 162.1 us)

commit v2 on v1

--- a/solution.py
+++ b/solution.py
@@ -16,6 +16,7 @@
 PIECES = (PIECE,) * 10
 X_AT, Y_LOW, SAME, Y_AT = 10, 11, 12, 13
 VMEM_LIMIT = 58 * 1024 * 1024
+VMEM_LATE = 44 * 1024 * 1024
 VMEM_SMALL = 16 * 1024 * 1024
 FROWS = 160
 MROWS = 192
@@ -281,7 +282,7 @@
             pltpu.SemaphoreType.DMA((len(PARTS), 3)),
             pltpu.SemaphoreType.DMA((len(pieces),)),
         ],
-        compiler_params=pltpu.CompilerParams(vmem_limit_bytes=VMEM_LIMIT),
+        compiler_params=pltpu.CompilerParams(vmem_limit_bytes=VMEM_LATE),
         cost_estimate=pl.CostEstimate(
             flops=3 * ROWS * depth * GCOLS, bytes_accessed=2 * depth * (ROWS + 2 * GCOLS), transcendentals=0
         ),
@@ -531,7 +532,7 @@
 
     blocks = (rows, one, three, two_top, two_low)
     value_early, query_key_early, edge_early, small = project_early(
-        blocks[:3], weights, conv_taps, norm_gain[None], (theirs[0], theirs[1])
+        blocks[:3], weights, conv_taps, norm_gain[None], ()
     )
     small_other = from_other(small)
     value_late, value_other, query_key_late, query_key_other, edge = project(

time: 156 us -> 150 us (0.962)
  waiting for transfers between devices: 53.9 us -> 49 us
  Pallas kernels: 34.7 us -> 32.9 us
    ppermute x34, waiting for transfers between devices: 51.7 us -> 48.6 us  [receive(): return lax.ppermute(array, AXES, pairs)]
    unnamed x36 -> x24, local copies, waits for them, and re-layouts: 5.13 us -> 2.85 us
    slice x1, local copies, waits for them, and re-layouts: 0.04 us -> 1.97 us  [body(): two_top = from_x(one[:part], 1)]
    ppermute x1, waiting for transfers between devices: 2.18 us -> 0.38 us  [from_far(): return lax.ppermute(array, AXES, pairs)]
    pallas_call x1, Pallas kernels: 12.4 us -> 10.8 us  [project(): pl.pallas_call(functools.partial(project_kernel, counts), out_shape=[jax....]
  transfers between devices with their start and end apart: 35 -> 35, of which waited for: 16 -> 20; matrix products, arithmetic and copies ran while one was open for 1% -> 3% of each run, Pallas kernels for 9% -> 9%
where the time goes in v2:
time: 150 us; the launch traced here: 149 us
  starting transfers between devices  60.1 us (40%)
  waiting for transfers between devices  49 us (33%)
  Pallas kernels  32.9 us (22%)
  local copies, waits for them, and re-layouts  6.9 us (5%)
    ppermute x34, starting transfers between devices, receive(): return lax.ppermute(array, AXES, pairs)  57.5 us
    ppermute x34, waiting for transfers between devices, receive(): return lax.ppermute(array, AXES, pairs)  48.6 us
    pallas_call x1, Pallas kernels, project(): pl.pallas_call(functools.partial(project_kernel, counts), out_shape=[jax....  10.8 us
    pallas_call x1, Pallas kernels, project_early(): pl.pallas_call(functools.partial(early_kernel, counts, len(after)), out_s...  8.63 us
    pallas_call x1, Pallas kernels, pack(): pl.pallas_call(functools.partial(pack_kernel, members), out_shape=[jax.Sh...  4.07 us
    pallas_call x1, Pallas kernels, attend(): pl.pallas_call(attend_kernel, out_shape=[jax.ShapeDtypeStruct((BLOCK, 2 *...  3.52 us
    pallas_call x1, Pallas kernels, states_of(): pl.pallas_call(state_kernel, out_shape=[jax.ShapeDtypeStruct((ROWS, VCOLS...  3.04 us
  transfers between devices with their start and end apart: 35, of which 20 were waited for; matrix products, arithmetic and copies ran while one was open for 3% of the time, Pallas kernels for 9%

profile of v2, /device:TPU:1, one launch (start us, length us, event | category | flops | bytes accessed | tf_op | source)
XLA Modules:
  0.0 149.2 jit_solution(15121864400276894838)
XLA Ops:
  0.0 2.0 %collective-permute-start.1 = (bf16[128,5120]{1,0:T(8,128)(2,1)}, bf16[128,5120]{1,0:T(8,128)(2,1)S(1)}, u32[]{:S(2)}, u32[]{:S(2)}) collective-permute-start(bf16[128,5120]{1,0:T(8,128)(2,1)} %bitcast.16), channel_id=1, source_target_pairs={{192,0},{193,1},{194,2},{195,3},{196,4},{197,5},{198,6},{199,7},{2... | collective-permute-start | bytes 3932168 | tf_op jit(solution)/shard_map/ppermute | solution.py:56
  3.9 4.1 %shard_map.65 = (bf16[512,896]{1,0:T(8,128)(2,1)}, bf16[512,896]{1,0:T(8,128)(2,1)}, bf16[512,896]{1,0:T(8,128)(2,1)}) custom-call(s32[14]{0:T(128)} %stack.63.control.offsets.place, bf16[5120,128]{1,0:T(8,128)(2,1)} %refs_5_.3, bf16[5120,128]{1,0:T(8,128)(2,1)} %refs_6_.3, bf16[5120,640]{1,0:T(8,128)(2,1)} %refs_7_.1), custom_call_target="tpu_custom_call" | custom-call | tf_op jit(solution)/shard_map/pallas_call | solution.py:398
  8.0 3.0 %collective-permute-start.4 = (bf16[512,896]{1,0:T(8,128)(2,1)}, bf16[512,896]{1,0:T(8,128)(2,1)S(1)}, u32[]{:S(2)}, u32[]{:S(2)}) collective-permute-start(bf16[512,896]{1,0:T(8,128)(2,1)} %get-tuple-element.32), channel_id=1, source_target_pairs={{48,0},{33,1},{50,2},{35,3},{52,4},{37,5},{54,6},{39,7},{56,8},{41... | collective-permute-start | bytes 2752520 | tf_op jit(solution)/shard_map/ppermute | solution.py:56
  11.6 10.0 %collective-permute-done.4.refs_8_ = bf16[512,896]{1,0:T(8,128)(2,1)S(1)} collective-permute-done((bf16[512,896]{1,0:T(8,128)(2,1)}, bf16[512,896]{1,0:T(8,128)(2,1)S(1)}, u32[]{:S(2)}, u32[]{:S(2)}) %collective-permute-start.4) | collective-permute-done | bytes 917536 | tf_op jit(solution)/shard_map/ppermute | solution.py:56
  21.7 5.6 %collective-permute-start.6 = (bf16[512,896]{1,0:T(8,128)(2,1)S(1)}, bf16[512,896]{1,0:T(8,128)(2,1)S(1)}, u32[]{:S(2)}, u32[]{:S(2)}) collective-permute-start(bf16[512,896]{1,0:T(8,128)(2,1)S(1)} %collective-permute-done.4.refs_8_), channel_id=1, source_target_pairs={{14,0},{3,1},{0,2},{5,3},{2,4},{7,5},{4,6},{9,7},{6,8},{11,9},{8,1... | collective-permute-start | bytes 2752520 | tf_op jit(solution)/shard_map/ppermute | solution.py:56
  27.2 4.3 %collective-permute-done.5.refs_9_ = bf16[512,896]{1,0:T(8,128)(2,1)S(1)} collective-permute-done((bf16[512,896]{1,0:T(8,128)(2,1)}, bf16[512,896]{1,0:T(8,128)(2,1)S(1)}, u32[]{:S(2)}, u32[]{:S(2)}) %collective-permute-start.5) | collective-permute-done | bytes 917536 | tf_op jit(solution)/shard_map/ppermute | solution.py:56
  31.5 5.6 %collective-permute-start.7 = (bf16[512,896]{1,0:T(8,128)(2,1)S(1)}, bf16[512,896]{1,0:T(8,128)(2,1)S(1)}, u32[]{:S(2)}, u32[]{:S(2)}) collective-permute-start(bf16[512,896]{1,0:T(8,128)(2,1)S(1)} %collective-permute-done.5.refs_9_), channel_id=1, source_target_pairs={{14,0},{3,1},{0,2},{5,3},{2,4},{7,5},{4,6},{9,7},{6,8},{11,9},{8,1... | collective-permute-start | bytes 2752520 | tf_op jit(solution)/shard_map/ppermute | solution.py:56
  39.0 2.0 %slice.8 = bf16[64,5120]{1,0:T(8,128)(2,1)} slice(bf16[128,5120]{1,0:T(8,128)(2,1)} %collective-permute-done.refs_1_), slice={[0:64], [0:5120]} | slice | bytes 1310720 | tf_op jit(solution)/shard_map/slice | solution.py:524
  41.0 2.7 %collective-permute-start.2 = (bf16[64,5120]{1,0:T(8,128)(2,1)}, bf16[64,5120]{1,0:T(8,128)(2,1)}, u32[]{:S(2)}, u32[]{:S(2)}) collective-permute-start(bf16[64,5120]{1,0:T(8,128)(2,1)} %slice.8), channel_id=1, source_target_pairs={{64,0},{65,1},{66,2},{67,3},{68,4},{69,5},{70,6},{71,7},{72,8},{73... | collective-permute-start | bytes 1966088 | tf_op jit(solution)/shard_map/ppermute | solution.py:56
  44.2 8.6 %shard_map.64 = (bf16[384,640]{1,0:T(8,128)(2,1)}, f32[384,256]{1,0:T(8,128)}, f32[8,640]{1,0:T(8,128)}, f32[4,640]{1,0:T(4,128)}) custom-call(bf16[128,5120]{1,0:T(8,128)(2,1)} %bitcast.18, bf16[128,5120]{1,0:T(8,128)(2,1)} %collective-permute-done.refs_1_, bf16[128,5120]{1,0:T(8,128)(2,1)} %copy-done.10, bf16[5120,128]{1,0:T(8,128)(2,1)} %refs_5_.3, ...), custom_call_target="tpu_custom_call" | custom-call | flops 3000000000 | bytes 3000000 | tf_op jit(solution)/shard_map/pallas_call | solution.py:172
  53.8 2.5 %collective-permute-done.14.early.refs_9_.refs_5_ = f32[4,640]{1,0:T(4,128)S(1)} collective-permute-done((f32[4,640]{1,0:T(4,128)}, f32[4,640]{1,0:T(4,128)S(1)}, u32[]{:S(2)}, u32[]{:S(2)}) %collective-permute-start.14) | collective-permute-done | bytes 10272 | tf_op jit(solution)/shard_map/ppermute | solution.py:56
  65.9 10.8 %shard_map.67 = (bf16[128,640]{1,0:T(8,128)(2,1)S(1)}, bf16[512,640]{1,0:T(8,128)(2,1)S(1)}, f32[128,256]{1,0:T(8,128)S(1)}, f32[512,256]{1,0:T(8,128)S(1)}, f32[16,640]{1,0:T(8,128)S(1)}) custom-call(s32[14]{0:T(128)S(1)} %copy-done, bf16[128,5120]{1,0:T(8,128)(2,1)} %bitcast.19, bf16[128,5120]{1,0:T(8,128)(2,1)} %collective-permute-done.refs_1_, ...), custom_call_target="tpu_custom_call" | custom-call | flops 7046430720 | bytes 23592960 | tf_op jit(solution)/shard_map/pallas_call | solution.py:269
  76.6 2.6 %collective-permute-start.16 = (f32[16,640]{1,0:T(8,128)S(1)}, f32[16,640]{1,0:T(8,128)S(1)}, u32[]{:S(2)}, u32[]{:S(2)}) collective-permute-start(f32[16,640]{1,0:T(8,128)S(1)} %get-tuple-element.42), channel_id=1, source_target_pairs={{32,1},{33,2},{34,3},{35,4},{36,5},{37,6},{38,7},{39,8},{40,9},{41... | collective-permute-start | bytes 122888 | tf_op jit(solution)/shard_map/ppermute | solution.py:84
  79.2 2.3 %collective-permute-start.15 = (f32[16,640]{1,0:T(8,128)S(1)}, f32[16,640]{1,0:T(8,128)S(1)}, u32[]{:S(2)}, u32[]{:S(2)}) collective-permute-start(f32[16,640]{1,0:T(8,128)S(1)} %get-tuple-element.42), channel_id=1, source_target_pairs={{32,0},{33,1},{34,2},{35,3},{36,4},{37,5},{38,6},{39,7},{40,8},{41... | collective-permute-start | bytes 122888 | tf_op jit(solution)/shard_map/ppermute | solution.py:56
  83.0 3.0 %shard_map.68 = (bf16[512,640]{1,0:T(8,128)(2,1)S(1)}, bf16[512,640]{1,0:T(8,128)(2,1)S(1)}, f32[128,512]{1,0:T(8,128)S(1)}, f32[128,512]{1,0:T(8,128)S(1)}, f32...) custom-call(s32[14]{0:T(128)S(1)} %copy-done, bf16[384,640]{1,0:T(8,128)(2,1)S(1)} %copy-done.6, ...), custom_call_target="tpu_custom_call" | custom-call | flops 6000000000 | bytes 8000000 | tf_op jit(solution)/shard_map/pallas_call | solution.py:361
  86.2 1.4 collective-permute-done.17.got
  88.2 1.5 %collective-permute-start.18 = (bf16[48,640]{1,0:T(8,128)(2,1)S(1)}, bf16[48,640]{1,0:T(8,128)(2,1)S(1)}, u32[]{:S(2)}, u32[]{:S(2)}) collective-permute-start(bf16[48,640]{1,0:T(8,128)(2,1)S(1)} %get-tuple-element.50), channel_id=1, source_target_pairs={{48,0},{49,1},{50,2},{51,3},{52,4},{53,5},{54,6},{55,7},{56,8},{57... | collective-permute-start | bytes 184328 | tf_op jit(solution)/shard_map/ppermute | solution.py:56
  89.8 3.9 %collective-permute-start.19 = (bf16[48,640]{1,0:T(8,128)(2,1)S(1)}, bf16[48,640]{1,0:T(8,128)(2,1)S(1)}, u32[]{:S(2)}, u32[]{:S(2)}) collective-permute-start(bf16[48,640]{1,0:T(8,128)(2,1)S(1)} %get-tuple-element.51), channel_id=1, source_target_pairs={{16,0},{17,1},{18,2},{19,3},{20,4},{21,5},{22,6},{23,7},{24,8},{25... | collective-permute-start | bytes 184328 | tf_op jit(solution)/shard_map/ppermute | solution.py:56
  93.7 2.0 %collective-permute-start.20 = (bf16[48,640]{1,0:T(8,128)(2,1)S(1)}, bf16[48,640]{1,0:T(8,128)(2,1)S(1)}, u32[]{:S(2)}, u32[]{:S(2)}) collective-permute-start(bf16[48,640]{1,0:T(8,128)(2,1)S(1)} %get-tuple-element.52), channel_id=1, source_target_pairs={{32,0},{33,1},{34,2},{35,3},{36,4},{37,5},{38,6},{39,7},{40,8},{41... | collective-permute-start | bytes 184328 | tf_op jit(solution)/shard_map/ppermute | solution.py:56
  97.1 3.5 %collective-permute-start.23 = (bf16[48,640]{1,0:T(8,128)(2,1)S(1)}, bf16[48,640]{1,0:T(8,128)(2,1)S(1)}, u32[]{:S(2)}, u32[]{:S(2)}) collective-permute-start(bf16[48,640]{1,0:T(8,128)(2,1)S(1)} %fusion), channel_id=1, source_target_pairs={{4,0},{5,1},{6,2},{7,3},{8,4},{9,5},{10,6},{11,7},{12,8},{13,9},{1... | collective-permute-start | bytes 184328 | tf_op jit(solution)/shard_map/ppermute | solution.py:56
  100.9 2.4 %collective-permute-start.21 = (bf16[48,640]{1,0:T(8,128)(2,1)S(1)}, bf16[48,640]{1,0:T(8,128)(2,1)S(1)}, u32[]{:S(2)}, u32[]{:S(2)}) collective-permute-start(bf16[48,640]{1,0:T(8,128)(2,1)S(1)} %fusion), channel_id=1, source_target_pairs={{2,0},{3,1},{4,2},{5,3},{6,4},{7,5},{8,6},{9,7},{10,8},{11,9},{12,... | collective-permute-start | bytes 184328 | tf_op jit(solution)/shard_map/ppermute | solution.py:56
  103.3 1.6 %collective-permute-done.22 = bf16[48,640]{1,0:T(8,128)(2,1)S(1)} collective-permute-done((bf16[48,640]{1,0:T(8,128)(2,1)S(1)}, bf16[48,640]{1,0:T(8,128)(2,1)S(1)}, u32[]{:S(2)}, u32[]{:S(2)}) %collective-permute-start.22) | collective-permute-done | bytes 61472 | tf_op jit(solution)/shard_map/ppermute | solution.py:56
  105.1 4.4 %collective-permute-start.24 = (bf16[48,640]{1,0:T(8,128)(2,1)S(1)}, bf16[48,640]{1,0:T(8,128)(2,1)S(1)}, u32[]{:S(2)}, u32[]{:S(2)}) collective-permute-start(bf16[48,640]{1,0:T(8,128)(2,1)S(1)} %get-tuple-element.57), channel_id=1, source_target_pairs={{8,0},{9,1},{10,2},{11,3},{12,4},{13,5},{14,6},{15,7},{0,8},{1,9},... | collective-permute-start | bytes 184328 | tf_op jit(solution)/shard_map/ppermute | solution.py:56
  109.5 2.7 %collective-permute-done.24 = bf16[48,640]{1,0:T(8,128)(2,1)S(1)} collective-permute-done((bf16[48,640]{1,0:T(8,128)(2,1)S(1)}, bf16[48,640]{1,0:T(8,128)(2,1)S(1)}, u32[]{:S(2)}, u32[]{:S(2)}) %collective-permute-start.24) | collective-permute-done | bytes 61472 | tf_op jit(solution)/shard_map/ppermute | solution.py:56
  113.2 3.1 %collective-permute-start.26 = (bf16[48,640]{1,0:T(8,128)(2,1)S(1)}, bf16[48,640]{1,0:T(8,128)(2,1)S(1)}, u32[]{:S(2)}, u32[]{:S(2)}) collective-permute-start(bf16[48,640]{1,0:T(8,128)(2,1)S(1)} %add_convert_fusion.refs_6_), channel_id=1, source_target_pairs={{16,0},{17,1},{18,2},{19,3},{20,4},{21,5},{22,6},{23,7},{24,8},{25... | collective-permute-start | bytes 184328 | tf_op jit(solution)/shard_map/ppermute | solution.py:56
  116.3 4.6 %collective-permute-start.28 = (bf16[48,640]{1,0:T(8,128)(2,1)S(1)}, bf16[48,640]{1,0:T(8,128)(2,1)S(1)}, u32[]{:S(2)}, u32[]{:S(2)}) collective-permute-start(bf16[48,640]{1,0:T(8,128)(2,1)S(1)} %add_convert_fusion.refs_6_), channel_id=1, source_target_pairs={{1,0},{0,1},{3,2},{2,3},{5,4},{4,5},{7,6},{6,7},{9,8},{8,9},{11,10... | collective-permute-start | bytes 184328 | tf_op jit(solution)/shard_map/ppermute | solution.py:56
  121.8 1.6 %collective-permute-start.30 = (bf16[48,640]{1,0:T(8,128)(2,1)S(1)}, bf16[48,640]{1,0:T(8,128)(2,1)S(1)}, u32[]{:S(2)}, u32[]{:S(2)}) collective-permute-start(bf16[48,640]{1,0:T(8,128)(2,1)S(1)} %collective-permute-done.26.refs_8_), channel_id=1, source_target_pairs={{1,0},{0,1},{3,2},{2,3},{5,4},{4,5},{7,6},{6,7},{9,8},{8,9},{11,10... | collective-permute-start | bytes 184328 | tf_op jit(solution)/shard_map/ppermute | solution.py:56
  125.6 3.5 %shard_map.70 = (bf16[128,1280]{1,0:T(8,128)(2,1)S(1)}, bf16[128,1280]{1,0:T(8,128)(2,1)S(1)}, bf16[128,1280]{1,0:T(8,128)(2,1)S(1)}, bf16[128,1280]{1,0:T(8,128)(2,1)S(1)}) custom-call(s32[14]{0:T(128)S(1)} %copy-done, f32[128,512]{1,0:T(8,128)S(1)} %get-tuple-element.43.refs_0_, bf16[512,640]{1,0:T(8,128)(2,1)S(1)} %get-tuple-element.44.refs_1_, ...), custom_call_target="tpu_custom_call" | custom-call | tf_op jit(solution)/shard_map/pallas_call | solution.py:484
  130.7 7.5 %collective-permute-done.32.refs_1_ = bf16[128,1280]{1,0:T(8,128)(2,1)S(1)} collective-permute-done((bf16[128,1280]{1,0:T(8,128)(2,1)S(1)}, bf16[128,1280]{1,0:T(8,128)(2,1)S(1)}, u32[]{:S(2)}, u32[]{:S(2)}) %collective-permute-start.32) | collective-permute-done | bytes 327712 | tf_op jit(solution)/shard_map/ppermute | solution.py:56
  138.2 1.4 collective-permute-done.33.refs_2_
  139.6 7.9 %collective-permute-done.34.refs_3_ = bf16[128,1280]{1,0:T(8,128)(2,1)S(1)} collective-permute-done((bf16[128,1280]{1,0:T(8,128)(2,1)S(1)}, bf16[128,1280]{1,0:T(8,128)(2,1)S(1)}, u32[]{:S(2)}, u32[]{:S(2)}) %collective-permute-start.34) | collective-permute-done | bytes 327712 | tf_op jit(solution)/shard_map/ppermute | solution.py:56
  147.5 1.7 %shard_map.71 = bf16[128,5120]{1,0:T(8,128)(2,1)} custom-call(s32[14]{0:T(128)S(1)} %copy-done, bf16[128,1280]{1,0:T(8,128)(2,1)S(1)} %get-tuple-element.53.refs_0_, bf16[128,1280]{1,0:T(8,128)(2,1)S(1)} %collective-permute-done.32.refs_1_, bf16[128,1280]{1,0:T(8,128)(2,1)S(1)} %collective-permute-done.33.refs_2_, ...), custom_call_target="tpu_custom_call" | custom-call | tf_op jit(solution)/shard_map/pallas_call | solution.py:441
  (77 shorter events, 25.4 us)
Async XLA Ops:
  0.0 37.1 %collective-permute-start.1 = (bf16[128,5120]{1,0:T(8,128)(2,1)}, bf16[128,5120]{1,0:T(8,128)(2,1)S(1)}, u32[]{:S(2)}, u32[]{:S(2)}) collective-permute-start(bf16[128,5120]{1,0:T(8,128)(2,1)} %bitcast.16), channel_id=1, source_target_pairs={{192,0},{193,1},{194,2},{195,3},{196,4},{197,5},{198,6},{199,7},{2... | collective-permute-start | bytes 3932168 | tf_op jit(solution)/shard_map/ppermute | solution.py:56
  2.0 37.0 %collective-permute-start = (bf16[128,5120]{1,0:T(8,128)(2,1)}, bf16[128,5120]{1,0:T(8,128)(2,1)}, u32[]{:S(2)}, u32[]{:S(2)}) collective-permute-start(bf16[128,5120]{1,0:T(8,128)(2,1)} %bitcast.17), channel_id=1, source_target_pairs={{64,0},{65,1},{66,2},{67,3},{68,4},{69,5},{70,6},{71,7},{72,8},{73... | collective-permute-start | bytes 3932168 | tf_op jit(solution)/shard_map/ppermute | solution.py:56
  8.0 13.7 %collective-permute-start.4 = (bf16[512,896]{1,0:T(8,128)(2,1)}, bf16[512,896]{1,0:T(8,128)(2,1)S(1)}, u32[]{:S(2)}, u32[]{:S(2)}) collective-permute-start(bf16[512,896]{1,0:T(8,128)(2,1)} %get-tuple-element.32), channel_id=1, source_target_pairs={{48,0},{33,1},{50,2},{35,3},{52,4},{37,5},{54,6},{39,7},{56,8},{41... | collective-permute-start | bytes 2752520 | tf_op jit(solution)/shard_map/ppermute | solution.py:56
  11.0 20.5 %collective-permute-start.5 = (bf16[512,896]{1,0:T(8,128)(2,1)}, bf16[512,896]{1,0:T(8,128)(2,1)S(1)}, u32[]{:S(2)}, u32[]{:S(2)}) collective-permute-start(bf16[512,896]{1,0:T(8,128)(2,1)} %get-tuple-element.33), channel_id=1, source_target_pairs={{48,0},{33,1},{50,2},{35,3},{52,4},{37,5},{54,6},{39,7},{56,8},{41... | collective-permute-start | bytes 2752520 | tf_op jit(solution)/shard_map/ppermute | solution.py:56
  11.5 41.4 %collective-permute-start.8 = (bf16[512,896]{1,0:T(8,128)(2,1)}, bf16[512,896]{1,0:T(8,128)(2,1)S(1)}, u32[]{:S(2)}, u32[]{:S(2)}) collective-permute-start(bf16[512,896]{1,0:T(8,128)(2,1)} %get-tuple-element.34), channel_id=1, source_target_pairs={{48,0},{33,1},{50,2},{35,3},{52,4},{37,5},{54,6},{39,7},{56,8},{41... | collective-permute-start | bytes 2752520 | tf_op jit(solution)/shard_map/ppermute | solution.py:56
  21.7 34.9 %collective-permute-start.6 = (bf16[512,896]{1,0:T(8,128)(2,1)S(1)}, bf16[512,896]{1,0:T(8,128)(2,1)S(1)}, u32[]{:S(2)}, u32[]{:S(2)}) collective-permute-start(bf16[512,896]{1,0:T(8,128)(2,1)S(1)} %collective-permute-done.4.refs_8_), channel_id=1, source_target_pairs={{14,0},{3,1},{0,2},{5,3},{2,4},{7,5},{4,6},{9,7},{6,8},{11,9},{8,1... | collective-permute-start | bytes 2752520 | tf_op jit(solution)/shard_map/ppermute | solution.py:56
  31.5 25.3 %collective-permute-start.7 = (bf16[512,896]{1,0:T(8,128)(2,1)S(1)}, bf16[512,896]{1,0:T(8,128)(2,1)S(1)}, u32[]{:S(2)}, u32[]{:S(2)}) collective-permute-start(bf16[512,896]{1,0:T(8,128)(2,1)S(1)} %collective-permute-done.5.refs_9_), channel_id=1, source_target_pairs={{14,0},{3,1},{0,2},{5,3},{2,4},{7,5},{4,6},{9,7},{6,8},{11,9},{8,1... | collective-permute-start | bytes 2752520 | tf_op jit(solution)/shard_map/ppermute | solution.py:56
  39.0 18.1 %collective-permute-start.3 = (bf16[64,5120]{1,0:T(8,128)(2,1)}, bf16[64,5120]{1,0:T(8,128)(2,1)S(1)}, u32[]{:S(2)}, u32[]{:S(2)}) collective-permute-start(bf16[64,5120]{1,0:T(8,128)(2,1)} %slice.9), channel_id=1, source_target_pairs={{192,0},{193,1},{194,2},{195,3},{196,4},{197,5},{198,6},{199,7},{2... | collective-permute-start | bytes 1966088 | tf_op jit(solution)/shard_map/ppermute | solution.py:56
  41.0 17.3 %collective-permute-start.2 = (bf16[64,5120]{1,0:T(8,128)(2,1)}, bf16[64,5120]{1,0:T(8,128)(2,1)}, u32[]{:S(2)}, u32[]{:S(2)}) collective-permute-start(bf16[64,5120]{1,0:T(8,128)(2,1)} %slice.8), channel_id=1, source_target_pairs={{64,0},{65,1},{66,2},{67,3},{68,4},{69,5},{70,6},{71,7},{72,8},{73... | collective-permute-start | bytes 1966088 | tf_op jit(solution)/shard_map/ppermute | solution.py:56
  52.9 3.3 %collective-permute-start.14 = (f32[4,640]{1,0:T(4,128)}, f32[4,640]{1,0:T(4,128)S(1)}, u32[]{:S(2)}, u32[]{:S(2)}) collective-permute-start(f32[4,640]{1,0:T(4,128)} %get-tuple-element.36.refs_8_.refs_2_), channel_id=1, source_target_pairs={{32,0},{33,1},{34,2},{35,3},{36,4},{37,5},{38,6},{39,7},{40,8},{41... | collective-permute-start | bytes 30728 | tf_op jit(solution)/shard_map/ppermute | solution.py:56
  56.5 3.6 %collective-permute-start.10 = (bf16[512,896]{1,0:T(8,128)(2,1)S(1)}, bf16[512,896]{1,0:T(8,128)(2,1)}, u32[]{:S(2)}, u32[]{:S(2)}) collective-permute-start(bf16[512,896]{1,0:T(8,128)(2,1)S(1)} %collective-permute-done.5.refs_9_), channel_id=1, source_target_pairs={{1,0},{0,1},{3,2},{2,3},{5,4},{4,5},{7,6},{6,7},{9,8},{8,9},{11,10... | collective-permute-start | bytes 2752520 | tf_op jit(solution)/shard_map/ppermute | solution.py:56
  56.7 4.7 %collective-permute-start.13 = (bf16[512,896]{1,0:T(8,128)(2,1)S(1)}, bf16[512,896]{1,0:T(8,128)(2,1)}, u32[]{:S(2)}, u32[]{:S(2)}) collective-permute-start(bf16[512,896]{1,0:T(8,128)(2,1)S(1)} %collective-permute-done.8.refs_12_), channel_id=1, source_target_pairs={{1,0},{0,1},{3,2},{2,3},{5,4},{4,5},{7,6},{6,7},{9,8},{8,9},{11,10... | collective-permute-start | bytes 2752520 | tf_op jit(solution)/shard_map/ppermute | solution.py:56
  57.1 5.7 %collective-permute-start.11 = (bf16[512,896]{1,0:T(8,128)(2,1)S(1)}, bf16[512,896]{1,0:T(8,128)(2,1)}, u32[]{:S(2)}, u32[]{:S(2)}) collective-permute-start(bf16[512,896]{1,0:T(8,128)(2,1)S(1)} %collective-permute-done.6.refs_10_), channel_id=1, source_target_pairs={{1,0},{0,1},{3,2},{2,3},{5,4},{4,5},{7,6},{6,7},{9,8},{8,9},{11,10... | collective-permute-start | bytes 2752520 | tf_op jit(solution)/shard_map/ppermute | solution.py:56
  58.3 5.8 %collective-permute-start.12 = (bf16[512,896]{1,0:T(8,128)(2,1)S(1)}, bf16[512,896]{1,0:T(8,128)(2,1)}, u32[]{:S(2)}, u32[]{:S(2)}) collective-permute-start(bf16[512,896]{1,0:T(8,128)(2,1)S(1)} %collective-permute-done.7.refs_11_), channel_id=1, source_target_pairs={{1,0},{0,1},{3,2},{2,3},{5,4},{4,5},{7,6},{6,7},{9,8},{8,9},{11,10... | collective-permute-start | bytes 2752520 | tf_op jit(solution)/shard_map/ppermute | solution.py:56
  76.6 5.3 %collective-permute-start.16 = (f32[16,640]{1,0:T(8,128)S(1)}, f32[16,640]{1,0:T(8,128)S(1)}, u32[]{:S(2)}, u32[]{:S(2)}) collective-permute-start(f32[16,640]{1,0:T(8,128)S(1)} %get-tuple-element.42), channel_id=1, source_target_pairs={{32,1},{33,2},{34,3},{35,4},{36,5},{37,6},{38,7},{39,8},{40,9},{41... | collective-permute-start | bytes 122888 | tf_op jit(solution)/shard_map/ppermute | solution.py:84
  79.2 3.7 %collective-permute-start.15 = (f32[16,640]{1,0:T(8,128)S(1)}, f32[16,640]{1,0:T(8,128)S(1)}, u32[]{:S(2)}, u32[]{:S(2)}) collective-permute-start(f32[16,640]{1,0:T(8,128)S(1)} %get-tuple-element.42), channel_id=1, source_target_pairs={{32,0},{33,1},{34,2},{35,3},{36,4},{37,5},{38,6},{39,7},{40,8},{41... | collective-permute-start | bytes 122888 | tf_op jit(solution)/shard_map/ppermute | solution.py:56
  88.2 7.4 %collective-permute-start.18 = (bf16[48,640]{1,0:T(8,128)(2,1)S(1)}, bf16[48,640]{1,0:T(8,128)(2,1)S(1)}, u32[]{:S(2)}, u32[]{:S(2)}) collective-permute-start(bf16[48,640]{1,0:T(8,128)(2,1)S(1)} %get-tuple-element.50), channel_id=1, source_target_pairs={{48,0},{49,1},{50,2},{51,3},{52,4},{53,5},{54,6},{55,7},{56,8},{57... | collective-permute-start | bytes 184328 | tf_op jit(solution)/shard_map/ppermute | solution.py:56
  89.8 7.2 %collective-permute-start.19 = (bf16[48,640]{1,0:T(8,128)(2,1)S(1)}, bf16[48,640]{1,0:T(8,128)(2,1)S(1)}, u32[]{:S(2)}, u32[]{:S(2)}) collective-permute-start(bf16[48,640]{1,0:T(8,128)(2,1)S(1)} %get-tuple-element.51), channel_id=1, source_target_pairs={{16,0},{17,1},{18,2},{19,3},{20,4},{21,5},{22,6},{23,7},{24,8},{25... | collective-permute-start | bytes 184328 | tf_op jit(solution)/shard_map/ppermute | solution.py:56
  93.7 3.4 %collective-permute-start.20 = (bf16[48,640]{1,0:T(8,128)(2,1)S(1)}, bf16[48,640]{1,0:T(8,128)(2,1)S(1)}, u32[]{:S(2)}, u32[]{:S(2)}) collective-permute-start(bf16[48,640]{1,0:T(8,128)(2,1)S(1)} %get-tuple-element.52), channel_id=1, source_target_pairs={{32,0},{33,1},{34,2},{35,3},{36,4},{37,5},{38,6},{39,7},{40,8},{41... | collective-permute-start | bytes 184328 | tf_op jit(solution)/shard_map/ppermute | solution.py:56
  97.1 6.2 %collective-permute-start.23 = (bf16[48,640]{1,0:T(8,128)(2,1)S(1)}, bf16[48,640]{1,0:T(8,128)(2,1)S(1)}, u32[]{:S(2)}, u32[]{:S(2)}) collective-permute-start(bf16[48,640]{1,0:T(8,128)(2,1)S(1)} %fusion), channel_id=1, source_target_pairs={{4,0},{5,1},{6,2},{7,3},{8,4},{9,5},{10,6},{11,7},{12,8},{13,9},{1... | collective-permute-start | bytes 184328 | tf_op jit(solution)/shard_map/ppermute | solution.py:56
  100.6 4.3 %collective-permute-start.22 = (bf16[48,640]{1,0:T(8,128)(2,1)S(1)}, bf16[48,640]{1,0:T(8,128)(2,1)S(1)}, u32[]{:S(2)}, u32[]{:S(2)}) collective-permute-start(bf16[48,640]{1,0:T(8,128)(2,1)S(1)} %fusion), channel_id=1, source_target_pairs={{14,0},{15,1},{0,2},{1,3},{2,4},{3,5},{4,6},{5,7},{6,8},{7,9},{8,1... | collective-permute-start | bytes 184328 | tf_op jit(solution)/shard_map/ppermute | solution.py:56
  100.9 4.1 %collective-permute-start.21 = (bf16[48,640]{1,0:T(8,128)(2,1)S(1)}, bf16[48,640]{1,0:T(8,128)(2,1)S(1)}, u32[]{:S(2)}, u32[]{:S(2)}) collective-permute-start(bf16[48,640]{1,0:T(8,128)(2,1)S(1)} %fusion), channel_id=1, source_target_pairs={{2,0},{3,1},{4,2},{5,3},{6,4},{7,5},{8,6},{9,7},{10,8},{11,9},{12,... | collective-permute-start | bytes 184328 | tf_op jit(solution)/shard_map/ppermute | solution.py:56
  105.1 7.1 %collective-permute-start.24 = (bf16[48,640]{1,0:T(8,128)(2,1)S(1)}, bf16[48,640]{1,0:T(8,128)(2,1)S(1)}, u32[]{:S(2)}, u32[]{:S(2)}) collective-permute-start(bf16[48,640]{1,0:T(8,128)(2,1)S(1)} %get-tuple-element.57), channel_id=1, source_target_pairs={{8,0},{9,1},{10,2},{11,3},{12,4},{13,5},{14,6},{15,7},{0,8},{1,9},... | collective-permute-start | bytes 184328 | tf_op jit(solution)/shard_map/ppermute | solution.py:56
  112.2 8.8 %collective-permute-start.27 = (bf16[48,640]{1,0:T(8,128)(2,1)S(1)}, bf16[48,640]{1,0:T(8,128)(2,1)S(1)}, u32[]{:S(2)}, u32[]{:S(2)}) collective-permute-start(bf16[48,640]{1,0:T(8,128)(2,1)S(1)} %add_convert_fusion.refs_6_), channel_id=1, source_target_pairs={{48,0},{49,1},{50,2},{51,3},{52,4},{53,5},{54,6},{55,7},{56,8},{57... | collective-permute-start | bytes 184328 | tf_op jit(solution)/shard_map/ppermute | solution.py:56
  113.2 8.6 %collective-permute-start.26 = (bf16[48,640]{1,0:T(8,128)(2,1)S(1)}, bf16[48,640]{1,0:T(8,128)(2,1)S(1)}, u32[]{:S(2)}, u32[]{:S(2)}) collective-permute-start(bf16[48,640]{1,0:T(8,128)(2,1)S(1)} %add_convert_fusion.refs_6_), channel_id=1, source_target_pairs={{16,0},{17,1},{18,2},{19,3},{20,4},{21,5},{22,6},{23,7},{24,8},{25... | collective-permute-start | bytes 184328 | tf_op jit(solution)/shard_map/ppermute | solution.py:56
  116.3 7.0 %collective-permute-start.25 = (bf16[48,640]{1,0:T(8,128)(2,1)S(1)}, bf16[48,640]{1,0:T(8,128)(2,1)S(1)}, u32[]{:S(2)}, u32[]{:S(2)}) collective-permute-start(bf16[48,640]{1,0:T(8,128)(2,1)S(1)} %add_convert_fusion.refs_6_), channel_id=1, source_target_pairs={{32,0},{33,1},{34,2},{35,3},{36,4},{37,5},{38,6},{39,7},{40,8},{41... | collective-permute-start | bytes 184328 | tf_op jit(solution)/shard_map/ppermute | solution.py:56
  116.3 8.4 %collective-permute-start.28 = (bf16[48,640]{1,0:T(8,128)(2,1)S(1)}, bf16[48,640]{1,0:T(8,128)(2,1)S(1)}, u32[]{:S(2)}, u32[]{:S(2)}) collective-permute-start(bf16[48,640]{1,0:T(8,128)(2,1)S(1)} %add_convert_fusion.refs_6_), channel_id=1, source_target_pairs={{1,0},{0,1},{3,2},{2,3},{5,4},{4,5},{7,6},{6,7},{9,8},{8,9},{11,10... | collective-permute-start | bytes 184328 | tf_op jit(solution)/shard_map/ppermute | solution.py:56
  120.9 3.8 %collective-permute-start.31 = (bf16[48,640]{1,0:T(8,128)(2,1)S(1)}, bf16[48,640]{1,0:T(8,128)(2,1)S(1)}, u32[]{:S(2)}, u32[]{:S(2)}) collective-permute-start(bf16[48,640]{1,0:T(8,128)(2,1)S(1)} %collective-permute-done.27.refs_9_), channel_id=1, source_target_pairs={{1,0},{0,1},{3,2},{2,3},{5,4},{4,5},{7,6},{6,7},{9,8},{8,9},{11,10... | collective-permute-start | bytes 184328 | tf_op jit(solution)/shard_map/ppermute | solution.py:56
  121.8 2.9 %collective-permute-start.30 = (bf16[48,640]{1,0:T(8,128)(2,1)S(1)}, bf16[48,640]{1,0:T(8,128)(2,1)S(1)}, u32[]{:S(2)}, u32[]{:S(2)}) collective-permute-start(bf16[48,640]{1,0:T(8,128)(2,1)S(1)} %collective-permute-done.26.refs_8_), channel_id=1, source_target_pairs={{1,0},{0,1},{3,2},{2,3},{5,4},{4,5},{7,6},{6,7},{9,8},{8,9},{11,10... | collective-permute-start | bytes 184328 | tf_op jit(solution)/shard_map/ppermute | solution.py:56
  129.2 9.0 %collective-permute-start.32 = (bf16[128,1280]{1,0:T(8,128)(2,1)S(1)}, bf16[128,1280]{1,0:T(8,128)(2,1)S(1)}, u32[]{:S(2)}, u32[]{:S(2)}) collective-permute-start(bf16[128,1280]{1,0:T(8,128)(2,1)S(1)} %get-tuple-element.54), channel_id=1, source_target_pairs={{64,0},{65,1},{66,2},{67,3},{68,4},{69,5},{70,6},{71,7},{72,8},{73... | collective-permute-start | bytes 983048 | tf_op jit(solution)/shard_map/ppermute | solution.py:56
  129.3 10.3 %collective-permute-start.33 = (bf16[128,1280]{1,0:T(8,128)(2,1)S(1)}, bf16[128,1280]{1,0:T(8,128)(2,1)S(1)}, u32[]{:S(2)}, u32[]{:S(2)}) collective-permute-start(bf16[128,1280]{1,0:T(8,128)(2,1)S(1)} %get-tuple-element.55), channel_id=1, source_target_pairs={{128,0},{129,1},{130,2},{131,3},{132,4},{133,5},{134,6},{135,7},{1... | collective-permute-start | bytes 983048 | tf_op jit(solution)/shard_map/ppermute | solution.py:56
  129.8 17.7 %collective-permute-start.34 = (bf16[128,1280]{1,0:T(8,128)(2,1)S(1)}, bf16[128,1280]{1,0:T(8,128)(2,1)S(1)}, u32[]{:S(2)}, u32[]{:S(2)}) collective-permute-start(bf16[128,1280]{1,0:T(8,128)(2,1)S(1)} %get-tuple-element.56), channel_id=1, source_target_pairs={{192,0},{193,1},{194,2},{195,3},{196,4},{197,5},{198,6},{199,7},{2... | collective-permute-start | bytes 983048 | tf_op jit(solution)/shard_map/ppermute | solution.py:56
  (15 other events, 136.0 us)

commit v3 on v2

--- a/solution.py
+++ b/solution.py
@@ -16,7 +16,7 @@
 PIECES = (PIECE,) * 10
 X_AT, Y_LOW, SAME, Y_AT = 10, 11, 12, 13
 VMEM_LIMIT = 58 * 1024 * 1024
-VMEM_LATE = 44 * 1024 * 1024
+VMEM_LATE = 40 * 1024 * 1024
 VMEM_SMALL = 16 * 1024 * 1024
 FROWS = 160
 MROWS = 192

time: 150 us -> 148 us (0.987)
    unnamed x24 -> x20, local copies, waits for them, and re-layouts: 2.85 us -> 0.72 us
where the time goes in v3:
time: 148 us
  starting transfers between devices  60.1 us (41%)
  waiting for transfers between devices  49 us (33%)
  Pallas kernels  32.9 us (22%)
  local copies, waits for them, and re-layouts  5.82 us (4%)
    ppermute x34, starting transfers between devices, receive(): return lax.ppermute(array, AXES, pairs)  57.5 us
    ppermute x34, waiting for transfers between devices, receive(): return lax.ppermute(array, AXES, pairs)  48.7 us
    pallas_call x1, Pallas kernels, project(): pl.pallas_call(functools.partial(project_kernel, counts), out_shape=[jax....  10.7 us
    pallas_call x1, Pallas kernels, project_early(): pl.pallas_call(functools.partial(early_kernel, counts, len(after)), out_s...  8.63 us
    pallas_call x1, Pallas kernels, pack(): pl.pallas_call(functools.partial(pack_kernel, members), out_shape=[jax.Sh...  4.08 us
    pallas_call x1, Pallas kernels, attend(): pl.pallas_call(attend_kernel, out_shape=[jax.ShapeDtypeStruct((BLOCK, 2 *...  3.53 us
    pallas_call x1, Pallas kernels, states_of(): pl.pallas_call(state_kernel, out_shape=[jax.ShapeDtypeStruct((ROWS, VCOLS...  3.05 us
  transfers between devices with their start and end apart: 35, of which 20 were waited for; matrix products, arithmetic and copies ran while one was open for 3% of the time, Pallas kernels for 9%

profile of v3, /device:TPU:1, one launch (start us, length us, event | category | flops | bytes accessed | tf_op | source)
XLA Modules:
  0.0 148.1 jit_solution(5472610938492070148)
XLA Ops:
  0.0 2.0 %collective-permute-start.1 = (bf16[128,5120]{1,0:T(8,128)(2,1)}, bf16[128,5120]{1,0:T(8,128)(2,1)}, u32[]{:S(2)}, u32[]{:S(2)}) collective-permute-start(bf16[128,5120]{1,0:T(8,128)(2,1)} %bitcast.16), channel_id=1, source_target_pairs={{192,0},{193,1},{194,2},{195,3},{196,4},{197,5},{198,6},{199,7},{2... | collective-permute-start | bytes 3932168 | tf_op jit(solution)/shard_map/ppermute | solution.py:56
  3.9 4.1 %shard_map.65 = (bf16[512,896]{1,0:T(8,128)(2,1)}, bf16[512,896]{1,0:T(8,128)(2,1)}, bf16[512,896]{1,0:T(8,128)(2,1)}) custom-call(s32[14]{0:T(128)} %stack.63.control.offsets.place, bf16[5120,128]{1,0:T(8,128)(2,1)} %refs_5_.3, bf16[5120,128]{1,0:T(8,128)(2,1)} %refs_6_.3, bf16[5120,640]{1,0:T(8,128)(2,1)} %refs_7_.1), custom_call_target="tpu_custom_call" | custom-call | tf_op jit(solution)/shard_map/pallas_call | solution.py:398
  8.0 3.0 %collective-permute-start.4 = (bf16[512,896]{1,0:T(8,128)(2,1)}, bf16[512,896]{1,0:T(8,128)(2,1)S(1)}, u32[]{:S(2)}, u32[]{:S(2)}) collective-permute-start(bf16[512,896]{1,0:T(8,128)(2,1)} %get-tuple-element.32), channel_id=1, source_target_pairs={{48,0},{33,1},{50,2},{35,3},{52,4},{37,5},{54,6},{39,7},{56,8},{41... | collective-permute-start | bytes 2752520 | tf_op jit(solution)/shard_map/ppermute | solution.py:56
  11.6 10.0 %collective-permute-done.4.refs_8_ = bf16[512,896]{1,0:T(8,128)(2,1)S(1)} collective-permute-done((bf16[512,896]{1,0:T(8,128)(2,1)}, bf16[512,896]{1,0:T(8,128)(2,1)S(1)}, u32[]{:S(2)}, u32[]{:S(2)}) %collective-permute-start.4) | collective-permute-done | bytes 917536 | tf_op jit(solution)/shard_map/ppermute | solution.py:56
  21.6 5.6 %collective-permute-start.6 = (bf16[512,896]{1,0:T(8,128)(2,1)S(1)}, bf16[512,896]{1,0:T(8,128)(2,1)S(1)}, u32[]{:S(2)}, u32[]{:S(2)}) collective-permute-start(bf16[512,896]{1,0:T(8,128)(2,1)S(1)} %collective-permute-done.4.refs_8_), channel_id=1, source_target_pairs={{14,0},{3,1},{0,2},{5,3},{2,4},{7,5},{4,6},{9,7},{6,8},{11,9},{8,1... | collective-permute-start | bytes 2752520 | tf_op jit(solution)/shard_map/ppermute | solution.py:56
  27.2 4.3 %collective-permute-done.5.refs_9_ = bf16[512,896]{1,0:T(8,128)(2,1)S(1)} collective-permute-done((bf16[512,896]{1,0:T(8,128)(2,1)}, bf16[512,896]{1,0:T(8,128)(2,1)S(1)}, u32[]{:S(2)}, u32[]{:S(2)}) %collective-permute-start.5) | collective-permute-done | bytes 917536 | tf_op jit(solution)/shard_map/ppermute | solution.py:56
  31.5 5.6 %collective-permute-start.7 = (bf16[512,896]{1,0:T(8,128)(2,1)S(1)}, bf16[512,896]{1,0:T(8,128)(2,1)S(1)}, u32[]{:S(2)}, u32[]{:S(2)}) collective-permute-start(bf16[512,896]{1,0:T(8,128)(2,1)S(1)} %collective-permute-done.5.refs_9_), channel_id=1, source_target_pairs={{14,0},{3,1},{0,2},{5,3},{2,4},{7,5},{4,6},{9,7},{6,8},{11,9},{8,1... | collective-permute-start | bytes 2752520 | tf_op jit(solution)/shard_map/ppermute | solution.py:56
  37.1 2.0 %slice.9 = bf16[64,5120]{1,0:T(8,128)(2,1)} slice(bf16[128,5120]{1,0:T(8,128)(2,1)} %collective-permute-done.1.refs_2_), slice={[64:128], [0:5120]} | slice | bytes 1310720 | tf_op jit(solution)/shard_map/slice | solution.py:525
  39.0 2.0 %slice.8 = bf16[64,5120]{1,0:T(8,128)(2,1)} slice(bf16[128,5120]{1,0:T(8,128)(2,1)} %collective-permute-done.refs_1_), slice={[0:64], [0:5120]} | slice | bytes 1310720 | tf_op jit(solution)/shard_map/slice | solution.py:524
  41.0 2.7 %collective-permute-start.2 = (bf16[64,5120]{1,0:T(8,128)(2,1)}, bf16[64,5120]{1,0:T(8,128)(2,1)}, u32[]{:S(2)}, u32[]{:S(2)}) collective-permute-start(bf16[64,5120]{1,0:T(8,128)(2,1)} %slice.8), channel_id=1, source_target_pairs={{64,0},{65,1},{66,2},{67,3},{68,4},{69,5},{70,6},{71,7},{72,8},{73... | collective-permute-start | bytes 1966088 | tf_op jit(solution)/shard_map/ppermute | solution.py:56
  44.3 8.6 %shard_map.64 = (bf16[384,640]{1,0:T(8,128)(2,1)}, f32[384,256]{1,0:T(8,128)}, f32[8,640]{1,0:T(8,128)}, f32[4,640]{1,0:T(4,128)}) custom-call(bf16[128,5120]{1,0:T(8,128)(2,1)} %bitcast.18, bf16[128,5120]{1,0:T(8,128)(2,1)} %collective-permute-done.refs_1_, bf16[128,5120]{1,0:T(8,128)(2,1)} %collective-permute-done.1.refs_2_, bf16[5120,128]{1,0:T(8,128)(2,1)} %refs_5_.3, ...), custom_call_target="tpu_custom_call" | custom-call | flops 3000000000 | bytes 3000000 | tf_op jit(solution)/shard_map/pallas_call | solution.py:172
  53.8 2.5 %collective-permute-done.14.early.refs_9_.refs_5_ = f32[4,640]{1,0:T(4,128)S(1)} collective-permute-done((f32[4,640]{1,0:T(4,128)}, f32[4,640]{1,0:T(4,128)S(1)}, u32[]{:S(2)}, u32[]{:S(2)}) %collective-permute-start.14) | collective-permute-done | bytes 10272 | tf_op jit(solution)/shard_map/ppermute | solution.py:56
  64.8 10.7 %shard_map.67 = (bf16[128,640]{1,0:T(8,128)(2,1)S(1)}, bf16[512,640]{1,0:T(8,128)(2,1)S(1)}, f32[128,256]{1,0:T(8,128)S(1)}, f32[512,256]{1,0:T(8,128)S(1)}, f32[16,640]{1,0:T(8,128)S(1)}) custom-call(s32[14]{0:T(128)S(1)} %copy-done.1, bf16[128,5120]{1,0:T(8,128)(2,1)S(1)} %bitcast.19, bf16[128,5120]{1,0:T(8,128)(2,1)} %collective-permute-done.refs_1_, ...), custom_call_target="tpu_custom_call" | custom-call | flops 7046430720 | bytes 23592960 | tf_op jit(solution)/shard_map/pallas_call | solution.py:269
  75.5 2.6 %collective-permute-start.16 = (f32[16,640]{1,0:T(8,128)S(1)}, f32[16,640]{1,0:T(8,128)S(1)}, u32[]{:S(2)}, u32[]{:S(2)}) collective-permute-start(f32[16,640]{1,0:T(8,128)S(1)} %get-tuple-element.42), channel_id=1, source_target_pairs={{32,1},{33,2},{34,3},{35,4},{36,5},{37,6},{38,7},{39,8},{40,9},{41... | collective-permute-start | bytes 122888 | tf_op jit(solution)/shard_map/ppermute | solution.py:84
  78.1 2.3 %collective-permute-start.15 = (f32[16,640]{1,0:T(8,128)S(1)}, f32[16,640]{1,0:T(8,128)S(1)}, u32[]{:S(2)}, u32[]{:S(2)}) collective-permute-start(f32[16,640]{1,0:T(8,128)S(1)} %get-tuple-element.42), channel_id=1, source_target_pairs={{32,0},{33,1},{34,2},{35,3},{36,4},{37,5},{38,6},{39,7},{40,8},{41... | collective-permute-start | bytes 122888 | tf_op jit(solution)/shard_map/ppermute | solution.py:56
  81.8 3.0 %shard_map.68 = (bf16[512,640]{1,0:T(8,128)(2,1)S(1)}, bf16[512,640]{1,0:T(8,128)(2,1)S(1)}, f32[128,512]{1,0:T(8,128)S(1)}, f32[128,512]{1,0:T(8,128)S(1)}, f32...) custom-call(s32[14]{0:T(128)S(1)} %copy-done.1, bf16[384,640]{1,0:T(8,128)(2,1)S(1)} %copy-done.5, ...), custom_call_target="tpu_custom_call" | custom-call | flops 6000000000 | bytes 8000000 | tf_op jit(solution)/shard_map/pallas_call | solution.py:361
  85.1 1.4 collective-permute-done.17.got
  87.1 1.5 %collective-permute-start.18 = (bf16[48,640]{1,0:T(8,128)(2,1)S(1)}, bf16[48,640]{1,0:T(8,128)(2,1)S(1)}, u32[]{:S(2)}, u32[]{:S(2)}) collective-permute-start(bf16[48,640]{1,0:T(8,128)(2,1)S(1)} %get-tuple-element.50), channel_id=1, source_target_pairs={{48,0},{49,1},{50,2},{51,3},{52,4},{53,5},{54,6},{55,7},{56,8},{57... | collective-permute-start | bytes 184328 | tf_op jit(solution)/shard_map/ppermute | solution.py:56
  88.6 4.1 %collective-permute-start.19 = (bf16[48,640]{1,0:T(8,128)(2,1)S(1)}, bf16[48,640]{1,0:T(8,128)(2,1)S(1)}, u32[]{:S(2)}, u32[]{:S(2)}) collective-permute-start(bf16[48,640]{1,0:T(8,128)(2,1)S(1)} %get-tuple-element.51), channel_id=1, source_target_pairs={{16,0},{17,1},{18,2},{19,3},{20,4},{21,5},{22,6},{23,7},{24,8},{25... | collective-permute-start | bytes 184328 | tf_op jit(solution)/shard_map/ppermute | solution.py:56
  92.7 2.0 %collective-permute-start.20 = (bf16[48,640]{1,0:T(8,128)(2,1)S(1)}, bf16[48,640]{1,0:T(8,128)(2,1)S(1)}, u32[]{:S(2)}, u32[]{:S(2)}) collective-permute-start(bf16[48,640]{1,0:T(8,128)(2,1)S(1)} %get-tuple-element.52), channel_id=1, source_target_pairs={{32,0},{33,1},{34,2},{35,3},{36,4},{37,5},{38,6},{39,7},{40,8},{41... | collective-permute-start | bytes 184328 | tf_op jit(solution)/shard_map/ppermute | solution.py:56
  96.1 3.4 %collective-permute-start.23 = (bf16[48,640]{1,0:T(8,128)(2,1)S(1)}, bf16[48,640]{1,0:T(8,128)(2,1)S(1)}, u32[]{:S(2)}, u32[]{:S(2)}) collective-permute-start(bf16[48,640]{1,0:T(8,128)(2,1)S(1)} %fusion), channel_id=1, source_target_pairs={{4,0},{5,1},{6,2},{7,3},{8,4},{9,5},{10,6},{11,7},{12,8},{13,9},{1... | collective-permute-start | bytes 184328 | tf_op jit(solution)/shard_map/ppermute | solution.py:56
  99.8 2.4 %collective-permute-start.21 = (bf16[48,640]{1,0:T(8,128)(2,1)S(1)}, bf16[48,640]{1,0:T(8,128)(2,1)S(1)}, u32[]{:S(2)}, u32[]{:S(2)}) collective-permute-start(bf16[48,640]{1,0:T(8,128)(2,1)S(1)} %fusion), channel_id=1, source_target_pairs={{2,0},{3,1},{4,2},{5,3},{6,4},{7,5},{8,6},{9,7},{10,8},{11,9},{12,... | collective-permute-start | bytes 184328 | tf_op jit(solution)/shard_map/ppermute | solution.py:56
  102.2 1.6 %collective-permute-done.22 = bf16[48,640]{1,0:T(8,128)(2,1)S(1)} collective-permute-done((bf16[48,640]{1,0:T(8,128)(2,1)S(1)}, bf16[48,640]{1,0:T(8,128)(2,1)S(1)}, u32[]{:S(2)}, u32[]{:S(2)}) %collective-permute-start.22) | collective-permute-done | bytes 61472 | tf_op jit(solution)/shard_map/ppermute | solution.py:56
  103.9 4.4 %collective-permute-start.24 = (bf16[48,640]{1,0:T(8,128)(2,1)S(1)}, bf16[48,640]{1,0:T(8,128)(2,1)S(1)}, u32[]{:S(2)}, u32[]{:S(2)}) collective-permute-start(bf16[48,640]{1,0:T(8,128)(2,1)S(1)} %get-tuple-element.57), channel_id=1, source_target_pairs={{8,0},{9,1},{10,2},{11,3},{12,4},{13,5},{14,6},{15,7},{0,8},{1,9},... | collective-permute-start | bytes 184328 | tf_op jit(solution)/shard_map/ppermute | solution.py:56
  108.4 2.7 %collective-permute-done.24 = bf16[48,640]{1,0:T(8,128)(2,1)S(1)} collective-permute-done((bf16[48,640]{1,0:T(8,128)(2,1)S(1)}, bf16[48,640]{1,0:T(8,128)(2,1)S(1)}, u32[]{:S(2)}, u32[]{:S(2)}) %collective-permute-start.24) | collective-permute-done | bytes 61472 | tf_op jit(solution)/shard_map/ppermute | solution.py:56
  112.1 3.1 %collective-permute-start.26 = (bf16[48,640]{1,0:T(8,128)(2,1)S(1)}, bf16[48,640]{1,0:T(8,128)(2,1)S(1)}, u32[]{:S(2)}, u32[]{:S(2)}) collective-permute-start(bf16[48,640]{1,0:T(8,128)(2,1)S(1)} %add_convert_fusion.refs_6_), channel_id=1, source_target_pairs={{16,0},{17,1},{18,2},{19,3},{20,4},{21,5},{22,6},{23,7},{24,8},{25... | collective-permute-start | bytes 184328 | tf_op jit(solution)/shard_map/ppermute | solution.py:56
  115.2 4.6 %collective-permute-start.28 = (bf16[48,640]{1,0:T(8,128)(2,1)S(1)}, bf16[48,640]{1,0:T(8,128)(2,1)S(1)}, u32[]{:S(2)}, u32[]{:S(2)}) collective-permute-start(bf16[48,640]{1,0:T(8,128)(2,1)S(1)} %add_convert_fusion.refs_6_), channel_id=1, source_target_pairs={{1,0},{0,1},{3,2},{2,3},{5,4},{4,5},{7,6},{6,7},{9,8},{8,9},{11,10... | collective-permute-start | bytes 184328 | tf_op jit(solution)/shard_map/ppermute | solution.py:56
  120.7 1.6 %collective-permute-start.30 = (bf16[48,640]{1,0:T(8,128)(2,1)S(1)}, bf16[48,640]{1,0:T(8,128)(2,1)S(1)}, u32[]{:S(2)}, u32[]{:S(2)}) collective-permute-start(bf16[48,640]{1,0:T(8,128)(2,1)S(1)} %collective-permute-done.26.refs_8_), channel_id=1, source_target_pairs={{1,0},{0,1},{3,2},{2,3},{5,4},{4,5},{7,6},{6,7},{9,8},{8,9},{11,10... | collective-permute-start | bytes 184328 | tf_op jit(solution)/shard_map/ppermute | solution.py:56
  124.5 3.5 %shard_map.70 = (bf16[128,1280]{1,0:T(8,128)(2,1)S(1)}, bf16[128,1280]{1,0:T(8,128)(2,1)S(1)}, bf16[128,1280]{1,0:T(8,128)(2,1)S(1)}, bf16[128,1280]{1,0:T(8,128)(2,1)S(1)}) custom-call(s32[14]{0:T(128)S(1)} %copy-done.1, f32[128,512]{1,0:T(8,128)S(1)} %get-tuple-element.43.refs_0_, bf16[512,640]{1,0:T(8,128)(2,1)S(1)} %get-tuple-element.44.refs_1_, ...), custom_call_target="tpu_custom_call" | custom-call | tf_op jit(solution)/shard_map/pallas_call | solution.py:484
  129.6 7.5 %collective-permute-done.32.refs_1_ = bf16[128,1280]{1,0:T(8,128)(2,1)S(1)} collective-permute-done((bf16[128,1280]{1,0:T(8,128)(2,1)S(1)}, bf16[128,1280]{1,0:T(8,128)(2,1)S(1)}, u32[]{:S(2)}, u32[]{:S(2)}) %collective-permute-start.32) | collective-permute-done | bytes 327712 | tf_op jit(solution)/shard_map/ppermute | solution.py:56
  138.4 7.9 %collective-permute-done.34.refs_3_ = bf16[128,1280]{1,0:T(8,128)(2,1)S(1)} collective-permute-done((bf16[128,1280]{1,0:T(8,128)(2,1)S(1)}, bf16[128,1280]{1,0:T(8,128)(2,1)S(1)}, u32[]{:S(2)}, u32[]{:S(2)}) %collective-permute-start.34) | collective-permute-done | bytes 327712 | tf_op jit(solution)/shard_map/ppermute | solution.py:56
  146.4 1.7 %shard_map.71 = bf16[128,5120]{1,0:T(8,128)(2,1)} custom-call(s32[14]{0:T(128)S(1)} %copy-done.1, bf16[128,1280]{1,0:T(8,128)(2,1)S(1)} %get-tuple-element.53.refs_0_, bf16[128,1280]{1,0:T(8,128)(2,1)S(1)} %collective-permute-done.32.refs_1_, bf16[128,1280]{1,0:T(8,128)(2,1)S(1)} %collective-permute-done.33.refs_2_, ...), custom_call_target="tpu_custom_call" | custom-call | tf_op jit(solution)/shard_map/pallas_call | solution.py:441
  (73 shorter events, 23.7 us)
Async XLA Ops:
  0.0 37.1 %collective-permute-start.1 = (bf16[128,5120]{1,0:T(8,128)(2,1)}, bf16[128,5120]{1,0:T(8,128)(2,1)}, u32[]{:S(2)}, u32[]{:S(2)}) collective-permute-start(bf16[128,5120]{1,0:T(8,128)(2,1)} %bitcast.16), channel_id=1, source_target_pairs={{192,0},{193,1},{194,2},{195,3},{196,4},{197,5},{198,6},{199,7},{2... | collective-permute-start | bytes 3932168 | tf_op jit(solution)/shard_map/ppermute | solution.py:56
  2.0 37.0 %collective-permute-start = (bf16[128,5120]{1,0:T(8,128)(2,1)}, bf16[128,5120]{1,0:T(8,128)(2,1)}, u32[]{:S(2)}, u32[]{:S(2)}) collective-permute-start(bf16[128,5120]{1,0:T(8,128)(2,1)} %bitcast.17), channel_id=1, source_target_pairs={{64,0},{65,1},{66,2},{67,3},{68,4},{69,5},{70,6},{71,7},{72,8},{73... | collective-permute-start | bytes 3932168 | tf_op jit(solution)/shard_map/ppermute | solution.py:56
  8.0 13.7 %collective-permute-start.4 = (bf16[512,896]{1,0:T(8,128)(2,1)}, bf16[512,896]{1,0:T(8,128)(2,1)S(1)}, u32[]{:S(2)}, u32[]{:S(2)}) collective-permute-start(bf16[512,896]{1,0:T(8,128)(2,1)} %get-tuple-element.32), channel_id=1, source_target_pairs={{48,0},{33,1},{50,2},{35,3},{52,4},{37,5},{54,6},{39,7},{56,8},{41... | collective-permute-start | bytes 2752520 | tf_op jit(solution)/shard_map/ppermute | solution.py:56
  11.0 20.5 %collective-permute-start.5 = (bf16[512,896]{1,0:T(8,128)(2,1)}, bf16[512,896]{1,0:T(8,128)(2,1)S(1)}, u32[]{:S(2)}, u32[]{:S(2)}) collective-permute-start(bf16[512,896]{1,0:T(8,128)(2,1)} %get-tuple-element.33), channel_id=1, source_target_pairs={{48,0},{33,1},{50,2},{35,3},{52,4},{37,5},{54,6},{39,7},{56,8},{41... | collective-permute-start | bytes 2752520 | tf_op jit(solution)/shard_map/ppermute | solution.py:56
  11.5 41.5 %collective-permute-start.8 = (bf16[512,896]{1,0:T(8,128)(2,1)}, bf16[512,896]{1,0:T(8,128)(2,1)S(1)}, u32[]{:S(2)}, u32[]{:S(2)}) collective-permute-start(bf16[512,896]{1,0:T(8,128)(2,1)} %get-tuple-element.34), channel_id=1, source_target_pairs={{48,0},{33,1},{50,2},{35,3},{52,4},{37,5},{54,6},{39,7},{56,8},{41... | collective-permute-start | bytes 2752520 | tf_op jit(solution)/shard_map/ppermute | solution.py:56
  21.6 34.9 %collective-permute-start.6 = (bf16[512,896]{1,0:T(8,128)(2,1)S(1)}, bf16[512,896]{1,0:T(8,128)(2,1)S(1)}, u32[]{:S(2)}, u32[]{:S(2)}) collective-permute-start(bf16[512,896]{1,0:T(8,128)(2,1)S(1)} %collective-permute-done.4.refs_8_), channel_id=1, source_target_pairs={{14,0},{3,1},{0,2},{5,3},{2,4},{7,5},{4,6},{9,7},{6,8},{11,9},{8,1... | collective-permute-start | bytes 2752520 | tf_op jit(solution)/shard_map/ppermute | solution.py:56
  31.5 25.3 %collective-permute-start.7 = (bf16[512,896]{1,0:T(8,128)(2,1)S(1)}, bf16[512,896]{1,0:T(8,128)(2,1)S(1)}, u32[]{:S(2)}, u32[]{:S(2)}) collective-permute-start(bf16[512,896]{1,0:T(8,128)(2,1)S(1)} %collective-permute-done.5.refs_9_), channel_id=1, source_target_pairs={{14,0},{3,1},{0,2},{5,3},{2,4},{7,5},{4,6},{9,7},{6,8},{11,9},{8,1... | collective-permute-start | bytes 2752520 | tf_op jit(solution)/shard_map/ppermute | solution.py:56
  39.0 18.1 %collective-permute-start.3 = (bf16[64,5120]{1,0:T(8,128)(2,1)}, bf16[64,5120]{1,0:T(8,128)(2,1)}, u32[]{:S(2)}, u32[]{:S(2)}) collective-permute-start(bf16[64,5120]{1,0:T(8,128)(2,1)} %slice.9), channel_id=1, source_target_pairs={{192,0},{193,1},{194,2},{195,3},{196,4},{197,5},{198,6},{199,7},{2... | collective-permute-start | bytes 1966088 | tf_op jit(solution)/shard_map/ppermute | solution.py:56
  41.0 17.3 %collective-permute-start.2 = (bf16[64,5120]{1,0:T(8,128)(2,1)}, bf16[64,5120]{1,0:T(8,128)(2,1)}, u32[]{:S(2)}, u32[]{:S(2)}) collective-permute-start(bf16[64,5120]{1,0:T(8,128)(2,1)} %slice.8), channel_id=1, source_target_pairs={{64,0},{65,1},{66,2},{67,3},{68,4},{69,5},{70,6},{71,7},{72,8},{73... | collective-permute-start | bytes 1966088 | tf_op jit(solution)/shard_map/ppermute | solution.py:56
  52.9 3.3 %collective-permute-start.14 = (f32[4,640]{1,0:T(4,128)}, f32[4,640]{1,0:T(4,128)S(1)}, u32[]{:S(2)}, u32[]{:S(2)}) collective-permute-start(f32[4,640]{1,0:T(4,128)} %get-tuple-element.36.refs_8_.refs_2_), channel_id=1, source_target_pairs={{32,0},{33,1},{34,2},{35,3},{36,4},{37,5},{38,6},{39,7},{40,8},{41... | collective-permute-start | bytes 30728 | tf_op jit(solution)/shard_map/ppermute | solution.py:56
  56.6 3.6 %collective-permute-start.10 = (bf16[512,896]{1,0:T(8,128)(2,1)S(1)}, bf16[512,896]{1,0:T(8,128)(2,1)}, u32[]{:S(2)}, u32[]{:S(2)}) collective-permute-start(bf16[512,896]{1,0:T(8,128)(2,1)S(1)} %collective-permute-done.5.refs_9_), channel_id=1, source_target_pairs={{1,0},{0,1},{3,2},{2,3},{5,4},{4,5},{7,6},{6,7},{9,8},{8,9},{11,10... | collective-permute-start | bytes 2752520 | tf_op jit(solution)/shard_map/ppermute | solution.py:56
  56.8 4.7 %collective-permute-start.13 = (bf16[512,896]{1,0:T(8,128)(2,1)S(1)}, bf16[512,896]{1,0:T(8,128)(2,1)}, u32[]{:S(2)}, u32[]{:S(2)}) collective-permute-start(bf16[512,896]{1,0:T(8,128)(2,1)S(1)} %collective-permute-done.8.refs_12_), channel_id=1, source_target_pairs={{1,0},{0,1},{3,2},{2,3},{5,4},{4,5},{7,6},{6,7},{9,8},{8,9},{11,10... | collective-permute-start | bytes 2752520 | tf_op jit(solution)/shard_map/ppermute | solution.py:56
  57.1 5.7 %collective-permute-start.11 = (bf16[512,896]{1,0:T(8,128)(2,1)S(1)}, bf16[512,896]{1,0:T(8,128)(2,1)}, u32[]{:S(2)}, u32[]{:S(2)}) collective-permute-start(bf16[512,896]{1,0:T(8,128)(2,1)S(1)} %collective-permute-done.6.refs_10_), channel_id=1, source_target_pairs={{1,0},{0,1},{3,2},{2,3},{5,4},{4,5},{7,6},{6,7},{9,8},{8,9},{11,10... | collective-permute-start | bytes 2752520 | tf_op jit(solution)/shard_map/ppermute | solution.py:56
  58.3 5.8 %collective-permute-start.12 = (bf16[512,896]{1,0:T(8,128)(2,1)S(1)}, bf16[512,896]{1,0:T(8,128)(2,1)}, u32[]{:S(2)}, u32[]{:S(2)}) collective-permute-start(bf16[512,896]{1,0:T(8,128)(2,1)S(1)} %collective-permute-done.7.refs_11_), channel_id=1, source_target_pairs={{1,0},{0,1},{3,2},{2,3},{5,4},{4,5},{7,6},{6,7},{9,8},{8,9},{11,10... | collective-permute-start | bytes 2752520 | tf_op jit(solution)/shard_map/ppermute | solution.py:56
  75.5 5.3 %collective-permute-start.16 = (f32[16,640]{1,0:T(8,128)S(1)}, f32[16,640]{1,0:T(8,128)S(1)}, u32[]{:S(2)}, u32[]{:S(2)}) collective-permute-start(f32[16,640]{1,0:T(8,128)S(1)} %get-tuple-element.42), channel_id=1, source_target_pairs={{32,1},{33,2},{34,3},{35,4},{36,5},{37,6},{38,7},{39,8},{40,9},{41... | collective-permute-start | bytes 122888 | tf_op jit(solution)/shard_map/ppermute | solution.py:84
  78.1 3.7 %collective-permute-start.15 = (f32[16,640]{1,0:T(8,128)S(1)}, f32[16,640]{1,0:T(8,128)S(1)}, u32[]{:S(2)}, u32[]{:S(2)}) collective-permute-start(f32[16,640]{1,0:T(8,128)S(1)} %get-tuple-element.42), channel_id=1, source_target_pairs={{32,0},{33,1},{34,2},{35,3},{36,4},{37,5},{38,6},{39,7},{40,8},{41... | collective-permute-start | bytes 122888 | tf_op jit(solution)/shard_map/ppermute | solution.py:56
  87.1 7.6 %collective-permute-start.18 = (bf16[48,640]{1,0:T(8,128)(2,1)S(1)}, bf16[48,640]{1,0:T(8,128)(2,1)S(1)}, u32[]{:S(2)}, u32[]{:S(2)}) collective-permute-start(bf16[48,640]{1,0:T(8,128)(2,1)S(1)} %get-tuple-element.50), channel_id=1, source_target_pairs={{48,0},{49,1},{50,2},{51,3},{52,4},{53,5},{54,6},{55,7},{56,8},{57... | collective-permute-start | bytes 184328 | tf_op jit(solution)/shard_map/ppermute | solution.py:56
  88.6 7.3 %collective-permute-start.19 = (bf16[48,640]{1,0:T(8,128)(2,1)S(1)}, bf16[48,640]{1,0:T(8,128)(2,1)S(1)}, u32[]{:S(2)}, u32[]{:S(2)}) collective-permute-start(bf16[48,640]{1,0:T(8,128)(2,1)S(1)} %get-tuple-element.51), channel_id=1, source_target_pairs={{16,0},{17,1},{18,2},{19,3},{20,4},{21,5},{22,6},{23,7},{24,8},{25... | collective-permute-start | bytes 184328 | tf_op jit(solution)/shard_map/ppermute | solution.py:56
  92.7 3.4 %collective-permute-start.20 = (bf16[48,640]{1,0:T(8,128)(2,1)S(1)}, bf16[48,640]{1,0:T(8,128)(2,1)S(1)}, u32[]{:S(2)}, u32[]{:S(2)}) collective-permute-start(bf16[48,640]{1,0:T(8,128)(2,1)S(1)} %get-tuple-element.52), channel_id=1, source_target_pairs={{32,0},{33,1},{34,2},{35,3},{36,4},{37,5},{38,6},{39,7},{40,8},{41... | collective-permute-start | bytes 184328 | tf_op jit(solution)/shard_map/ppermute | solution.py:56
  96.1 6.1 %collective-permute-start.23 = (bf16[48,640]{1,0:T(8,128)(2,1)S(1)}, bf16[48,640]{1,0:T(8,128)(2,1)S(1)}, u32[]{:S(2)}, u32[]{:S(2)}) collective-permute-start(bf16[48,640]{1,0:T(8,128)(2,1)S(1)} %fusion), channel_id=1, source_target_pairs={{4,0},{5,1},{6,2},{7,3},{8,4},{9,5},{10,6},{11,7},{12,8},{13,9},{1... | collective-permute-start | bytes 184328 | tf_op jit(solution)/shard_map/ppermute | solution.py:56
  99.5 4.3 %collective-permute-start.22 = (bf16[48,640]{1,0:T(8,128)(2,1)S(1)}, bf16[48,640]{1,0:T(8,128)(2,1)S(1)}, u32[]{:S(2)}, u32[]{:S(2)}) collective-permute-start(bf16[48,640]{1,0:T(8,128)(2,1)S(1)} %fusion), channel_id=1, source_target_pairs={{14,0},{15,1},{0,2},{1,3},{2,4},{3,5},{4,6},{5,7},{6,8},{7,9},{8,1... | collective-permute-start | bytes 184328 | tf_op jit(solution)/shard_map/ppermute | solution.py:56
  99.8 4.1 %collective-permute-start.21 = (bf16[48,640]{1,0:T(8,128)(2,1)S(1)}, bf16[48,640]{1,0:T(8,128)(2,1)S(1)}, u32[]{:S(2)}, u32[]{:S(2)}) collective-permute-start(bf16[48,640]{1,0:T(8,128)(2,1)S(1)} %fusion), channel_id=1, source_target_pairs={{2,0},{3,1},{4,2},{5,3},{6,4},{7,5},{8,6},{9,7},{10,8},{11,9},{12,... | collective-permute-start | bytes 184328 | tf_op jit(solution)/shard_map/ppermute | solution.py:56
  103.9 7.1 %collective-permute-start.24 = (bf16[48,640]{1,0:T(8,128)(2,1)S(1)}, bf16[48,640]{1,0:T(8,128)(2,1)S(1)}, u32[]{:S(2)}, u32[]{:S(2)}) collective-permute-start(bf16[48,640]{1,0:T(8,128)(2,1)S(1)} %get-tuple-element.57), channel_id=1, source_target_pairs={{8,0},{9,1},{10,2},{11,3},{12,4},{13,5},{14,6},{15,7},{0,8},{1,9},... | collective-permute-start | bytes 184328 | tf_op jit(solution)/shard_map/ppermute | solution.py:56
  111.0 8.8 %collective-permute-start.27 = (bf16[48,640]{1,0:T(8,128)(2,1)S(1)}, bf16[48,640]{1,0:T(8,128)(2,1)S(1)}, u32[]{:S(2)}, u32[]{:S(2)}) collective-permute-start(bf16[48,640]{1,0:T(8,128)(2,1)S(1)} %add_convert_fusion.refs_6_), channel_id=1, source_target_pairs={{48,0},{49,1},{50,2},{51,3},{52,4},{53,5},{54,6},{55,7},{56,8},{57... | collective-permute-start | bytes 184328 | tf_op jit(solution)/shard_map/ppermute | solution.py:56
  112.1 8.6 %collective-permute-start.26 = (bf16[48,640]{1,0:T(8,128)(2,1)S(1)}, bf16[48,640]{1,0:T(8,128)(2,1)S(1)}, u32[]{:S(2)}, u32[]{:S(2)}) collective-permute-start(bf16[48,640]{1,0:T(8,128)(2,1)S(1)} %add_convert_fusion.refs_6_), channel_id=1, source_target_pairs={{16,0},{17,1},{18,2},{19,3},{20,4},{21,5},{22,6},{23,7},{24,8},{25... | collective-permute-start | bytes 184328 | tf_op jit(solution)/shard_map/ppermute | solution.py:56
  115.2 7.0 %collective-permute-start.25 = (bf16[48,640]{1,0:T(8,128)(2,1)S(1)}, bf16[48,640]{1,0:T(8,128)(2,1)S(1)}, u32[]{:S(2)}, u32[]{:S(2)}) collective-permute-start(bf16[48,640]{1,0:T(8,128)(2,1)S(1)} %add_convert_fusion.refs_6_), channel_id=1, source_target_pairs={{32,0},{33,1},{34,2},{35,3},{36,4},{37,5},{38,6},{39,7},{40,8},{41... | collective-permute-start | bytes 184328 | tf_op jit(solution)/shard_map/ppermute | solution.py:56
  115.2 8.4 %collective-permute-start.28 = (bf16[48,640]{1,0:T(8,128)(2,1)S(1)}, bf16[48,640]{1,0:T(8,128)(2,1)S(1)}, u32[]{:S(2)}, u32[]{:S(2)}) collective-permute-start(bf16[48,640]{1,0:T(8,128)(2,1)S(1)} %add_convert_fusion.refs_6_), channel_id=1, source_target_pairs={{1,0},{0,1},{3,2},{2,3},{5,4},{4,5},{7,6},{6,7},{9,8},{8,9},{11,10... | collective-permute-start | bytes 184328 | tf_op jit(solution)/shard_map/ppermute | solution.py:56
  119.8 3.8 %collective-permute-start.31 = (bf16[48,640]{1,0:T(8,128)(2,1)S(1)}, bf16[48,640]{1,0:T(8,128)(2,1)S(1)}, u32[]{:S(2)}, u32[]{:S(2)}) collective-permute-start(bf16[48,640]{1,0:T(8,128)(2,1)S(1)} %collective-permute-done.27.refs_9_), channel_id=1, source_target_pairs={{1,0},{0,1},{3,2},{2,3},{5,4},{4,5},{7,6},{6,7},{9,8},{8,9},{11,10... | collective-permute-start | bytes 184328 | tf_op jit(solution)/shard_map/ppermute | solution.py:56
  120.7 2.9 %collective-permute-start.30 = (bf16[48,640]{1,0:T(8,128)(2,1)S(1)}, bf16[48,640]{1,0:T(8,128)(2,1)S(1)}, u32[]{:S(2)}, u32[]{:S(2)}) collective-permute-start(bf16[48,640]{1,0:T(8,128)(2,1)S(1)} %collective-permute-done.26.refs_8_), channel_id=1, source_target_pairs={{1,0},{0,1},{3,2},{2,3},{5,4},{4,5},{7,6},{6,7},{9,8},{8,9},{11,10... | collective-permute-start | bytes 184328 | tf_op jit(solution)/shard_map/ppermute | solution.py:56
  128.0 9.0 %collective-permute-start.32 = (bf16[128,1280]{1,0:T(8,128)(2,1)S(1)}, bf16[128,1280]{1,0:T(8,128)(2,1)S(1)}, u32[]{:S(2)}, u32[]{:S(2)}) collective-permute-start(bf16[128,1280]{1,0:T(8,128)(2,1)S(1)} %get-tuple-element.54), channel_id=1, source_target_pairs={{64,0},{65,1},{66,2},{67,3},{68,4},{69,5},{70,6},{71,7},{72,8},{73... | collective-permute-start | bytes 983048 | tf_op jit(solution)/shard_map/ppermute | solution.py:56
  128.2 10.3 %collective-permute-start.33 = (bf16[128,1280]{1,0:T(8,128)(2,1)S(1)}, bf16[128,1280]{1,0:T(8,128)(2,1)S(1)}, u32[]{:S(2)}, u32[]{:S(2)}) collective-permute-start(bf16[128,1280]{1,0:T(8,128)(2,1)S(1)} %get-tuple-element.55), channel_id=1, source_target_pairs={{128,0},{129,1},{130,2},{131,3},{132,4},{133,5},{134,6},{135,7},{1... | collective-permute-start | bytes 983048 | tf_op jit(solution)/shard_map/ppermute | solution.py:56
  128.7 17.7 %collective-permute-start.34 = (bf16[128,1280]{1,0:T(8,128)(2,1)S(1)}, bf16[128,1280]{1,0:T(8,128)(2,1)S(1)}, u32[]{:S(2)}, u32[]{:S(2)}) collective-permute-start(bf16[128,1280]{1,0:T(8,128)(2,1)S(1)} %get-tuple-element.56), channel_id=1, source_target_pairs={{192,0},{193,1},{194,2},{195,3},{196,4},{197,5},{198,6},{199,7},{2... | collective-permute-start | bytes 983048 | tf_op jit(solution)/shard_map/ppermute | solution.py:56
  (13 other events, 143.4 us)
